TPU v7x, 32 devices: a whole 2x2x4 slice. The times are simulated.
32 devices in a mesh: plate: 4 (over z), tower: 4 (over y, core), gz: 2 (over x).
Axes of the slice: x: 2, y: 2, z: 4, core: 2. Of those that a mesh axis runs over, the one named last changes fastest.
Arguments:
- positions: float32 [4, 4, 2, 3, 128], P('plate', 'tower', 'gz'), may hold values from 0 to 1
- features: bfloat16 [4, 4, 2, 576, 128], P('plate', 'tower', 'gz'), may hold values from -6 to 6
- species: int32 [4, 4, 2, 128], P('plate', 'tower', 'gz'), may hold values from 0 to 5
- emb_table: bfloat16 [6, 64], replicated, may hold values from -4 to 4
- edges: int32 [4, 4, 2, 2, 512], P('plate', 'tower', 'gz'), may hold values from 0 to 1151, as said below
- edge_count: int32 [4, 4, 2], P('plate', 'tower', 'gz'), may hold values from 1 to 512, as said below
- w_first: bfloat16 [128, 328], replicated, may hold values from -0.3125 to 0.3125
- w_second: bfloat16 [64, 128], replicated, may hold values from -0.5 to 0.5
- w_out: bfloat16 [64], replicated, may hold values from -0.75 to 0.75
Outputs:
- forces: float32 [4, 4, 2, 3, 128], P('plate', 'tower', 'gz')
- edge_energy: float32 [4, 4, 2, 512], P('plate', 'tower', 'gz')
Inputs may be any that keep to these rules, and one draw needn't show every extreme that they name: `edges`: row 0 holds plate-set indices below 384; row 1 holds column-set indices below 1152. Slots at or beyond a box's edge_count are padding with arbitrary valid indices. `edge_count`: some box holds exactly 512 live edges in every draw.
All inputs are finite; a program needn't handle non-finite values.
Results may differ from a plain program's by a relative error of at most 0.011.
Values may be sent and summed in bfloat16 or wider, within the bound.
No kernel may reach another device: no remote copies, remote signals or barrier semaphores. Data moves between devices by JAX's collectives and lax.ppermute only.
A program may use at most 64 MiB of HBM per device.

v0:
```python
import math

import jax
import jax.numpy as jnp
from jax import lax
from jax.sharding import PartitionSpec as P

RB = 8


RADIUS = 3.0
SOFTEN = 0.04


def with_halo(cells, sides, width):
    for axis, dim in sides:
        count = lax.axis_size(axis)
        head = lax.slice_in_dim(cells, 0, width, axis=dim)
        tail = lax.slice_in_dim(cells, cells.shape[dim] - width, cells.shape[dim], axis=dim)
        cells = jnp.concatenate(
            [
                lax.ppermute(tail, axis, [(i, (i + 1) % count) for i in range(count)]),
                cells,
                lax.ppermute(head, axis, [((i + 1) % count, i) for i in range(count)]),
            ],
            axis=dim,
        )
    return cells


def harmonics(unit_vec):
    cx, cy, cz = (unit_vec[0], unit_vec[1], unit_vec[2])
    root3 = math.sqrt(3.0)
    root15 = math.sqrt(15.0)
    root5 = math.sqrt(5.0)
    return jnp.stack(
        [
            jnp.ones_like(cx),
            root3 * cx,
            root3 * cy,
            root3 * cz,
            root15 * cx * cy,
            root15 * cy * cz,
            0.5 * root5 * (3.0 * cz * cz - 1.0),
            root15 * cx * cz,
            0.5 * root15 * (cx * cx - cy * cy),
        ]
    )


def pack_block(positions, features, species, emb_table):
    pos_hi = positions.astype(jnp.bfloat16)
    back = lax.optimization_barrier(pos_hi).astype(jnp.float32)
    pos_lo = (positions - back).astype(jnp.bfloat16)
    kinds = jnp.arange(emb_table.shape[0], dtype=jnp.int32)
    onehot = (species[..., None, :] == kinds[:, None]).astype(jnp.float32)
    emb = jnp.einsum("sc,...sa->...ca", emb_table.astype(jnp.float32), onehot).astype(jnp.bfloat16)
    return jnp.concatenate([features, emb, pos_hi, pos_lo], axis=-2)


def make_offsets(atoms):
    shifts = jnp.arange(3, dtype=jnp.float32) - 1.0
    plate_x = jnp.repeat(shifts, atoms)
    zeros_plate = jnp.zeros_like(plate_x)
    plate_off = jnp.stack([plate_x, zeros_plate, zeros_plate])
    column_y = jnp.repeat(jnp.repeat(shifts, 3), atoms)
    column_z = jnp.repeat(jnp.tile(shifts, 3), atoms)
    column_off = jnp.stack([jnp.zeros_like(column_y), column_y, column_z])
    return (plate_off, column_off)


def degree_sums(terms):
    return jnp.concatenate([terms[0], jnp.sum(terms[1:4], 0), jnp.sum(terms[4:9], 0)], 0)


def edge_model(coord_i, coord_j, feat_i, feat_j, emb_i, emb_j, w_first, w_second, w_out):
    width = emb_i.shape[0]
    delta = coord_j - coord_i
    dist2 = jnp.sum(delta * delta, 0) + SOFTEN
    dist = jnp.sqrt(dist2)
    harmonic = harmonics(delta / dist)
    orders = jnp.arange(1, RB + 1, dtype=jnp.float32)
    radial = jnp.sin(orders[:, None] * (math.pi / RADIUS) * dist[None, :]) / dist[None, :]
    envelope = jnp.square(jnp.maximum(1.0 - dist2 / (RADIUS * RADIUS), 0.0))
    proj_i = degree_sums(feat_i.astype(jnp.float32).reshape(9, width, -1) * harmonic[:, None, :])
    proj_j = degree_sums(feat_j.astype(jnp.float32).reshape(9, width, -1) * harmonic[:, None, :])
    inputs = jnp.concatenate(
        [radial, emb_i.astype(jnp.float32), emb_j.astype(jnp.float32), proj_i * proj_j], 0
    ).astype(jnp.bfloat16)
    hidden = jax.nn.silu(jnp.dot(w_first, inputs, preferred_element_type=jnp.float32)).astype(
        jnp.bfloat16
    )
    second_layer = jax.nn.silu(jnp.dot(w_second, hidden, preferred_element_type=jnp.float32))
    return envelope * jnp.sum(w_out.astype(jnp.float32)[:, None] * second_layer, 0)


def split_rows(picked, offsets, width):
    coord = (
        picked[10 * width : 10 * width + 3].astype(jnp.float32)
        + picked[10 * width + 3 : 10 * width + 6].astype(jnp.float32)
        + offsets
    )
    return (coord, picked[: 9 * width], picked[9 * width : 10 * width])


def device_pass(plate_rows, column_rows, edge_list, live_count, w_first, w_second, w_out):
    width = (plate_rows.shape[0] - 6) // 10
    atoms = plate_rows.shape[1] // 3
    plate_off, column_off = make_offsets(atoms)
    total = edge_list.shape[-1]
    block = min(1024, total)

    def step(index, carry):
        plate_part, column_part, energy = carry
        start = index * block
        left_index = edge_list[0]
        right_index = edge_list[1]
        slots = start + jnp.arange(block, dtype=jnp.int32)
        live_mask = (slots < live_count).astype(jnp.float32)
        coord_i, feat_i, emb_i = split_rows(
            jnp.take(plate_rows, left_index, axis=1), jnp.take(plate_off, left_index, axis=1), width
        )
        coord_j, feat_j, emb_j = split_rows(
            jnp.take(column_rows, right_index, axis=1),
            jnp.take(column_off, right_index, axis=1),
            width,
        )

        def energy_of(left_coord, right_coord):
            return live_mask * edge_model(
                left_coord, right_coord, feat_i, feat_j, emb_i, emb_j, w_first, w_second, w_out
            )

        values, pullback = jax.vjp(energy_of, coord_i, coord_j)
        grad_i, grad_j = pullback(jnp.ones_like(values))
        plate_part = plate_part.at[:, left_index].add(grad_i)
        column_part = column_part.at[:, right_index].add(grad_j)
        energy = values
        return (plate_part, column_part, energy)

    start_carry = (
        jnp.zeros((3, 3 * atoms), jnp.float32),
        jnp.zeros((3, 9 * atoms), jnp.float32),
        jnp.zeros((total,), jnp.float32),
    )
    upper = total // block
    return lax.fori_loop(0, upper, step, start_carry)


def shards(positions, features, species, emb_table, edges, edge_count, w_first, w_second, w_out):
    atoms = positions.shape[-1]
    packed = pack_block(positions, features, species, emb_table)
    rows_atom = packed.shape[3]
    plate_ext = with_halo(packed, (("plate", 0),), 1)
    plate_rows = jnp.transpose(plate_ext[:, 0, 0], (1, 0, 2)).reshape(rows_atom, 3 * atoms)
    column_ext = with_halo(packed, (("tower", 1), ("gz", 2)), 1)
    column_rows = jnp.transpose(column_ext[0].reshape(9, rows_atom, atoms), (1, 0, 2)).reshape(
        rows_atom, 9 * atoms
    )
    plate_part, column_part, energy = device_pass(
        plate_rows, column_rows, edges[0, 0, 0], edge_count[0, 0, 0], w_first, w_second, w_out
    )
    plate_slots = jnp.transpose(plate_part.reshape(3, 3, atoms), (1, 0, 2))
    column_slots = jnp.transpose(column_part.reshape(3, 3, 3, atoms), (1, 2, 0, 3))
    plate_back = with_halo(plate_slots, (("plate", 0),), 1)
    plate_mine = jnp.sum(plate_back[0::2], 0)
    column_back = with_halo(column_slots, (("tower", 0), ("gz", 1)), 1)
    column_mine = jnp.sum(column_back[0::2, 0::2], (0, 1))
    forces = -(plate_mine + column_mine)
    return (forces.reshape(1, 1, 1, 3, atoms), energy.reshape(1, 1, 1, -1))


def solution(mesh):
    placed = (
        P("plate", "tower", "gz", None, None),
        P("plate", "tower", "gz", None, None),
        P("plate", "tower", "gz", None),
        P(),
        P("plate", "tower", "gz", None, None),
        P("plate", "tower", "gz"),
        P(),
        P(),
        P(),
    )
    return jax.shard_map(
        shards,
        mesh=mesh,
        in_specs=placed,
        out_specs=(P("plate", "tower", "gz", None, None), P("plate", "tower", "gz", None)),
        check_vma=False,
    )
```

profile of v0, /device:TPU:0, one launch (start us, length us, event | category | flops | bytes accessed | tf_op | source)
XLA Modules:
  0.0 69.6 jit_solution(11644664099394711580)
XLA Ops:
  0.7 0.7 %copy.56 = bf16[1,1,1,3,128]{4,3,2,1,0:T(4,128)(2,1)S(1)} copy(f32[1,1,1,3,128]{4,2,3,1,0:T(1,128)} %param.9) | data formatting | bytes 2304 | tf_op args[0]
  1.4 0.7 fusion.44
  2.1 0.9 %fusion.6 = bf16[1,1,1,64,128]{4,3,2,1,0:T(8,128)(2,1)S(1)} fusion(bf16[6,64]{1,0:T(8,128)(2,1)} %param.12, s32[128]{0:T(128)} %bitcast.111), kind=kOutput, calls=%fused_computation.22 | convolution fusion | flops 107264 | bytes 17664 | tf_op jit(solution)/shard_map/sc,...sa->...ca/dot_general | solution.py:57
  3.0 0.9 %pad_maximum_fusion.4 = bf16[1,1,1,646,128]{4,3,2,1,0:T(8,128)(2,1)S(1)} fusion(bf16[1,1,1,3,128]{4,3,2,1,0:T(4,128)(2,1)S(1)} %fusion.44, bf16[1,1,1,3,128]{4,3,2,1,0:T(4,128)(2,1)S(1)} %copy.56, bf16[1,1,1,64,128]{4,3,2,1,0:T(8,128)(2,1)S(1)} %fusion.6, bf16[1,1,1,576,128]{4,3,2,1,0:T(8,128)(2,1)} %param.10), kind=kLoop, calls=%fused_computation.55 | loop fusion | flops 661504 | bytes 330752 | tf_op jit(solution)/shard_map/concatenate | solution.py:58
  3.9 3.1 %collective-permute-start.4 = (bf16[1,1,1,646,128]{4,3,2,1,0:T(8,128)(2,1)S(1)}, bf16[1,1,1,646,128]{4,3,2,1,0:T(8,128)(2,1)S(1)}, u32[]{:S(2)}, u32[]{:S(2)}) collective-permute-start(bf16[1,1,1,646,128]{4,3,2,1,0:T(8,128)(2,1)S(1)} %pad_maximum_fusion.4), channel_id=1, source_target_pairs={{0,8},{8,16},{16,24},{24,0},{1,9},{9,17},{17,25},{25,1},{2,10},{10... | collective-permute-start | bytes 496136 | tf_op jit(solution)/shard_map/ppermute | solution.py:22
  7.0 2.1 %collective-permute-start.5 = (bf16[1,1,1,646,128]{4,3,2,1,0:T(8,128)(2,1)S(1)}, bf16[1,1,1,646,128]{4,3,2,1,0:T(8,128)(2,1)S(1)}, u32[]{:S(2)}, u32[]{:S(2)}) collective-permute-start(bf16[1,1,1,646,128]{4,3,2,1,0:T(8,128)(2,1)S(1)} %pad_maximum_fusion.4), channel_id=1, source_target_pairs={{8,0},{16,8},{24,16},{0,24},{9,1},{17,9},{25,17},{1,25},{10,2},{18... | collective-permute-start | bytes 496136 | tf_op jit(solution)/shard_map/ppermute | solution.py:24
  9.1 0.7 collective-permute-start.1
  9.7 0.8 %fusion.70 = (s32[1,1,1,1,512]{4,3,2,1,0:T(1,128)S(1)}, s32[1,1,1,1,512]{4,3,2,1,0:T(1,128)S(1)}) fusion(s32[1,1,1,2,512]{4,3,2,1,0:T(2,128)} %param.13), kind=kLoop, calls=%fused_computation.159 | loop fusion | bytes 8192 | tf_op jit(solution)/shard_map/while/body/eval_jaxpr/slice | solution.py:117
  10.5 0.8 %compare_select_fusion = (s32[512,1]{0,1:T(1,128)S(1)}, s32[512,1]{0,1:T(1,128)S(1)}) fusion(s32[1,1,1,2,512]{4,3,2,1,0:T(2,128)} %param.13), kind=kLoop, calls=%fused_computation.84 | loop fusion | flops 3072 | bytes 8192 | tf_op jit(solution)/shard_map/while/body/eval_jaxpr/jit(_take)/jit(_where)/select_n | solution.py:124
  11.9 0.6 compare_and_fusion.1
  12.4 1.6 %collective-permute-done.1 = bf16[1,1,1,646,128]{4,3,2,1,0:T(8,128)(2,1)S(1)} collective-permute-done((bf16[1,1,1,646,128]{4,3,2,1,0:T(8,128)(2,1)S(1)}, bf16[1,1,1,646,128]{4,3,2,1,0:T(8,128)(2,1)S(1)}, u32[]{:S(2)}, u32[]{:S(2)}) %collective-permute-start.1) | collective-permute-done | bytes 165408 | tf_op jit(solution)/shard_map/ppermute | solution.py:24
  14.0 1.8 %collective-permute-done = bf16[1,1,1,646,128]{4,3,2,1,0:T(8,128)(2,1)S(1)} collective-permute-done((bf16[1,1,1,646,128]{4,3,2,1,0:T(8,128)(2,1)S(1)}, bf16[1,1,1,646,128]{4,3,2,1,0:T(8,128)(2,1)S(1)}, u32[]{:S(2)}, u32[]{:S(2)}) %collective-permute-start) | collective-permute-done | bytes 165408 | tf_op jit(solution)/shard_map/ppermute | solution.py:22
  15.8 1.0 %pad_maximum_fusion.1 = bf16[1,3,1,646,128]{4,3,2,1,0:T(8,128)(2,1)S(1)} fusion(bf16[1,1,1,646,128]{4,3,2,1,0:T(8,128)(2,1)S(1)} %collective-permute-done.1, bf16[1,1,1,3,128]{4,3,2,1,0:T(4,128)(2,1)S(1)} %fusion.44, bf16[1,1,1,3,128]{4,3,2,1,0:T(4,128)(2,1)S(1)} %copy.56, bf16[1,1,1,64,128]{4,3,2,1,0:T(8,128)(2,1)S(1)} %fusion.6, ...), kind=kLoop, calls=%fused_computation.27 | loop fusion | flops 2976768 | bytes 992256 | tf_op jit(solution)/shard_map/concatenate | solution.py:20
  16.8 1.6 %collective-permute-start.3 = (bf16[1,3,1,646,128]{4,3,2,1,0:T(8,128)(2,1)S(1)}, bf16[1,3,1,646,128]{4,3,2,1,0:T(8,128)(2,1)}, u32[]{:S(2)}, u32[]{:S(2)}) collective-permute-start(bf16[1,3,1,646,128]{4,3,2,1,0:T(8,128)(2,1)S(1)} %pad_maximum_fusion.1), channel_id=1, source_target_pairs={{1,0},{0,1},{3,2},{2,3},{5,4},{4,5},{7,6},{6,7},{9,8},{8,9},{11,10... | collective-permute-start | bytes 1488392 | tf_op jit(solution)/shard_map/ppermute | solution.py:24
  18.3 0.5 collective-permute-start.2
  18.9 0.5 compare_and_fusion
  20.1 0.5 convert_element_type.90
  20.8 1.0 %gather_fusion.1 = f32[512,3]{1,0:T(8,128)S(1)} fusion(f32[3,1152]{0,1:T(8,128)S(1)} %copy.35, s32[1024]{0:T(1024)S(1)} %pad_clamp_fusion.1), kind=kCustom, calls=%fused_computation.1 | custom fusion | bytes 14336 | tf_op jit(solution)/shard_map/while/body/eval_jaxpr/jit(_take)/gather | solution.py:125
  22.0 4.6 %gather_fusion.3 = f32[512]{0:T(512)} fusion(f32[384]{0:T(512)S(1)} %broadcast_bitcast_fusion.2, s32[1024]{0:T(1024)S(1)} %pad_clamp_fusion), kind=kCustom, calls=%fused_computation.3 | custom fusion | bytes 6144 | tf_op jit(solution)/shard_map/while/body/eval_jaxpr/jit(_take)/gather | solution.py:121
  26.6 0.5 add_multiply_fusion
  27.2 0.3 copy.37
  27.5 2.0 %gather_fusion.2 = bf16[512,646]{1,0:T(8,128)(2,1)S(1)} fusion(bf16[646,384]{0,1:T(8,128)(2,1)S(1)} %bitcast.88, s32[1024]{0:T(1024)S(1)} %pad_clamp_fusion), kind=kCustom, calls=%fused_computation.2 | custom fusion | bytes 1325056 | tf_op jit(solution)/shard_map/while/body/eval_jaxpr/jit(_take)/gather | solution.py:121
  29.5 1.1 %copy.38 = bf16[512,646]{0,1:T(8,128)(2,1)} copy(bf16[512,646]{1,0:T(8,128)(2,1)S(1)} %gather_fusion.2) | data formatting | bytes 1323008 | tf_op jit(solution)/shard_map/while/body/eval_jaxpr/jit(_take)/gather | solution.py:121
  30.6 0.6 collective-permute-done.3
  31.2 9.4 %collective-permute-done.2 = bf16[1,3,1,646,128]{4,3,2,1,0:T(8,128)(2,1)} collective-permute-done((bf16[1,3,1,646,128]{4,3,2,1,0:T(8,128)(2,1)S(1)}, bf16[1,3,1,646,128]{4,3,2,1,0:T(8,128)(2,1)}, u32[]{:S(2)}, u32[]{:S(2)}) %collective-permute-start.2) | collective-permute-done | bytes 496160 | tf_op jit(solution)/shard_map/ppermute | solution.py:22
  40.6 1.8 %pad_maximum_fusion = bf16[1,3,3,646,128]{4,3,2,1,0:T(8,128)(2,1)S(1)} fusion(bf16[1,3,1,646,128]{4,3,2,1,0:T(8,128)(2,1)} %collective-permute-done.3, bf16[1,1,1,646,128]{4,3,2,1,0:T(8,128)(2,1)S(1)} %collective-permute-done.1, bf16[1,1,1,3,128]{4,3,2,1,0:T(4,128)(2,1)S(1)} %fusion.44, bf16[1,1,1,3,128]{4,3,2,1,0:T(4,128)(2,1)S(1)} %copy.56, ...), kind=kLoop, calls=%fused_computation.6 | loop fusion | flops 11907072 | bytes 2976768 | tf_op jit(solution)/shard_map/concatenate | solution.py:20
  42.4 0.9 %copy.33 = bf16[9,646,128]{1,2,0:T(8,128)(2,1)S(1)} copy(bf16[9,646,128]{2,1,0:T(8,128)(2,1)S(1)} %bitcast.90) | data formatting | bytes 2976768 | tf_op jit(solution)/shard_map/reshape;squeeze | solution.py:157
  43.3 2.0 %gather_fusion = bf16[512,646]{1,0:T(8,128)(2,1)S(1)} fusion(bf16[646,1152]{0,1:T(8,128)(2,1)S(1)} %bitcast.89, s32[1024]{0:T(1024)S(1)} %pad_clamp_fusion.1), kind=kCustom, calls=%fused_computation | custom fusion | bytes 1325056 | tf_op jit(solution)/shard_map/while/body/eval_jaxpr/jit(_take)/gather | solution.py:124
  45.6 0.8 %copy-done.1 = bf16[512,646]{0,1:T(8,128)(2,1)S(1)} copy-done((bf16[512,646]{0,1:T(8,128)(2,1)S(1)}, bf16[512,646]{0,1:T(8,128)(2,1)}, u32[]{:S(2)}) %copy-start.1) | copy-done | bytes 661528
  46.7 0.5 copy-done.5
  47.4 0.3 convert_multiply_fusion.1
  48.0 0.4 copy-done.8
  48.6 0.3 convolution_bitcast_fusion
  48.9 0.3 multiply_reduce_fusion
  49.2 0.6 fusion.1
  50.0 0.3 fusion.2
  50.4 0.3 fusion.3
  51.3 2.4 %scatter_custom_fusion = f32[3,384]{0,1:T(8,128)S(1)} fusion(s32[512]{0:T(512)} %bitcast.106, f32[512,3]{1,0:T(8,128)S(1)} %copy.39, f32[]{:T(128)} %constant.110.clone.1), kind=kCustom, calls=%fused_computation.65 | custom fusion | flops 1536 | bytes 5120 | tf_op jit(solution)/shard_map/while/body/eval_jaxpr/scatter-add | solution.py:136
  53.9 3.8 %collective-permute-start.7 = (f32[1,3,128]{2,1,0:T(4,128)S(1)}, f32[1,3,128]{2,1,0:T(4,128)S(1)}, u32[]{:S(2)}, u32[]{:S(2)}) collective-permute-start(f32[1,3,128]{2,1,0:T(4,128)S(1)} %get-tuple-element.76), channel_id=1, source_target_pairs={{8,0},{16,8},{24,16},{0,24},{9,1},{17,9},{25,17},{1,25},{10,2},{18... | collective-permute-start | bytes 4616 | tf_op jit(solution)/shard_map/ppermute | solution.py:24
  57.7 2.5 %scatter_custom_fusion.1 = f32[3,1152]{0,1:T(8,128)S(1)} fusion(s32[512]{0:T(512)} %bitcast.104, f32[512,3]{1,0:T(8,128)S(1)} %copy.42, f32[]{:T(128)} %constant.110.clone.1), kind=kCustom, calls=%fused_computation.44 | custom fusion | flops 1536 | bytes 14336 | tf_op jit(solution)/shard_map/while/body/eval_jaxpr/scatter-add | solution.py:137
  60.5 1.7 %collective-permute-start.9 = (f32[1,3,3,128]{3,2,1,0:T(4,128)S(1)}, f32[1,3,3,128]{3,2,1,0:T(4,128)S(1)}, u32[]{:S(2)}, u32[]{:S(2)}) collective-permute-start(f32[1,3,3,128]{3,2,1,0:T(4,128)S(1)} %get-tuple-element.66), channel_id=1, source_target_pairs={{2,0},{4,2},{6,4},{0,6},{3,1},{5,3},{7,5},{1,7},{10,8},{12,10},{14... | collective-permute-start | bytes 13832 | tf_op jit(solution)/shard_map/ppermute | solution.py:24
  62.2 0.6 compare_select_fusion.2
  62.8 0.7 %collective-permute-done.8 = f32[1,3,3,128]{3,2,1,0:T(4,128)S(1)} collective-permute-done((f32[1,3,3,128]{3,2,1,0:T(4,128)S(1)}, f32[1,3,3,128]{3,2,1,0:T(4,128)S(1)}, u32[]{:S(2)}, u32[]{:S(2)}) %collective-permute-start.8) | collective-permute-done | bytes 4640 | tf_op jit(solution)/shard_map/ppermute | solution.py:22
  63.6 1.5 %collective-permute-start.10 = (f32[5,1,3,128]{3,2,1,0:T(4,128)S(1)}, f32[5,1,3,128]{3,2,1,0:T(4,128)S(1)}, u32[]{:S(2)}, u32[]{:S(2)}) collective-permute-start(f32[5,1,3,128]{3,2,1,0:T(4,128)S(1)} %get-tuple-element.63), channel_id=1, source_target_pairs={{0,1},{1,0},{2,3},{3,2},{4,5},{5,4},{6,7},{7,6},{8,9},{9,8},{10,11... | collective-permute-start | bytes 23048 | tf_op jit(solution)/shard_map/ppermute | solution.py:22
  65.1 0.5 collective-permute-start.11
  65.8 1.5 %collective-permute-done.10 = f32[5,1,3,128]{3,2,1,0:T(4,128)S(1)} collective-permute-done((f32[5,1,3,128]{3,2,1,0:T(4,128)S(1)}, f32[5,1,3,128]{3,2,1,0:T(4,128)S(1)}, u32[]{:S(2)}, u32[]{:S(2)}) %collective-permute-start.10) | collective-permute-done | bytes 7712 | tf_op jit(solution)/shard_map/ppermute | solution.py:22
  67.3 1.5 %collective-permute-done.11 = f32[5,1,3,128]{3,2,1,0:T(4,128)S(1)} collective-permute-done((f32[5,1,3,128]{3,2,1,0:T(4,128)S(1)}, f32[5,1,3,128]{3,2,1,0:T(4,128)S(1)}, u32[]{:S(2)}, u32[]{:S(2)}) %collective-permute-start.11) | collective-permute-done | bytes 7712 | tf_op jit(solution)/shard_map/ppermute | solution.py:24
  68.9 0.6 copy.45
  (93 shorter events, 3.7 us)
Async XLA Ops:
  0.6 47.9 %copy-start = (bf16[128,328]{0,1:T(8,128)(2,1)S(1)}, bf16[128,328]{0,1:T(8,128)(2,1)}, u32[]{:S(2)}) copy-start(bf16[128,328]{0,1:T(8,128)(2,1)} %param.15) | copy-start | bytes 251908
  0.6 19.4 %copy-start.10 = (bf16[64]{0:T(256)(128)(2,1)S(1)}, bf16[64]{0:T(256)(128)(2,1)}, u32[]{:S(2)}) copy-start(bf16[64]{0:T(256)(128)(2,1)} %param.17) | copy-start | bytes 388
  3.9 23.3 %collective-permute-start.4 = (bf16[1,1,1,646,128]{4,3,2,1,0:T(8,128)(2,1)S(1)}, bf16[1,1,1,646,128]{4,3,2,1,0:T(8,128)(2,1)S(1)}, u32[]{:S(2)}, u32[]{:S(2)}) collective-permute-start(bf16[1,1,1,646,128]{4,3,2,1,0:T(8,128)(2,1)S(1)} %pad_maximum_fusion.4), channel_id=1, source_target_pairs={{0,8},{8,16},{16,24},{24,0},{1,9},{9,17},{17,25},{25,1},{2,10},{10... | collective-permute-start | bytes 496136 | tf_op jit(solution)/shard_map/ppermute | solution.py:22
  7.0 20.2 %collective-permute-start.5 = (bf16[1,1,1,646,128]{4,3,2,1,0:T(8,128)(2,1)S(1)}, bf16[1,1,1,646,128]{4,3,2,1,0:T(8,128)(2,1)S(1)}, u32[]{:S(2)}, u32[]{:S(2)}) collective-permute-start(bf16[1,1,1,646,128]{4,3,2,1,0:T(8,128)(2,1)S(1)} %pad_maximum_fusion.4), channel_id=1, source_target_pairs={{8,0},{16,8},{24,16},{0,24},{9,1},{17,9},{25,17},{1,25},{10,2},{18... | collective-permute-start | bytes 496136 | tf_op jit(solution)/shard_map/ppermute | solution.py:24
  9.1 5.0 %collective-permute-start.1 = (bf16[1,1,1,646,128]{4,3,2,1,0:T(8,128)(2,1)S(1)}, bf16[1,1,1,646,128]{4,3,2,1,0:T(8,128)(2,1)S(1)}, u32[]{:S(2)}, u32[]{:S(2)}) collective-permute-start(bf16[1,1,1,646,128]{4,3,2,1,0:T(8,128)(2,1)S(1)} %pad_maximum_fusion.4), channel_id=1, source_target_pairs={{2,0},{4,2},{6,4},{0,6},{3,1},{5,3},{7,5},{1,7},{10,8},{12,10},{14... | collective-permute-start | bytes 496136 | tf_op jit(solution)/shard_map/ppermute | solution.py:24
  9.7 6.1 %collective-permute-start = (bf16[1,1,1,646,128]{4,3,2,1,0:T(8,128)(2,1)S(1)}, bf16[1,1,1,646,128]{4,3,2,1,0:T(8,128)(2,1)S(1)}, u32[]{:S(2)}, u32[]{:S(2)}) collective-permute-start(bf16[1,1,1,646,128]{4,3,2,1,0:T(8,128)(2,1)S(1)} %pad_maximum_fusion.4), channel_id=1, source_target_pairs={{0,2},{2,4},{4,6},{6,0},{1,3},{3,5},{5,7},{7,1},{8,10},{10,12},{12... | collective-permute-start | bytes 496136 | tf_op jit(solution)/shard_map/ppermute | solution.py:22
  11.3 15.3 %copy-start.3 = (s32[512,1]{0,1:T(1,128)}, s32[512,1]{0,1:T(1,128)S(1)}, u32[]{:S(2)}) copy-start(s32[512,1]{0,1:T(1,128)S(1)} %get-tuple-element.81) | copy-start | bytes 6148
  11.3 15.3 %copy-start.4 = (s32[512,1]{0,1:T(1,128)}, s32[512,1]{0,1:T(1,128)S(1)}, u32[]{:S(2)}) copy-start(s32[512,1]{0,1:T(1,128)S(1)} %get-tuple-element.82) | copy-start | bytes 6148
  16.8 14.4 %collective-permute-start.3 = (bf16[1,3,1,646,128]{4,3,2,1,0:T(8,128)(2,1)S(1)}, bf16[1,3,1,646,128]{4,3,2,1,0:T(8,128)(2,1)}, u32[]{:S(2)}, u32[]{:S(2)}) collective-permute-start(bf16[1,3,1,646,128]{4,3,2,1,0:T(8,128)(2,1)S(1)} %pad_maximum_fusion.1), channel_id=1, source_target_pairs={{1,0},{0,1},{3,2},{2,3},{5,4},{4,5},{7,6},{6,7},{9,8},{8,9},{11,10... | collective-permute-start | bytes 1488392 | tf_op jit(solution)/shard_map/ppermute | solution.py:24
  18.3 22.3 %collective-permute-start.2 = (bf16[1,3,1,646,128]{4,3,2,1,0:T(8,128)(2,1)S(1)}, bf16[1,3,1,646,128]{4,3,2,1,0:T(8,128)(2,1)}, u32[]{:S(2)}, u32[]{:S(2)}) collective-permute-start(bf16[1,3,1,646,128]{4,3,2,1,0:T(8,128)(2,1)S(1)} %pad_maximum_fusion.1), channel_id=1, source_target_pairs={{0,1},{1,0},{2,3},{3,2},{4,5},{5,4},{6,7},{7,6},{8,9},{9,8},{10,11... | collective-permute-start | bytes 1488392 | tf_op jit(solution)/shard_map/ppermute | solution.py:22
  20.6 6.6 %copy-start.2 = (bf16[1,1,1,576,128]{4,3,2,1,0:T(8,128)(2,1)S(1)}, bf16[1,1,1,576,128]{4,3,2,1,0:T(8,128)(2,1)}, u32[]{:S(2)}) copy-start(bf16[1,1,1,576,128]{4,3,2,1,0:T(8,128)(2,1)} %param.10) | copy-start | bytes 442372
  43.3 2.3 %copy-start.6 = (pred[512]{0:T(512)(128)(4,1)S(1)}, pred[512]{0:T(512)(128)(4,1)}, u32[]{:S(2)}) copy-start(pred[512]{0:T(512)(128)(4,1)} %compare_and_fusion.1) | copy-start | bytes 1540
  43.3 2.3 %copy-start.7 = (pred[512]{0:T(512)(128)(4,1)S(1)}, pred[512]{0:T(512)(128)(4,1)}, u32[]{:S(2)}) copy-start(pred[512]{0:T(512)(128)(4,1)} %compare_and_fusion) | copy-start | bytes 1540
  45.3 1.1 %copy-start.1 = (bf16[512,646]{0,1:T(8,128)(2,1)S(1)}, bf16[512,646]{0,1:T(8,128)(2,1)}, u32[]{:S(2)}) copy-start(bf16[512,646]{0,1:T(8,128)(2,1)} %copy.38) | copy-start | bytes 1984516
  46.6 0.7 copy-start.5
  47.7 0.6 copy-start.8
  47.9 1.0 %copy-start.9 = (bf16[64,128]{1,0:T(8,128)(2,1)S(1)}, bf16[64,128]{1,0:T(8,128)(2,1)}, u32[]{:S(2)}) copy-start(bf16[64,128]{1,0:T(8,128)(2,1)} %param.16) | copy-start | bytes 49156
  47.9 1.0 %copy-start.11 = (f32[64]{0:T(128)S(1)}, f32[64]{0:T(128)}, u32[]{:S(2)}) copy-start(f32[64]{0:T(128)} %convert_element_type.90) | copy-start | bytes 772
  53.8 9.0 %collective-permute-start.6 = (f32[1,3,128]{2,1,0:T(4,128)S(1)}, f32[1,3,128]{2,1,0:T(4,128)S(1)}, u32[]{:S(2)}, u32[]{:S(2)}) collective-permute-start(f32[1,3,128]{2,1,0:T(4,128)S(1)} %get-tuple-element.75), channel_id=1, source_target_pairs={{0,8},{8,16},{16,24},{24,0},{1,9},{9,17},{17,25},{25,1},{2,10},{10... | collective-permute-start | bytes 4616 | tf_op jit(solution)/shard_map/ppermute | solution.py:22
  53.9 8.9 %collective-permute-start.7 = (f32[1,3,128]{2,1,0:T(4,128)S(1)}, f32[1,3,128]{2,1,0:T(4,128)S(1)}, u32[]{:S(2)}, u32[]{:S(2)}) collective-permute-start(f32[1,3,128]{2,1,0:T(4,128)S(1)} %get-tuple-element.76), channel_id=1, source_target_pairs={{8,0},{16,8},{24,16},{0,24},{9,1},{17,9},{25,17},{1,25},{10,2},{18... | collective-permute-start | bytes 4616 | tf_op jit(solution)/shard_map/ppermute | solution.py:24
  60.4 3.1 %collective-permute-start.8 = (f32[1,3,3,128]{3,2,1,0:T(4,128)S(1)}, f32[1,3,3,128]{3,2,1,0:T(4,128)S(1)}, u32[]{:S(2)}, u32[]{:S(2)}) collective-permute-start(f32[1,3,3,128]{3,2,1,0:T(4,128)S(1)} %get-tuple-element.65), channel_id=1, source_target_pairs={{0,2},{2,4},{4,6},{6,0},{1,3},{3,5},{5,7},{7,1},{8,10},{10,12},{12... | collective-permute-start | bytes 13832 | tf_op jit(solution)/shard_map/ppermute | solution.py:22
  60.5 3.1 %collective-permute-start.9 = (f32[1,3,3,128]{3,2,1,0:T(4,128)S(1)}, f32[1,3,3,128]{3,2,1,0:T(4,128)S(1)}, u32[]{:S(2)}, u32[]{:S(2)}) collective-permute-start(f32[1,3,3,128]{3,2,1,0:T(4,128)S(1)} %get-tuple-element.66), channel_id=1, source_target_pairs={{2,0},{4,2},{6,4},{0,6},{3,1},{5,3},{7,5},{1,7},{10,8},{12,10},{14... | collective-permute-start | bytes 13832 | tf_op jit(solution)/shard_map/ppermute | solution.py:24
  63.6 3.7 %collective-permute-start.10 = (f32[5,1,3,128]{3,2,1,0:T(4,128)S(1)}, f32[5,1,3,128]{3,2,1,0:T(4,128)S(1)}, u32[]{:S(2)}, u32[]{:S(2)}) collective-permute-start(f32[5,1,3,128]{3,2,1,0:T(4,128)S(1)} %get-tuple-element.63), channel_id=1, source_target_pairs={{0,1},{1,0},{2,3},{3,2},{4,5},{5,4},{6,7},{7,6},{8,9},{9,8},{10,11... | collective-permute-start | bytes 23048 | tf_op jit(solution)/shard_map/ppermute | solution.py:22
  65.1 3.7 %collective-permute-start.11 = (f32[5,1,3,128]{3,2,1,0:T(4,128)S(1)}, f32[5,1,3,128]{3,2,1,0:T(4,128)S(1)}, u32[]{:S(2)}, u32[]{:S(2)}) collective-permute-start(f32[5,1,3,128]{3,2,1,0:T(4,128)S(1)} %get-tuple-element.64), channel_id=1, source_target_pairs={{1,0},{0,1},{3,2},{2,3},{5,4},{4,5},{7,6},{6,7},{9,8},{8,9},{11,10... | collective-permute-start | bytes 23048 | tf_op jit(solution)/shard_map/ppermute | solution.py:24
where the time goes:
time: 70 us; the launch traced here: 69.6 us
  local copies, waits for them, and re-layouts  18.2 us (26%)
  waiting for transfers between devices  17.2 us (25%)
  starting transfers between devices  15.6 us (22%)
  other arithmetic  14.7 us (21%)
  matrix products  2.03 us (3%)
  between operations  1.81 us (3%)
    ppermute x6, waiting for transfers between devices, with_halo(): lax.ppermute(tail, axis, [(i, (i + 1) % count) for i in range(count)])  13.4 us
    ppermute x6, starting transfers between devices, with_halo(): lax.ppermute(head, axis, [((i + 1) % count, i) for i in range(count)])  10.4 us
    ppermute x6, starting transfers between devices, with_halo(): lax.ppermute(tail, axis, [(i, (i + 1) % count) for i in range(count)])  5.23 us
    gather x1, local copies, waits for them, and re-layouts, step(): jnp.take(plate_off, left_index, axis=1)  4.65 us
    ppermute x6, waiting for transfers between devices, with_halo(): lax.ppermute(head, axis, [((i + 1) % count, i) for i in range(count)])  3.73 us
    unnamed x30, local copies, waits for them, and re-layouts  3.51 us
    gather x2, local copies, waits for them, and re-layouts, step(): jnp.take(plate_rows, left_index, axis=1)  3.11 us
    concatenate x4, other arithmetic, with_halo(): jnp.concatenate([lax.ppermute(tail, axis, [(i, (i + 1) % count) for i in...  2.74 us
  transfers between devices with their start and end apart: 12, of which 7 were waited for; matrix products, arithmetic and copies ran while one was open for 26% of the time, Pallas kernels for 0%

commit v1 on v0

v1 whole, which is shorter than its diff:
```python
import functools
import math

import jax
import jax.numpy as jnp
from jax import lax
from jax.experimental import pallas as pl
from jax.experimental.pallas import tpu as pltpu
from jax.sharding import PartitionSpec as P

RB = 8
RADIUS = 3.0
SOFTEN = 0.04
EXTRA = 16
F32 = jnp.float32
BF16 = jnp.bfloat16


def fetch(x, axis, shift):
    count = lax.axis_size(axis)
    return lax.ppermute(x, axis, [(i, (i - shift) % count) for i in range(count)])


def distinct(axis):
    count = lax.axis_size(axis)
    shifts, which = [0], []
    for shift in (-1, 0, 1):
        same = [k for k, s in enumerate(shifts) if (s - shift) % count == 0]
        if not same:
            shifts.append(shift)
        which.append(same[0] if same else len(shifts) - 1)
    return shifts, which


def pick(index, table):
    out = jnp.full_like(index, table[0])
    for k in range(1, len(table)):
        if table[k] != table[k - 1]:
            out = out + jnp.where(index >= k, table[k] - table[k - 1], 0)
    return out


def count_steps(index, step, last):
    out = jnp.zeros_like(index)
    for k in range(1, last):
        out = out + jnp.where(index >= k * step, 1, 0)
    return out


def sigmoid(v):
    return 1.0 / (1.0 + jnp.exp(-v))


def edge_kernel(plan, *refs):
    n_plate, n_column, plate_which, tower_which, gz_which, n_gz = plan
    block_refs = refs[: n_plate + n_column]
    (edges_ref, count_ref, emb_ref, w1_ref, w2_ref, wo_ref, energy_ref, plate_ref, column_ref) = refs[
        n_plate + n_column :
    ]
    rows, atoms = block_refs[0].shape
    total = edges_ref.shape[1]
    width = (rows - EXTRA) // 9

    left = edges_ref[0:1, :]
    right = edges_ref[1:2, :]
    side_i = count_steps(left, atoms, 3)
    atom_i = left - side_i * atoms
    row_i = pick(side_i, plate_which) * atoms + atom_i
    blk_j = count_steps(right, atoms, 9)
    atom_j = right - blk_j * atoms
    u_j = jnp.where(blk_j >= 3, 1, 0) + jnp.where(blk_j >= 6, 1, 0)
    v_j = blk_j - 3 * u_j
    row_j = (pick(u_j, tower_which) * n_gz + pick(v_j, gz_which)) * atoms + atom_j

    iota_i = lax.broadcasted_iota(jnp.int32, (n_plate * atoms, total), 0)
    hot_i = jnp.where(iota_i == row_i, 1.0, 0.0).astype(BF16)
    iota_j = lax.broadcasted_iota(jnp.int32, (n_column * atoms, total), 0)
    hot_j = jnp.where(iota_j == row_j, 1.0, 0.0).astype(BF16)

    plate_all = jnp.concatenate([block_refs[k][...] for k in range(n_plate)], axis=1)
    column_all = jnp.concatenate([block_refs[n_plate + k][...] for k in range(n_column)], axis=1)
    got_i = jnp.dot(plate_all, hot_i, preferred_element_type=F32)
    got_j = jnp.dot(column_all, hot_j, preferred_element_type=F32)

    base = 9 * width

    def row(got, k):
        return got[base + k : base + k + 1, :]

    d = []
    for axis in range(3):
        ci = row(got_i, axis) + row(got_i, 3 + axis)
        cj = row(got_j, axis) + row(got_j, 3 + axis)
        off = (None, u_j, v_j)[axis]
        if axis == 0:
            ci = ci + (side_i - 1).astype(F32)
        else:
            cj = cj + (off - 1).astype(F32)
        d.append(cj - ci)
    r2 = d[0] * d[0] + d[1] * d[1] + d[2] * d[2] + SOFTEN
    r = jnp.sqrt(r2)
    inv = 1.0 / r
    nx, ny, nz = d[0] * inv, d[1] * inv, d[2] * inv
    root3, root5, root15 = math.sqrt(3.0), math.sqrt(5.0), math.sqrt(15.0)
    harm = [
        None,
        root3 * nx,
        root3 * ny,
        root3 * nz,
        root15 * nx * ny,
        root15 * ny * nz,
        0.5 * root5 * (3.0 * nz * nz - 1.0),
        root15 * nx * nz,
        0.5 * root15 * (nx * nx - ny * ny),
    ]
    freq = (lax.broadcasted_iota(jnp.int32, (RB, 1), 0) + 1).astype(F32) * (math.pi / RADIUS)
    phase = freq * r
    radial = jnp.sin(phase) * inv
    wave = jnp.cos(phase)
    gap = jnp.maximum(1.0 - r2 / (RADIUS * RADIUS), 0.0)
    env = gap * gap

    def feat(got, m):
        return got[m * width : (m + 1) * width, :]

    def degrees(got):
        one = harm[1] * feat(got, 1) + harm[2] * feat(got, 2) + harm[3] * feat(got, 3)
        two = harm[4] * feat(got, 4)
        for m in range(5, 9):
            two = two + harm[m] * feat(got, m)
        return feat(got, 0), one, two

    s_i = degrees(got_i)
    s_j = degrees(got_j)
    q = jnp.concatenate([(a * b).astype(BF16) for a, b in zip(s_i, s_j)], axis=0)

    kinds = emb_ref.shape[0]
    kind_iota = lax.broadcasted_iota(jnp.int32, (kinds, total), 0).astype(F32)
    tn = (((0,), (0,)), ((), ()))

    def emb_of(got):
        hot = jnp.where(kind_iota == row(got, 6), 1.0, 0.0).astype(BF16)
        return lax.dot_general(emb_ref[...], hot, tn, preferred_element_type=F32).astype(BF16)

    emb = jnp.concatenate([emb_of(got_i), emb_of(got_j)], axis=0)
    w1 = w1_ref[...]
    w_rad = w1[:, :RB]
    w_emb = w1[:, RB : RB + 2 * width]
    w_q = w1[:, RB + 2 * width :]
    pre1 = (
        jnp.dot(w_q, q, preferred_element_type=F32)
        + jnp.dot(w_emb, emb, preferred_element_type=F32)
        + jnp.dot(w_rad, radial.astype(BF16), preferred_element_type=F32)
    )
    sig1 = sigmoid(pre1)
    hidden = (pre1 * sig1).astype(BF16)
    w2 = w2_ref[...]
    pre2 = jnp.dot(w2, hidden, preferred_element_type=F32)
    sig2 = sigmoid(pre2)
    chan = wo_ref.shape[1]
    eye = lax.broadcasted_iota(jnp.int32, (chan, chan), 0) == lax.broadcasted_iota(jnp.int32, (chan, chan), 1)
    w_out = jnp.sum(jnp.where(eye, wo_ref[...].astype(F32), 0.0), axis=1, keepdims=True)
    score = jnp.sum(w_out * (pre2 * sig2), axis=0, keepdims=True)
    slots = lax.broadcasted_iota(jnp.int32, (1, total), 1)
    live = jnp.where(slots < count_ref[0], 1.0, 0.0)
    live_env = live * env
    energy_ref[...] = live_env * score

    g2 = (live_env * w_out) * (sig2 * (1.0 + pre2 * (1.0 - sig2)))
    dh = lax.dot_general(w2, g2.astype(BF16), tn, preferred_element_type=F32).astype(BF16).astype(F32)
    g1 = (dh * (sig1 * (1.0 + pre1 * (1.0 - sig1)))).astype(BF16)
    dq = lax.dot_general(w_q, g1, tn, preferred_element_type=F32).astype(BF16).astype(F32)
    dradial = lax.dot_general(w_rad, g1, tn, preferred_element_type=F32).astype(BF16).astype(F32)
    dy = [None] * 9
    for deg, members in ((1, range(1, 4)), (2, range(4, 9))):
        part = dq[deg * width : (deg + 1) * width, :]
        for_i = part * s_j[deg]
        for_j = part * s_i[deg]
        for m in members:
            dy[m] = jnp.sum(for_i * feat(got_i, m) + for_j * feat(got_j, m), axis=0, keepdims=True)
    gn = [
        root3 * dy[1] + root15 * (ny * dy[4] + nz * dy[7] + nx * dy[8]),
        root3 * dy[2] + root15 * (nx * dy[4] + nz * dy[5] - ny * dy[8]),
        root3 * dy[3] + root15 * (ny * dy[5] + nx * dy[7]) + (3.0 * root5) * nz * dy[6],
    ]
    dr = jnp.sum(dradial * (freq * wave - radial), axis=0, keepdims=True)
    dr = (dr - (gn[0] * nx + gn[1] * ny + gn[2] * nz)) * inv
    dr2 = dr * (0.5 * inv) - (live * score) * gap * (2.0 / (RADIUS * RADIUS))
    grad = jnp.concatenate([gn[k] * inv + 2.0 * d[k] * dr2 for k in range(3)], axis=0)
    high = grad.astype(BF16)
    low = (grad - high.astype(F32)).astype(BF16)
    nt = (((1,), (1,)), ((), ()))

    def spread(hot):
        return lax.dot_general(high, hot, nt, preferred_element_type=F32) + lax.dot_general(
            low, hot, nt, preferred_element_type=F32
        )

    to_plate = spread(hot_i)
    to_column = spread(hot_j)
    own = to_plate[:, :atoms] - to_column[:, :atoms]
    for k in range(1, n_plate):
        plate_ref[k - 1] = to_plate[:, k * atoms : (k + 1) * atoms]
    column_ref[0, 0] = own
    for k in range(1, n_column):
        column_ref[k // n_gz, k % n_gz] = -to_column[:, k * atoms : (k + 1) * atoms]


def shards(positions, features, species, emb_table, edges, edge_count, w_first, w_second, w_out):
    atoms = positions.shape[-1]
    total = edges.shape[-1]
    pos = positions[0, 0, 0]
    high = lax.reduce_precision(pos, 8, 7)
    small = jnp.concatenate(
        [high, pos - high, species[0, 0, 0][None, :].astype(F32), jnp.zeros((EXTRA - 7, atoms), F32)], axis=0
    ).astype(BF16)
    packed = jnp.concatenate([features[0, 0, 0], small], axis=0)

    plate_shifts, plate_which = distinct("plate")
    tower_shifts, tower_which = distinct("tower")
    gz_shifts, gz_which = distinct("gz")
    n_gz = len(gz_shifts)
    plate_blocks = [packed] + [fetch(packed, "plate", s) for s in plate_shifts[1:]]
    gz_blocks = [packed] + [fetch(packed, "gz", s) for s in gz_shifts[1:]]
    column_blocks = list(gz_blocks)
    for s in tower_shifts[1:]:
        column_blocks += [fetch(block, "tower", s) for block in gz_blocks]
    n_plate, n_column = len(plate_blocks), len(column_blocks)

    plan = (n_plate, n_column, plate_which, tower_which, gz_which, n_gz)
    vmem = pl.BlockSpec(memory_space=pltpu.VMEM)
    n_vmem = n_plate + n_column
    energy, plate_part, column_part = pl.pallas_call(
        functools.partial(edge_kernel, plan),
        out_shape=(
            jax.ShapeDtypeStruct((1, total), F32),
            jax.ShapeDtypeStruct((max(n_plate - 1, 1), 3, atoms), F32),
            jax.ShapeDtypeStruct((len(tower_shifts), n_gz, 3, atoms), F32),
        ),
        in_specs=[vmem] * (n_vmem + 1) + [pl.BlockSpec(memory_space=pltpu.SMEM)] + [vmem] * 4,
        out_specs=(vmem, vmem, vmem),
        compiler_params=pltpu.CompilerParams(vmem_limit_bytes=48 * 1024 * 1024),
        name="edge_work",
    )(
        *plate_blocks,
        *column_blocks,
        edges[0, 0, 0],
        edge_count.reshape(1),
        emb_table,
        w_first,
        w_second,
        w_out.reshape(1, -1),
    )

    forces = 0.0
    for k, s in enumerate(plate_shifts[1:]):
        forces = forces + fetch(plate_part[k], "plate", -s)
    column = column_part[:, 0]
    for k, s in enumerate(gz_shifts[1:]):
        column = column + fetch(column_part[:, 1 + k], "gz", -s)
    forces = forces + column[0]
    for k, s in enumerate(tower_shifts[1:]):
        forces = forces + fetch(column[1 + k], "tower", -s)
    return (forces.reshape(1, 1, 1, 3, atoms), energy.reshape(1, 1, 1, -1))


def solution(mesh):
    placed = (
        P("plate", "tower", "gz", None, None),
        P("plate", "tower", "gz", None, None),
        P("plate", "tower", "gz", None),
        P(),
        P("plate", "tower", "gz", None, None),
        P("plate", "tower", "gz"),
        P(),
        P(),
        P(),
    )
    return jax.shard_map(
        shards,
        mesh=mesh,
        in_specs=placed,
        out_specs=(P("plate", "tower", "gz", None, None), P("plate", "tower", "gz", None)),
        check_vma=False,
    )
```

time: 70 us -> 30 us (0.43)
  local copies, waits for them, and re-layouts: 18.2 us -> 2.49 us
  other arithmetic: 14.7 us -> 0.68 us
  waiting for transfers between devices: 17.2 us -> 8.62 us
  Pallas kernels: 0 us -> 2.78 us
  matrix products: 2.03 us -> 0 us
  starting transfers between devices: 15.6 us -> 13.8 us
    gather x7 -> x0, local copies, waits for them, and re-layouts: 11.2 us -> none  [the longest x1 4.65 us: step(): jnp.take(plate_off, left_index, axis=1)]
    ppermute x12, waiting for transfers between devices: 17.2 us -> 8.62 us  [fetch(): lax.ppermute(x, axis, [(i, (i - shift) % count) for i in range(count)])]
    scatter-add x2 -> x0, other arithmetic: 4.94 us -> none  [the longest x1 2.51 us: step(): column_part = column_part.at[:, right_index].add(grad_j)]
    concatenate x5 -> x0, other arithmetic: 3.67 us -> none  [the longest x4 2.74 us: with_halo(): jnp.concatenate([lax.ppermute(tail, axis, [(i, (i + 1) % count) for i in...]
    pallas_call x0 -> x1, Pallas kernels: none -> 2.78 us  [shards(): pl.pallas_call(functools.partial(edge_kernel, plan), out_shape=(jax.Shape...]
    unnamed x30 -> x14, local copies, waits for them, and re-layouts: 3.51 us -> 1.35 us
    dot_general x4 -> x0, matrix products: 2.03 us -> none  [the longest x1 0.89 us: pack_block(): jnp.einsum('sc,...sa->...ca', emb_table.astype(jnp.float32), onehot)]
    ppermute x12, starting transfers between devices: 15.6 us -> 13.8 us  [fetch(): lax.ppermute(x, axis, [(i, (i - shift) % count) for i in range(count)])]
  transfers between devices with their start and end apart: 12 -> 12, of which waited for: 7 -> 4; matrix products, arithmetic and copies ran while one was open for 26% -> 0% of each run, Pallas kernels for 0% -> 0%
where the time goes in v1:
time: 30 us; the launch traced here: 29.8 us
  starting transfers between devices  13.8 us (46%)
  waiting for transfers between devices  8.62 us (29%)
  Pallas kernels  2.78 us (9%)
  local copies, waits for them, and re-layouts  2.49 us (8%)
  between operations  1.4 us (5%)
  other arithmetic  0.68 us (2%)
    ppermute x12, starting transfers between devices, fetch(): lax.ppermute(x, axis, [(i, (i - shift) % count) for i in range(count)])  13.8 us
    ppermute x12, waiting for transfers between devices, fetch(): lax.ppermute(x, axis, [(i, (i - shift) % count) for i in range(count)])  8.62 us
    pallas_call x1, Pallas kernels, shards(): pl.pallas_call(functools.partial(edge_kernel, plan), out_shape=(jax.Shape...  2.78 us
    unnamed x14, local copies, waits for them, and re-layouts  1.35 us
    concatenate x1, local copies, waits for them, and re-layouts, shards(): packed = jnp.concatenate([features[0, 0, 0], small], axis=0)  1.12 us
    convert_element_type x1, other arithmetic, shards(): species[0, 0, 0][None, :].astype(F32)  0.66 us
  transfers between devices with their start and end apart: 12, of which 4 were waited for; matrix products, arithmetic and copies ran while one was open for 0% of the time, Pallas kernels for 0%

profile of v1, /device:TPU:0, one launch (start us, length us, event | category | flops | bytes accessed | tf_op | source)
XLA Modules:
  0.0 29.8 jit_solution(138289295282129625)
XLA Ops:
  0.6 0.0 copy-start.5
  0.6 0.7 %convert_bitcast_fusion = bf16[1,128]{1,0:T(2,128)(2,1)S(1)} fusion(s32[1,1,1,128]{3,2,1,0:T(1,128)} %param.11), kind=kLoop, calls=%fused_computation.15 | loop fusion | flops 256 | bytes 768 | tf_op jit(solution)/shard_map/convert_element_type | solution.py:215
  1.3 0.0 copy-done.5
  1.3 0.0 copy-start.4
  1.3 1.1 %concatenate.6.refs_0_.refs_3_ = bf16[592,128]{1,0:T(8,128)(2,1)S(1)} concatenate(bf16[576,128]{1,0:T(8,128)(2,1)} %bitcast.39, bf16[3,128]{1,0:T(4,128)(2,1)S(1)} %get-tuple-element.15, bf16[3,128]{1,0:T(4,128)(2,1)S(1)} %get-tuple-element.14, bf16[1,128]{1,0:T(2,128)(2,1)S(1)} %convert_bitcast_fusion, bf16[9,128]{1,0:T(8,128)(2,1)S(1)} %broadcast_in_dim.3), dimensions={0} | concatenate | bytes 303104 | tf_op jit(solution)/shard_map/concatenate | solution.py:217
  2.5 3.0 %collective-permute-start.2 = (bf16[592,128]{1,0:T(8,128)(2,1)S(1)}, bf16[592,128]{1,0:T(8,128)(2,1)S(1)}, u32[]{:S(2)}, u32[]{:S(2)}) collective-permute-start(bf16[592,128]{1,0:T(8,128)(2,1)S(1)} %concatenate.6.refs_0_.refs_3_), channel_id=1, source_target_pairs={{0,1},{1,0},{2,3},{3,2},{4,5},{5,4},{6,7},{7,6},{8,9},{9,8},{10,11... | collective-permute-start | bytes 454664 | tf_op jit(solution)/shard_map/ppermute | solution.py:21
  5.5 0.7 %collective-permute-start.5 = (bf16[592,128]{1,0:T(8,128)(2,1)S(1)}, bf16[592,128]{1,0:T(8,128)(2,1)S(1)}, u32[]{:S(2)}, u32[]{:S(2)}) collective-permute-start(bf16[592,128]{1,0:T(8,128)(2,1)S(1)} %concatenate.6.refs_0_.refs_3_), channel_id=1, source_target_pairs={{0,6},{2,0},{4,2},{6,4},{1,7},{3,1},{5,3},{7,5},{8,14},{10,8},{12,... | collective-permute-start | bytes 454664 | tf_op jit(solution)/shard_map/ppermute | solution.py:21
  6.2 0.0 collective-permute-start.3
  6.2 3.6 %collective-permute-start.1 = (bf16[592,128]{1,0:T(8,128)(2,1)S(1)}, bf16[592,128]{1,0:T(8,128)(2,1)S(1)}, u32[]{:S(2)}, u32[]{:S(2)}) collective-permute-start(bf16[592,128]{1,0:T(8,128)(2,1)S(1)} %concatenate.6.refs_0_.refs_3_), channel_id=1, source_target_pairs={{0,24},{8,0},{16,8},{24,16},{1,25},{9,1},{17,9},{25,17},{2,26},{10... | collective-permute-start | bytes 454664 | tf_op jit(solution)/shard_map/ppermute | solution.py:21
  9.8 0.0 collective-permute-start
  9.8 0.0 collective-permute-done.2.refs_4_
  9.8 1.5 %collective-permute-start.6 = (bf16[592,128]{1,0:T(8,128)(2,1)S(1)}, bf16[592,128]{1,0:T(8,128)(2,1)S(1)}, u32[]{:S(2)}, u32[]{:S(2)}) collective-permute-start(bf16[592,128]{1,0:T(8,128)(2,1)S(1)} %collective-permute-done.2.refs_4_), channel_id=1, source_target_pairs={{0,6},{2,0},{4,2},{6,4},{1,7},{3,1},{5,3},{7,5},{8,14},{10,8},{12,... | collective-permute-start | bytes 454664 | tf_op jit(solution)/shard_map/ppermute | solution.py:21
  11.2 0.0 collective-permute-done.5.refs_7_
  11.2 0.1 collective-permute-start.4
  12.0 0.0 copy-done.4
  12.0 0.0 copy-start
  12.0 0.0 copy-start.2
  12.0 0.1 copy.11.refs_12_
  12.2 0.0 copy-start.1
  12.2 0.0 collective-permute-done.3.refs_5_
  12.2 1.9 %collective-permute-done.1.refs_2_ = bf16[592,128]{1,0:T(8,128)(2,1)S(1)} collective-permute-done((bf16[592,128]{1,0:T(8,128)(2,1)S(1)}, bf16[592,128]{1,0:T(8,128)(2,1)S(1)}, u32[]{:S(2)}, u32[]{:S(2)}) %collective-permute-start.1) | collective-permute-done | bytes 151584 | tf_op jit(solution)/shard_map/ppermute | solution.py:21
  14.1 4.1 %collective-permute-done.refs_1_ = bf16[592,128]{1,0:T(8,128)(2,1)S(1)} collective-permute-done((bf16[592,128]{1,0:T(8,128)(2,1)S(1)}, bf16[592,128]{1,0:T(8,128)(2,1)S(1)}, u32[]{:S(2)}, u32[]{:S(2)}) %collective-permute-start) | collective-permute-done | bytes 151584 | tf_op jit(solution)/shard_map/ppermute | solution.py:21
  18.2 0.0 collective-permute-done.6.refs_8_
  18.2 0.0 collective-permute-done.4.refs_6_
  18.2 0.0 copy-start.3
  18.2 0.0 copy-done
  18.2 0.0 copy-done.2
  18.3 0.0 copy-done.1
  18.3 0.6 %copy-done.3 = bf16[64]{0:T(256)(128)(2,1)S(1)} copy-done((bf16[64]{0:T(256)(128)(2,1)S(1)}, bf16[64]{0:T(256)(128)(2,1)}, u32[]{:S(2)}) %copy-start.3) | copy-done | bytes 152
  18.9 2.8 %edge_work.1 = (f32[1,512]{1,0:T(1,128)}, f32[2,3,128]{2,1,0:T(4,128)S(1)}, f32[3,2,3,128]{3,2,1,0:T(4,128)S(1)}) custom-call(bf16[592,128]{1,0:T(8,128)(2,1)S(1)} %concatenate.6.refs_0_.refs_3_, bf16[592,128]{1,0:T(8,128)(2,1)S(1)} %collective-permute-done.refs_1_, bf16[592,128]{1,0:T(8,128)(2,1)S(1)} %collective-permute-done.1.refs_2_, ...), custom_call_target="tpu_custom_call" | custom-call | tf_op jit(solution)/shard_map/edge_work/pallas_call | solution.py:233
  21.7 0.6 %collective-permute-start.9 = (f32[3,3,128]{2,1,0:T(4,128)S(1)}, f32[3,3,128]{2,1,0:T(4,128)S(1)}, u32[]{:S(2)}, u32[]{:S(2)}) collective-permute-start(f32[3,3,128]{2,1,0:T(4,128)S(1)} %slice_bitcast_fusion.1), channel_id=1, source_target_pairs={{0,1},{1,0},{2,3},{3,2},{4,5},{5,4},{6,7},{7,6},{8,9},{9,8},{10,11... | collective-permute-start | bytes 13832 | tf_op jit(solution)/shard_map/ppermute | solution.py:21
  22.2 1.6 %collective-permute-start.8 = (f32[3,128]{1,0:T(4,128)S(1)}, f32[3,128]{1,0:T(4,128)S(1)}, u32[]{:S(2)}, u32[]{:S(2)}) collective-permute-start(f32[3,128]{1,0:T(4,128)S(1)} %get-tuple-element.12), channel_id=1, source_target_pairs={{0,8},{8,16},{16,24},{24,0},{1,9},{9,17},{17,25},{25,1},{2,10},{10... | collective-permute-start | bytes 4616 | tf_op jit(solution)/shard_map/ppermute | solution.py:21
  23.9 2.2 %collective-permute-start.7 = (f32[3,128]{1,0:T(4,128)S(1)}, f32[3,128]{1,0:T(4,128)S(1)}, u32[]{:S(2)}, u32[]{:S(2)}) collective-permute-start(f32[3,128]{1,0:T(4,128)S(1)} %get-tuple-element.13), channel_id=1, source_target_pairs={{0,24},{8,0},{16,8},{24,16},{1,25},{9,1},{17,9},{25,17},{2,26},{10... | collective-permute-start | bytes 4616 | tf_op jit(solution)/shard_map/ppermute | solution.py:21
  26.1 0.0 collective-permute-done.9
  26.1 0.1 collective-permute-start.10
  26.1 0.5 %collective-permute-start.11 = (f32[3,128]{1,0:T(4,128)S(1)}, f32[3,128]{1,0:T(4,128)S(1)}, u32[]{:S(2)}, u32[]{:S(2)}) collective-permute-start(f32[3,128]{1,0:T(4,128)S(1)} %get-tuple-element.11), channel_id=1, source_target_pairs={{0,2},{2,4},{4,6},{6,0},{1,3},{3,5},{5,7},{7,1},{8,10},{10,12},{12... | collective-permute-start | bytes 4616 | tf_op jit(solution)/shard_map/ppermute | solution.py:21
  26.6 1.0 %collective-permute-done.8 = f32[3,128]{1,0:T(4,128)S(1)} collective-permute-done((f32[3,128]{1,0:T(4,128)S(1)}, f32[3,128]{1,0:T(4,128)S(1)}, u32[]{:S(2)}, u32[]{:S(2)}) %collective-permute-start.8) | collective-permute-done | bytes 1568 | tf_op jit(solution)/shard_map/ppermute | solution.py:21
  27.6 0.0 collective-permute-done.7
  27.6 0.0 collective-permute-done.10
  27.6 1.6 %collective-permute-done.11 = f32[3,128]{1,0:T(4,128)S(1)} collective-permute-done((f32[3,128]{1,0:T(4,128)S(1)}, f32[3,128]{1,0:T(4,128)S(1)}, u32[]{:S(2)}, u32[]{:S(2)}) %collective-permute-start.11) | collective-permute-done | bytes 1568 | tf_op jit(solution)/shard_map/ppermute | solution.py:21
  29.2 0.6 %copy.13 = f32[1,1,1,3,128]{4,2,3,1,0:T(1,128)} copy(f32[1,1,1,3,128]{4,3,2,1,0:T(4,128)S(1)} %fusion.5) | data formatting | bytes 3072
  (7 shorter events, 0.0 us)
Async XLA Ops:
  0.6 0.7 %copy-start.5 = (f32[1,1,1,3,128]{4,2,3,1,0:T(1,128)S(1)}, f32[1,1,1,3,128]{4,2,3,1,0:T(1,128)}, u32[]{:S(2)}) copy-start(f32[1,1,1,3,128]{4,2,3,1,0:T(1,128)} %param.9) | copy-start | bytes 4612
  1.3 10.7 %copy-start.4 = (bf16[128,328]{0,1:T(8,128)(2,1)S(1)}, bf16[128,328]{0,1:T(8,128)(2,1)}, u32[]{:S(2)}) copy-start(bf16[128,328]{0,1:T(8,128)(2,1)} %param.15) | copy-start | bytes 251908
  2.5 7.3 %collective-permute-start.2 = (bf16[592,128]{1,0:T(8,128)(2,1)S(1)}, bf16[592,128]{1,0:T(8,128)(2,1)S(1)}, u32[]{:S(2)}, u32[]{:S(2)}) collective-permute-start(bf16[592,128]{1,0:T(8,128)(2,1)S(1)} %concatenate.6.refs_0_.refs_3_), channel_id=1, source_target_pairs={{0,1},{1,0},{2,3},{3,2},{4,5},{5,4},{6,7},{7,6},{8,9},{9,8},{10,11... | collective-permute-start | bytes 454664 | tf_op jit(solution)/shard_map/ppermute | solution.py:21
  5.5 5.8 %collective-permute-start.5 = (bf16[592,128]{1,0:T(8,128)(2,1)S(1)}, bf16[592,128]{1,0:T(8,128)(2,1)S(1)}, u32[]{:S(2)}, u32[]{:S(2)}) collective-permute-start(bf16[592,128]{1,0:T(8,128)(2,1)S(1)} %concatenate.6.refs_0_.refs_3_), channel_id=1, source_target_pairs={{0,6},{2,0},{4,2},{6,4},{1,7},{3,1},{5,3},{7,5},{8,14},{10,8},{12,... | collective-permute-start | bytes 454664 | tf_op jit(solution)/shard_map/ppermute | solution.py:21
  6.2 6.0 %collective-permute-start.3 = (bf16[592,128]{1,0:T(8,128)(2,1)S(1)}, bf16[592,128]{1,0:T(8,128)(2,1)S(1)}, u32[]{:S(2)}, u32[]{:S(2)}) collective-permute-start(bf16[592,128]{1,0:T(8,128)(2,1)S(1)} %concatenate.6.refs_0_.refs_3_), channel_id=1, source_target_pairs={{0,2},{2,4},{4,6},{6,0},{1,3},{3,5},{5,7},{7,1},{8,10},{10,12},{12... | collective-permute-start | bytes 454664 | tf_op jit(solution)/shard_map/ppermute | solution.py:21
  6.2 8.0 %collective-permute-start.1 = (bf16[592,128]{1,0:T(8,128)(2,1)S(1)}, bf16[592,128]{1,0:T(8,128)(2,1)S(1)}, u32[]{:S(2)}, u32[]{:S(2)}) collective-permute-start(bf16[592,128]{1,0:T(8,128)(2,1)S(1)} %concatenate.6.refs_0_.refs_3_), channel_id=1, source_target_pairs={{0,24},{8,0},{16,8},{24,16},{1,25},{9,1},{17,9},{25,17},{2,26},{10... | collective-permute-start | bytes 454664 | tf_op jit(solution)/shard_map/ppermute | solution.py:21
  9.8 8.5 %collective-permute-start = (bf16[592,128]{1,0:T(8,128)(2,1)S(1)}, bf16[592,128]{1,0:T(8,128)(2,1)S(1)}, u32[]{:S(2)}, u32[]{:S(2)}) collective-permute-start(bf16[592,128]{1,0:T(8,128)(2,1)S(1)} %concatenate.6.refs_0_.refs_3_), channel_id=1, source_target_pairs={{0,8},{8,16},{16,24},{24,0},{1,9},{9,17},{17,25},{25,1},{2,10},{10... | collective-permute-start | bytes 454664 | tf_op jit(solution)/shard_map/ppermute | solution.py:21
  9.8 8.5 %collective-permute-start.6 = (bf16[592,128]{1,0:T(8,128)(2,1)S(1)}, bf16[592,128]{1,0:T(8,128)(2,1)S(1)}, u32[]{:S(2)}, u32[]{:S(2)}) collective-permute-start(bf16[592,128]{1,0:T(8,128)(2,1)S(1)} %collective-permute-done.2.refs_4_), channel_id=1, source_target_pairs={{0,6},{2,0},{4,2},{6,4},{1,7},{3,1},{5,3},{7,5},{8,14},{10,8},{12,... | collective-permute-start | bytes 454664 | tf_op jit(solution)/shard_map/ppermute | solution.py:21
  11.2 7.0 %collective-permute-start.4 = (bf16[592,128]{1,0:T(8,128)(2,1)S(1)}, bf16[592,128]{1,0:T(8,128)(2,1)S(1)}, u32[]{:S(2)}, u32[]{:S(2)}) collective-permute-start(bf16[592,128]{1,0:T(8,128)(2,1)S(1)} %collective-permute-done.2.refs_4_), channel_id=1, source_target_pairs={{0,2},{2,4},{4,6},{6,0},{1,3},{3,5},{5,7},{7,1},{8,10},{10,12},{12... | collective-permute-start | bytes 454664 | tf_op jit(solution)/shard_map/ppermute | solution.py:21
  12.0 6.2 %copy-start = (bf16[64,128]{1,0:T(8,128)(2,1)S(1)}, bf16[64,128]{1,0:T(8,128)(2,1)}, u32[]{:S(2)}) copy-start(bf16[64,128]{1,0:T(8,128)(2,1)} %refs_13_.1) | copy-start | bytes 49156
  12.0 6.2 %copy-start.2 = (bf16[6,64]{1,0:T(8,128)(2,1)S(1)}, bf16[6,64]{1,0:T(8,128)(2,1)}, u32[]{:S(2)}) copy-start(bf16[6,64]{1,0:T(8,128)(2,1)} %refs_11_.1) | copy-start | bytes 2308
  12.2 6.1 %copy-start.1 = (s32[1,1,1,2,512]{4,3,2,1,0:T(2,128)S(1)}, s32[1,1,1,2,512]{4,3,2,1,0:T(2,128)}, u32[]{:S(2)}) copy-start(s32[1,1,1,2,512]{4,3,2,1,0:T(2,128)} %param.13) | copy-start | bytes 12292
  18.2 0.7 %copy-start.3 = (bf16[64]{0:T(256)(128)(2,1)S(1)}, bf16[64]{0:T(256)(128)(2,1)}, u32[]{:S(2)}) copy-start(bf16[64]{0:T(256)(128)(2,1)} %param.17) | copy-start | bytes 388
  21.7 4.4 %collective-permute-start.9 = (f32[3,3,128]{2,1,0:T(4,128)S(1)}, f32[3,3,128]{2,1,0:T(4,128)S(1)}, u32[]{:S(2)}, u32[]{:S(2)}) collective-permute-start(f32[3,3,128]{2,1,0:T(4,128)S(1)} %slice_bitcast_fusion.1), channel_id=1, source_target_pairs={{0,1},{1,0},{2,3},{3,2},{4,5},{5,4},{6,7},{7,6},{8,9},{9,8},{10,11... | collective-permute-start | bytes 13832 | tf_op jit(solution)/shard_map/ppermute | solution.py:21
  22.2 5.4 %collective-permute-start.8 = (f32[3,128]{1,0:T(4,128)S(1)}, f32[3,128]{1,0:T(4,128)S(1)}, u32[]{:S(2)}, u32[]{:S(2)}) collective-permute-start(f32[3,128]{1,0:T(4,128)S(1)} %get-tuple-element.12), channel_id=1, source_target_pairs={{0,8},{8,16},{16,24},{24,0},{1,9},{9,17},{17,25},{25,1},{2,10},{10... | collective-permute-start | bytes 4616 | tf_op jit(solution)/shard_map/ppermute | solution.py:21
  23.9 3.8 %collective-permute-start.7 = (f32[3,128]{1,0:T(4,128)S(1)}, f32[3,128]{1,0:T(4,128)S(1)}, u32[]{:S(2)}, u32[]{:S(2)}) collective-permute-start(f32[3,128]{1,0:T(4,128)S(1)} %get-tuple-element.13), channel_id=1, source_target_pairs={{0,24},{8,0},{16,8},{24,16},{1,25},{9,1},{17,9},{25,17},{2,26},{10... | collective-permute-start | bytes 4616 | tf_op jit(solution)/shard_map/ppermute | solution.py:21
  26.1 1.6 %collective-permute-start.10 = (f32[3,128]{1,0:T(4,128)S(1)}, f32[3,128]{1,0:T(4,128)S(1)}, u32[]{:S(2)}, u32[]{:S(2)}) collective-permute-start(f32[3,128]{1,0:T(4,128)S(1)} %get-tuple-element.10), channel_id=1, source_target_pairs={{0,6},{2,0},{4,2},{6,4},{1,7},{3,1},{5,3},{7,5},{8,14},{10,8},{12,... | collective-permute-start | bytes 4616 | tf_op jit(solution)/shard_map/ppermute | solution.py:21
  26.1 3.1 %collective-permute-start.11 = (f32[3,128]{1,0:T(4,128)S(1)}, f32[3,128]{1,0:T(4,128)S(1)}, u32[]{:S(2)}, u32[]{:S(2)}) collective-permute-start(f32[3,128]{1,0:T(4,128)S(1)} %get-tuple-element.11), channel_id=1, source_target_pairs={{0,2},{2,4},{4,6},{6,0},{1,3},{3,5},{5,7},{7,1},{8,10},{10,12},{12... | collective-permute-start | bytes 4616 | tf_op jit(solution)/shard_map/ppermute | solution.py:21

commit v2 on v1

v2 whole, which is shorter than its diff:
```python
import functools
import math

import jax
import jax.numpy as jnp
from jax import lax
from jax.experimental import pallas as pl
from jax.experimental.pallas import tpu as pltpu
from jax.sharding import PartitionSpec as P

RB = 8
RADIUS = 3.0
SOFTEN = 0.04
EXTRA = 16
F32 = jnp.float32
BF16 = jnp.bfloat16


def moves(axis):
    count = lax.axis_size(axis)
    if count == 1:
        return []
    if count % 2:
        up = [(i, (i + 1) % count) for i in range(count)]
        down = [(i, (i - 1) % count) for i in range(count)]
        return [(up, down), (down, up)]
    first = [(i, i ^ 1) for i in range(count)]
    if count == 2:
        return [(first, first)]
    second = [(i, ((i + 1) if i % 2 else (i - 1)) % count) for i in range(count)]
    return [(first, first), (second, second)]


def which_block(shift, axis, count):
    if count == 1:
        return jnp.zeros_like(shift)
    if count == 2:
        return jnp.where(shift == 1, 0, 1)
    odd = 1 if count % 2 else lax.axis_index(axis) % 2
    return jnp.where(shift == 1, 0, jnp.where(shift == 2, 1 + odd, 2 - odd))


def count_steps(index, step, last):
    out = jnp.zeros_like(index)
    for k in range(1, last):
        out = out + jnp.where(index >= k * step, 1, 0)
    return out


def sigmoid(v):
    return 1.0 / (1.0 + jnp.exp(-v))


def pack_kernel(pos_ref, feat_ref, kind_ref, out_ref, pos_vmem, kind_vmem, sems):
    rows, atoms = feat_ref.shape
    copies = [
        pltpu.make_async_copy(pos_ref, pos_vmem, sems.at[0]),
        pltpu.make_async_copy(kind_ref, kind_vmem, sems.at[1]),
        pltpu.make_async_copy(feat_ref, out_ref.at[pl.ds(0, rows)], sems.at[2]),
    ]
    for copy in copies:
        copy.start()
    copies[0].wait()
    copies[1].wait()
    pos = jnp.concatenate([pos_vmem[k] for k in range(3)], axis=0)
    high = pos.astype(BF16).astype(F32)
    fill = jnp.zeros((EXTRA - 7, atoms), F32)
    small = jnp.concatenate([high, pos - high, kind_vmem[...].astype(F32), fill], axis=0)
    out_ref[pl.ds(rows, EXTRA), :] = small.astype(BF16)
    copies[2].wait()


def pack(positions, features, species):
    rows, atoms = features.shape
    hbm = pl.BlockSpec(memory_space=pltpu.HBM)
    return pl.pallas_call(
        pack_kernel,
        out_shape=jax.ShapeDtypeStruct((rows + EXTRA, atoms), BF16),
        in_specs=[hbm, hbm, hbm],
        out_specs=pl.BlockSpec(memory_space=pltpu.VMEM),
        scratch_shapes=[
            pltpu.VMEM(positions.shape, F32),
            pltpu.VMEM(species.shape, jnp.int32),
            pltpu.SemaphoreType.DMA((3,)),
        ],
        compiler_params=pltpu.CompilerParams(vmem_limit_bytes=4 * 1024 * 1024),
        name="pack",
    )(positions, features, species)


def prep_kernel(plan, edges_hbm, count_ref, emb_hbm, w1_hbm, w2_hbm, wo_hbm, after_ref, *refs):
    n_plate, n_column, n_gz, counts, atoms = plan
    hot_i_ref, hot_j_ref, side_ref, emb_ref, w1_ref, w2_ref, wo_ref, edges_ref, row_ref, sems = refs
    pairs = ((edges_hbm, edges_ref), (emb_hbm, emb_ref), (w1_hbm, w1_ref), (w2_hbm, w2_ref), (wo_hbm, row_ref))
    copies = [pltpu.make_async_copy(src, dst, sems.at[k]) for k, (src, dst) in enumerate(pairs)]
    for copy in copies:
        copy.start()
    for copy in copies:
        copy.wait()
    total = edges_ref.shape[1]
    left = edges_ref[0:1, :]
    right = edges_ref[1:2, :]
    side_i = count_steps(left, atoms, 3)
    row_i = which_block(side_i, "plate", counts[0]) * atoms + (left - side_i * atoms)
    blk_j = count_steps(right, atoms, 9)
    u_j = count_steps(blk_j, 3, 3)
    v_j = blk_j - 3 * u_j
    slot_j = which_block(u_j, "tower", counts[1]) * n_gz + which_block(v_j, "gz", counts[2])
    row_j = slot_j * atoms + (right - blk_j * atoms)
    iota_i = lax.broadcasted_iota(jnp.int32, (n_plate * atoms, total), 0)
    hot_i_ref[...] = jnp.where(iota_i == row_i, 1.0, 0.0).astype(BF16)
    iota_j = lax.broadcasted_iota(jnp.int32, (n_column * atoms, total), 0)
    hot_j_ref[...] = jnp.where(iota_j == row_j, 1.0, 0.0).astype(BF16)
    slots = lax.broadcasted_iota(jnp.int32, (1, total), 1)
    live = jnp.where(slots < count_ref[0], 1, 0)
    side_ref[...] = jnp.concatenate([side_i - 1, u_j - 1, v_j - 1, live] * 2, axis=0).astype(F32)
    chan = row_ref.shape[1]
    eye = lax.broadcasted_iota(jnp.int32, (chan, chan), 0) == lax.broadcasted_iota(jnp.int32, (chan, chan), 1)
    wo_ref[...] = jnp.sum(jnp.where(eye, row_ref[...].astype(F32), 0.0), axis=1, keepdims=True)


def edge_kernel(plan, *refs):
    n_plate, n_column, n_gz, counts, atoms = plan
    block_refs = refs[: n_plate + n_column]
    (hot_i_ref, hot_j_ref, side_ref, emb_ref, w1_ref, w2_ref, wo_ref) = refs[n_plate + n_column : n_plate + n_column + 7]
    energy_ref, plate_ref, column_ref = refs[n_plate + n_column + 7 :]
    rows = block_refs[0].shape[0]
    total = hot_i_ref.shape[1]
    width = (rows - EXTRA) // 9
    hot_i = hot_i_ref[...]
    hot_j = hot_j_ref[...]

    plate_all = jnp.concatenate([block_refs[k][...] for k in range(n_plate)], axis=1)
    column_all = jnp.concatenate([block_refs[n_plate + k][...] for k in range(n_column)], axis=1)
    got_i = jnp.dot(plate_all, hot_i, preferred_element_type=F32)
    got_j = jnp.dot(column_all, hot_j, preferred_element_type=F32)

    base = 9 * width

    def row(got, k):
        return got[base + k : base + k + 1, :]

    d = []
    for axis in range(3):
        ci = row(got_i, axis) + row(got_i, 3 + axis)
        cj = row(got_j, axis) + row(got_j, 3 + axis)
        off = side_ref[axis : axis + 1, :]
        if axis == 0:
            ci = ci + off
        else:
            cj = cj + off
        d.append(cj - ci)
    r2 = d[0] * d[0] + d[1] * d[1] + d[2] * d[2] + SOFTEN
    r = jnp.sqrt(r2)
    inv = 1.0 / r
    nx, ny, nz = d[0] * inv, d[1] * inv, d[2] * inv
    root3, root5, root15 = math.sqrt(3.0), math.sqrt(5.0), math.sqrt(15.0)
    harm = [
        None,
        root3 * nx,
        root3 * ny,
        root3 * nz,
        root15 * nx * ny,
        root15 * ny * nz,
        0.5 * root5 * (3.0 * nz * nz - 1.0),
        root15 * nx * nz,
        0.5 * root15 * (nx * nx - ny * ny),
    ]
    freq = (lax.broadcasted_iota(jnp.int32, (RB, 1), 0) + 1).astype(F32) * (math.pi / RADIUS)
    phase = freq * r
    radial = jnp.sin(phase) * inv
    wave = jnp.cos(phase)
    gap = jnp.maximum(1.0 - r2 / (RADIUS * RADIUS), 0.0)
    env = gap * gap

    def feat(got, m):
        return got[m * width : (m + 1) * width, :]

    def degrees(got):
        one = harm[1] * feat(got, 1) + harm[2] * feat(got, 2) + harm[3] * feat(got, 3)
        two = harm[4] * feat(got, 4)
        for m in range(5, 9):
            two = two + harm[m] * feat(got, m)
        return feat(got, 0), one, two

    s_i = degrees(got_i)
    s_j = degrees(got_j)
    q = jnp.concatenate([(a * b).astype(BF16) for a, b in zip(s_i, s_j)], axis=0)

    kinds = emb_ref.shape[0]
    kind_iota = lax.broadcasted_iota(jnp.int32, (kinds, total), 0).astype(F32)
    tn = (((0,), (0,)), ((), ()))

    def emb_of(got):
        hot = jnp.where(kind_iota == row(got, 6), 1.0, 0.0).astype(BF16)
        return lax.dot_general(emb_ref[...], hot, tn, preferred_element_type=F32).astype(BF16)

    emb = jnp.concatenate([emb_of(got_i), emb_of(got_j)], axis=0)
    w1 = w1_ref[...]
    w_rad = w1[:RB, :]
    w_emb = w1[RB : RB + 2 * width, :]
    w_q = w1[RB + 2 * width :, :]
    pre1 = (
        lax.dot_general(w_q, q, tn, preferred_element_type=F32)
        + lax.dot_general(w_emb, emb, tn, preferred_element_type=F32)
        + lax.dot_general(w_rad, radial.astype(BF16), tn, preferred_element_type=F32)
    )
    sig1 = sigmoid(pre1)
    hidden = (pre1 * sig1).astype(BF16)
    w2 = w2_ref[...]
    pre2 = jnp.dot(w2, hidden, preferred_element_type=F32)
    sig2 = sigmoid(pre2)
    w_out = wo_ref[...]
    score = jnp.sum(w_out * (pre2 * sig2), axis=0, keepdims=True)
    live = side_ref[3:4, :]
    live_env = live * env
    energy_ref[...] = live_env * score

    g2 = (live_env * w_out) * (sig2 * (1.0 + pre2 * (1.0 - sig2)))
    dh = lax.dot_general(w2, g2.astype(BF16), tn, preferred_element_type=F32).astype(BF16).astype(F32)
    g1 = (dh * (sig1 * (1.0 + pre1 * (1.0 - sig1)))).astype(BF16)
    dq = jnp.dot(w_q, g1, preferred_element_type=F32).astype(BF16).astype(F32)
    dradial = jnp.dot(w_rad, g1, preferred_element_type=F32).astype(BF16).astype(F32)
    dy = [None] * 9
    for deg, members in ((1, range(1, 4)), (2, range(4, 9))):
        part = dq[deg * width : (deg + 1) * width, :]
        for_i = part * s_j[deg]
        for_j = part * s_i[deg]
        for m in members:
            dy[m] = jnp.sum(for_i * feat(got_i, m) + for_j * feat(got_j, m), axis=0, keepdims=True)
    gn = [
        root3 * dy[1] + root15 * (ny * dy[4] + nz * dy[7] + nx * dy[8]),
        root3 * dy[2] + root15 * (nx * dy[4] + nz * dy[5] - ny * dy[8]),
        root3 * dy[3] + root15 * (ny * dy[5] + nx * dy[7]) + (3.0 * root5) * nz * dy[6],
    ]
    dr = jnp.sum(dradial * (freq * wave - radial), axis=0, keepdims=True)
    dr = (dr - (gn[0] * nx + gn[1] * ny + gn[2] * nz)) * inv
    dr2 = dr * (0.5 * inv) - (live * score) * gap * (2.0 / (RADIUS * RADIUS))
    grad = jnp.concatenate([gn[k] * inv + 2.0 * d[k] * dr2 for k in range(3)], axis=0)
    high = grad.astype(BF16).astype(F32)
    both = jnp.concatenate([high, grad - high, jnp.zeros((10, total), F32)], axis=0).astype(BF16)
    nt = (((1,), (1,)), ((), ()))

    def spread(hot):
        out = lax.dot_general(both, hot, nt, preferred_element_type=F32)
        return out[0:3, :] + out[3:6, :]

    to_plate = spread(hot_i)
    to_column = spread(hot_j)
    own = to_plate[:, :atoms] - to_column[:, :atoms]
    for k in range(1, n_plate):
        plate_ref[k - 1] = to_plate[:, k * atoms : (k + 1) * atoms]
    column_ref[0, 0] = own
    for k in range(1, n_column):
        column_ref[k // n_gz, k % n_gz] = -to_column[:, k * atoms : (k + 1) * atoms]


def shards(positions, features, species, emb_table, edges, edge_count, w_first, w_second, w_out):
    atoms = positions.shape[-1]
    total = edges.shape[-1]
    packed = pack(positions.reshape(3, 1, atoms), features[0, 0, 0], species[0, 0])

    plate_moves, tower_moves, gz_moves = moves("plate"), moves("tower"), moves("gz")
    n_gz = 1 + len(gz_moves)
    plate_blocks = [packed] + [lax.ppermute(packed, "plate", there) for there, _ in plate_moves]
    gz_blocks = [packed] + [lax.ppermute(packed, "gz", there) for there, _ in gz_moves]
    far = [[lax.ppermute(b, "tower", there) for b in gz_blocks] for there, _ in tower_moves[1:]]
    near = [[lax.ppermute(b, "tower", there) for b in gz_blocks] for there, _ in tower_moves[:1]]
    column_blocks = gz_blocks + [b for blocks in near + far for b in blocks]
    n_plate, n_column = len(plate_blocks), len(column_blocks)

    counts = (lax.axis_size("plate"), lax.axis_size("tower"), lax.axis_size("gz"))
    plan = (n_plate, n_column, n_gz, counts, atoms)
    vmem = pl.BlockSpec(memory_space=pltpu.VMEM)
    hbm = pl.BlockSpec(memory_space=pltpu.HBM)
    smem = pl.BlockSpec(memory_space=pltpu.SMEM)
    w_table = w_first.T
    w_row = w_out.reshape(1, -1)
    edge_list = edges[0, 0, 0]
    prepared = pl.pallas_call(
        functools.partial(prep_kernel, plan),
        out_shape=(
            jax.ShapeDtypeStruct((n_plate * atoms, total), BF16),
            jax.ShapeDtypeStruct((n_column * atoms, total), BF16),
            jax.ShapeDtypeStruct((8, total), F32),
            jax.ShapeDtypeStruct(emb_table.shape, BF16),
            jax.ShapeDtypeStruct(w_table.shape, BF16),
            jax.ShapeDtypeStruct(w_second.shape, BF16),
            jax.ShapeDtypeStruct((w_row.shape[1], 1), F32),
        ),
        in_specs=[hbm, smem, hbm, hbm, hbm, hbm, pl.BlockSpec(memory_space=pl.ANY)],
        out_specs=(vmem,) * 7,
        scratch_shapes=[
            pltpu.VMEM(edge_list.shape, jnp.int32),
            pltpu.VMEM(w_row.shape, BF16),
            pltpu.SemaphoreType.DMA((5,)),
        ],
        compiler_params=pltpu.CompilerParams(vmem_limit_bytes=8 * 1024 * 1024),
        name="prep",
    )(edge_list, edge_count.reshape(1), emb_table, w_table, w_second, w_row, gz_blocks[-1])
    energy, plate_part, column_part = pl.pallas_call(
        functools.partial(edge_kernel, plan),
        out_shape=(
            jax.ShapeDtypeStruct((1, total), F32),
            jax.ShapeDtypeStruct((max(n_plate - 1, 1), 3, atoms), F32),
            jax.ShapeDtypeStruct((1 + len(tower_moves), n_gz, 3, atoms), F32),
        ),
        in_specs=[vmem] * (n_plate + n_column + 7),
        out_specs=(vmem, vmem, vmem),
        compiler_params=pltpu.CompilerParams(vmem_limit_bytes=32 * 1024 * 1024),
        name="edge_work",
    )(*plate_blocks, *column_blocks, *prepared)

    forces = 0.0
    for k, (_, back) in enumerate(plate_moves):
        forces = forces + lax.ppermute(plate_part[k], "plate", back)
    column = column_part[:, 0]
    for k, (_, back) in enumerate(gz_moves):
        column = column + lax.ppermute(column_part[:, 1 + k], "gz", back)
    forces = forces + column[0]
    for k, (_, back) in enumerate(tower_moves):
        forces = forces + lax.ppermute(column[1 + k], "tower", back)
    return (forces.reshape(1, 1, 1, 3, atoms), energy.reshape(1, 1, 1, -1))


def solution(mesh):
    placed = (
        P("plate", "tower", "gz", None, None),
        P("plate", "tower", "gz", None, None),
        P("plate", "tower", "gz", None),
        P(),
        P("plate", "tower", "gz", None, None),
        P("plate", "tower", "gz"),
        P(),
        P(),
        P(),
    )
    return jax.shard_map(
        shards,
        mesh=mesh,
        in_specs=placed,
        out_specs=(P("plate", "tower", "gz", None, None), P("plate", "tower", "gz", None)),
        check_vma=False,
    )
```

time: 30 us -> 28.2 us (0.940)
  starting transfers between devices: 13.8 us -> 11.8 us
  other arithmetic: 0.68 us -> 0.01 us
  Pallas kernels: 2.78 us -> 3.37 us
  local copies, waits for them, and re-layouts: 2.49 us -> 2.82 us
    ppermute x12, starting transfers between devices: 13.8 us -> 11.8 us  [the longest x2 3.6 us: shards(): lax.ppermute(packed, 'plate', there)]
    unnamed x14 -> x17, local copies, waits for them, and re-layouts: 1.35 us -> 2.81 us
    concatenate x1 -> x0, local copies, waits for them, and re-layouts: 1.12 us -> none  [shards(): packed = jnp.concatenate([features[0, 0, 0], small], axis=0)]
    pallas_call x0 -> x2, Pallas kernels: none -> 0.92 us  [the longest x1 0.69 us: shards(): pl.pallas_call(functools.partial(prep_kernel, plan), out_shape=(jax.Shape...]
    convert_element_type x1 -> x0, other arithmetic: 0.66 us -> none  [shards(): species[0, 0, 0][None, :].astype(F32)]
    pallas_call x1, Pallas kernels: 2.78 us -> 2.45 us  [shards(): pl.pallas_call(functools.partial(edge_kernel, plan), out_shape=(jax.Shape...]
  transfers between devices with their start and end apart: 12 -> 12, of which waited for: 4 -> 7; matrix products, arithmetic and copies ran while one was open for 0% -> 0% of each run, Pallas kernels for 0% -> 2%
where the time goes in v2:
time: 28.2 us; the launch traced here: 28 us
  starting transfers between devices  11.8 us (42%)
  waiting for transfers between devices  8.61 us (31%)
  Pallas kernels  3.37 us (12%)
  local copies, waits for them, and re-layouts  2.82 us (10%)
  between operations  1.39 us (5%)
    ppermute x2, waiting for transfers between devices, shards(): lax.ppermute(packed, 'plate', there)  4.34 us
    ppermute x2, starting transfers between devices, shards(): lax.ppermute(packed, 'plate', there)  3.6 us
    ppermute x1, starting transfers between devices, shards(): lax.ppermute(packed, 'gz', there)  3 us
    unnamed x17, local copies, waits for them, and re-layouts  2.81 us
    pallas_call x1, Pallas kernels, shards(): pl.pallas_call(functools.partial(edge_kernel, plan), out_shape=(jax.Shape...  2.45 us
    ppermute x2, starting transfers between devices, shards(): forces = forces + lax.ppermute(plate_part[k], 'plate', back)  2.21 us
    ppermute x2, waiting for transfers between devices, shards(): forces = forces + lax.ppermute(plate_part[k], 'plate', back)  2.07 us
    ppermute x4, starting transfers between devices, shards(): lax.ppermute(b, 'tower', there)  1.75 us
  transfers between devices with their start and end apart: 12, of which 7 were waited for; matrix products, arithmetic and copies ran while one was open for 0% of the time, Pallas kernels for 2%

profile of v2, /device:TPU:0, one launch (start us, length us, event | category | flops | bytes accessed | tf_op | source)
XLA Modules:
  0.0 28.0 jit_solution(16753752812097103756)
XLA Ops:
  0.6 0.0 copy-start.5
  0.6 0.0 copy-start.6
  0.7 0.7 %copy-done.5 = f32[1,1,1,3,128]{4,2,3,1,0:T(1,128)S(1)} copy-done((f32[1,1,1,3,128]{4,2,3,1,0:T(1,128)S(1)}, f32[1,1,1,3,128]{4,2,3,1,0:T(1,128)}, u32[]{:S(2)}) %copy-start.5) | copy-done | bytes 1560
  1.3 0.0 copy-done.6
  1.3 0.0 copy-start
  1.3 0.9 %copy-done = bf16[1,1,1,576,128]{4,3,2,1,0:T(8,128)(2,1)S(1)} copy-done((bf16[1,1,1,576,128]{4,3,2,1,0:T(8,128)(2,1)S(1)}, bf16[1,1,1,576,128]{4,3,2,1,0:T(8,128)(2,1)}, u32[]{:S(2)}) %copy-start) | copy-done | bytes 147480
  2.2 0.0 copy-start.1
  2.2 0.0 copy-start.2
  2.2 0.2 pack.1.refs_0_.refs_3_
  2.5 3.0 %collective-permute-start.2 = (bf16[592,128]{1,0:T(8,128)(2,1)S(1)}, bf16[592,128]{1,0:T(8,128)(2,1)S(1)}, u32[]{:S(2)}, u32[]{:S(2)}) collective-permute-start(bf16[592,128]{1,0:T(8,128)(2,1)S(1)} %pack.1.refs_0_.refs_3_), channel_id=1, source_target_pairs={{0,1},{1,0},{2,3},{3,2},{4,5},{5,4},{6,7},{7,6},{8,9},{9,8},{10,11... | collective-permute-start | bytes 454664 | tf_op jit(solution)/shard_map/ppermute | solution.py:266
  5.5 0.7 %collective-permute-start.5 = (bf16[592,128]{1,0:T(8,128)(2,1)S(1)}, bf16[592,128]{1,0:T(8,128)(2,1)S(1)}, u32[]{:S(2)}, u32[]{:S(2)}) collective-permute-start(bf16[592,128]{1,0:T(8,128)(2,1)S(1)} %pack.1.refs_0_.refs_3_), channel_id=1, source_target_pairs={{0,6},{2,4},{4,2},{6,0},{1,7},{3,5},{5,3},{7,1},{8,14},{10,12},{12... | collective-permute-start | bytes 454664 | tf_op jit(solution)/shard_map/ppermute | solution.py:267
  6.1 1.0 %collective-permute-start.3 = (bf16[592,128]{1,0:T(8,128)(2,1)S(1)}, bf16[592,128]{1,0:T(8,128)(2,1)S(1)}, u32[]{:S(2)}, u32[]{:S(2)}) collective-permute-start(bf16[592,128]{1,0:T(8,128)(2,1)S(1)} %pack.1.refs_0_.refs_3_), channel_id=1, source_target_pairs={{0,2},{2,0},{4,6},{6,4},{1,3},{3,1},{5,7},{7,5},{8,10},{10,8},{12,... | collective-permute-start | bytes 454664 | tf_op jit(solution)/shard_map/ppermute | solution.py:268
  7.1 3.6 %collective-permute-start.1 = (bf16[592,128]{1,0:T(8,128)(2,1)S(1)}, bf16[592,128]{1,0:T(8,128)(2,1)S(1)}, u32[]{:S(2)}, u32[]{:S(2)}) collective-permute-start(bf16[592,128]{1,0:T(8,128)(2,1)S(1)} %pack.1.refs_0_.refs_3_), channel_id=1, source_target_pairs={{0,24},{8,16},{16,8},{24,0},{1,25},{9,17},{17,9},{25,1},{2,26},{10... | collective-permute-start | bytes 454664 | tf_op jit(solution)/shard_map/ppermute | solution.py:265
  10.7 0.0 collective-permute-start
  10.7 0.0 collective-permute-done.2.after_ref.refs_4_
  10.7 0.0 collective-permute-start.6
  10.7 0.9 %collective-permute-done.5.refs_7_ = bf16[592,128]{1,0:T(8,128)(2,1)S(1)} collective-permute-done((bf16[592,128]{1,0:T(8,128)(2,1)S(1)}, bf16[592,128]{1,0:T(8,128)(2,1)S(1)}, u32[]{:S(2)}, u32[]{:S(2)}) %collective-permute-start.5) | collective-permute-done | bytes 151584 | tf_op jit(solution)/shard_map/ppermute | solution.py:267
  11.6 0.1 collective-permute-start.4
  12.4 0.0 copy-start.3
  12.4 0.0 copy-start.4
  12.4 0.0 copy-start.7
  12.4 0.0 copy-done.1
  12.4 0.0 copy-done.2
  12.5 0.6 %copy-done.3 = s32[1,1,1,2,512]{4,3,2,1,0:T(2,128)S(1)} copy-done((s32[1,1,1,2,512]{4,3,2,1,0:T(2,128)S(1)}, s32[1,1,1,2,512]{4,3,2,1,0:T(2,128)}, u32[]{:S(2)}) %copy-start.3) | copy-done | bytes 4120
  13.1 0.0 copy-done.4
  13.1 0.0 copy-done.7
  13.1 0.7 %prep.1 = (bf16[384,512]{1,0:T(8,128)(2,1)S(1)}, bf16[768,512]{1,0:T(8,128)(2,1)S(1)}, f32[8,512]{1,0:T(8,128)S(1)}, bf16[6,64]{1,0:T(8,128)(2,1)S(1)}, bf16[328...) custom-call(s32[2,512]{1,0:T(2,128)S(1)} %bitcast.37, s32[1]{0:T(128)} %bitcast.34.count_ref, ...), custom_call_target="tpu_custom_call" | custom-call | tf_op jit(solution)/shard_map/prep/pallas_call | solution.py:280
  13.8 0.0 collective-permute-done.3.refs_5_
  13.8 1.9 %collective-permute-done.1.refs_2_ = bf16[592,128]{1,0:T(8,128)(2,1)S(1)} collective-permute-done((bf16[592,128]{1,0:T(8,128)(2,1)S(1)}, bf16[592,128]{1,0:T(8,128)(2,1)S(1)}, u32[]{:S(2)}, u32[]{:S(2)}) %collective-permute-start.1) | collective-permute-done | bytes 151584 | tf_op jit(solution)/shard_map/ppermute | solution.py:265
  15.7 2.4 %collective-permute-done.refs_1_ = bf16[592,128]{1,0:T(8,128)(2,1)S(1)} collective-permute-done((bf16[592,128]{1,0:T(8,128)(2,1)S(1)}, bf16[592,128]{1,0:T(8,128)(2,1)S(1)}, u32[]{:S(2)}, u32[]{:S(2)}) %collective-permute-start) | collective-permute-done | bytes 151584 | tf_op jit(solution)/shard_map/ppermute | solution.py:265
  18.2 0.0 collective-permute-done.6.refs_8_
  18.2 0.0 collective-permute-done.4.refs_6_
  18.2 2.4 %edge_work.1 = (f32[1,512]{1,0:T(1,128)}, f32[2,3,128]{2,1,0:T(4,128)S(1)}, f32[3,2,3,128]{3,2,1,0:T(4,128)S(1)}) custom-call(bf16[592,128]{1,0:T(8,128)(2,1)S(1)} %pack.1.refs_0_.refs_3_, bf16[592,128]{1,0:T(8,128)(2,1)S(1)} %collective-permute-done.refs_1_, bf16[592,128]{1,0:T(8,128)(2,1)S(1)} %collective-permute-done.1.refs_2_, ...), custom_call_target="tpu_custom_call" | custom-call | tf_op jit(solution)/shard_map/edge_work/pallas_call | solution.py:301
  20.6 0.6 %collective-permute-start.9 = (f32[3,3,128]{2,1,0:T(4,128)S(1)}, f32[3,3,128]{2,1,0:T(4,128)S(1)}, u32[]{:S(2)}, u32[]{:S(2)}) collective-permute-start(f32[3,3,128]{2,1,0:T(4,128)S(1)} %slice_bitcast_fusion.1), channel_id=1, source_target_pairs={{0,1},{1,0},{2,3},{3,2},{4,5},{5,4},{6,7},{7,6},{8,9},{9,8},{10,11... | collective-permute-start | bytes 13832 | tf_op jit(solution)/shard_map/ppermute | solution.py:319
  21.2 2.2 %collective-permute-start.8 = (f32[3,128]{1,0:T(4,128)S(1)}, f32[3,128]{1,0:T(4,128)S(1)}, u32[]{:S(2)}, u32[]{:S(2)}) collective-permute-start(f32[3,128]{1,0:T(4,128)S(1)} %get-tuple-element.26), channel_id=1, source_target_pairs={{0,24},{8,16},{16,8},{24,0},{1,25},{9,17},{17,9},{25,1},{2,26},{10... | collective-permute-start | bytes 4616 | tf_op jit(solution)/shard_map/ppermute | solution.py:316
  23.4 0.0 collective-permute-start.7
  23.4 0.9 %collective-permute-done.9 = f32[3,3,128]{2,1,0:T(4,128)S(1)} collective-permute-done((f32[3,3,128]{2,1,0:T(4,128)S(1)}, f32[3,3,128]{2,1,0:T(4,128)S(1)}, u32[]{:S(2)}, u32[]{:S(2)}) %collective-permute-start.9) | collective-permute-done | bytes 4640 | tf_op jit(solution)/shard_map/ppermute | solution.py:319
  24.3 0.0 collective-permute-start.10
  24.3 0.6 %collective-permute-start.11 = (f32[3,128]{1,0:T(4,128)S(1)}, f32[3,128]{1,0:T(4,128)S(1)}, u32[]{:S(2)}, u32[]{:S(2)}) collective-permute-start(f32[3,128]{1,0:T(4,128)S(1)} %get-tuple-element.25), channel_id=1, source_target_pairs={{0,6},{2,4},{4,2},{6,0},{1,7},{3,5},{5,3},{7,1},{8,14},{10,12},{12... | collective-permute-start | bytes 4616 | tf_op jit(solution)/shard_map/ppermute | solution.py:322
  24.9 1.7 %collective-permute-done.8 = f32[3,128]{1,0:T(4,128)S(1)} collective-permute-done((f32[3,128]{1,0:T(4,128)S(1)}, f32[3,128]{1,0:T(4,128)S(1)}, u32[]{:S(2)}, u32[]{:S(2)}) %collective-permute-start.8) | collective-permute-done | bytes 1568 | tf_op jit(solution)/shard_map/ppermute | solution.py:316
  26.6 0.4 %collective-permute-done.7 = f32[3,128]{1,0:T(4,128)S(1)} collective-permute-done((f32[3,128]{1,0:T(4,128)S(1)}, f32[3,128]{1,0:T(4,128)S(1)}, u32[]{:S(2)}, u32[]{:S(2)}) %collective-permute-start.7) | collective-permute-done | bytes 1568 | tf_op jit(solution)/shard_map/ppermute | solution.py:316
  27.0 0.0 collective-permute-done.10
  27.0 0.4 %collective-permute-done.11 = f32[3,128]{1,0:T(4,128)S(1)} collective-permute-done((f32[3,128]{1,0:T(4,128)S(1)}, f32[3,128]{1,0:T(4,128)S(1)}, u32[]{:S(2)}, u32[]{:S(2)}) %collective-permute-start.11) | collective-permute-done | bytes 1568 | tf_op jit(solution)/shard_map/ppermute | solution.py:322
  27.4 0.6 %copy.12 = f32[1,1,1,3,128]{4,2,3,1,0:T(1,128)} copy(f32[1,1,1,3,128]{4,3,2,1,0:T(4,128)S(1)} %fusion.4) | data formatting | bytes 3072
  (5 shorter events, 0.0 us)
Async XLA Ops:
  0.6 0.7 %copy-start.5 = (f32[1,1,1,3,128]{4,2,3,1,0:T(1,128)S(1)}, f32[1,1,1,3,128]{4,2,3,1,0:T(1,128)}, u32[]{:S(2)}) copy-start(f32[1,1,1,3,128]{4,2,3,1,0:T(1,128)} %param.9) | copy-start | bytes 4612
  0.6 0.7 %copy-start.6 = (s32[1,1,1,128]{3,2,1,0:T(1,128)S(1)}, s32[1,1,1,128]{3,2,1,0:T(1,128)}, u32[]{:S(2)}) copy-start(s32[1,1,1,128]{3,2,1,0:T(1,128)} %param.11) | copy-start | bytes 1540
  1.3 0.9 %copy-start = (bf16[1,1,1,576,128]{4,3,2,1,0:T(8,128)(2,1)S(1)}, bf16[1,1,1,576,128]{4,3,2,1,0:T(8,128)(2,1)}, u32[]{:S(2)}) copy-start(bf16[1,1,1,576,128]{4,3,2,1,0:T(8,128)(2,1)} %param.10) | copy-start | bytes 442372
  2.2 10.2 %copy-start.1 = (bf16[128,328]{0,1:T(8,128)(2,1)S(1)}, bf16[128,328]{0,1:T(8,128)(2,1)}, u32[]{:S(2)}) copy-start(bf16[128,328]{0,1:T(8,128)(2,1)} %param.15) | copy-start | bytes 251908
  2.2 10.2 %copy-start.2 = (bf16[64,128]{1,0:T(8,128)(2,1)S(1)}, bf16[64,128]{1,0:T(8,128)(2,1)}, u32[]{:S(2)}) copy-start(bf16[64,128]{1,0:T(8,128)(2,1)} %w2_hbm.1) | copy-start | bytes 49156
  2.5 8.2 %collective-permute-start.2 = (bf16[592,128]{1,0:T(8,128)(2,1)S(1)}, bf16[592,128]{1,0:T(8,128)(2,1)S(1)}, u32[]{:S(2)}, u32[]{:S(2)}) collective-permute-start(bf16[592,128]{1,0:T(8,128)(2,1)S(1)} %pack.1.refs_0_.refs_3_), channel_id=1, source_target_pairs={{0,1},{1,0},{2,3},{3,2},{4,5},{5,4},{6,7},{7,6},{8,9},{9,8},{10,11... | collective-permute-start | bytes 454664 | tf_op jit(solution)/shard_map/ppermute | solution.py:266
  5.5 6.2 %collective-permute-start.5 = (bf16[592,128]{1,0:T(8,128)(2,1)S(1)}, bf16[592,128]{1,0:T(8,128)(2,1)S(1)}, u32[]{:S(2)}, u32[]{:S(2)}) collective-permute-start(bf16[592,128]{1,0:T(8,128)(2,1)S(1)} %pack.1.refs_0_.refs_3_), channel_id=1, source_target_pairs={{0,6},{2,4},{4,2},{6,0},{1,7},{3,5},{5,3},{7,1},{8,14},{10,12},{12... | collective-permute-start | bytes 454664 | tf_op jit(solution)/shard_map/ppermute | solution.py:267
  6.1 7.7 %collective-permute-start.3 = (bf16[592,128]{1,0:T(8,128)(2,1)S(1)}, bf16[592,128]{1,0:T(8,128)(2,1)S(1)}, u32[]{:S(2)}, u32[]{:S(2)}) collective-permute-start(bf16[592,128]{1,0:T(8,128)(2,1)S(1)} %pack.1.refs_0_.refs_3_), channel_id=1, source_target_pairs={{0,2},{2,0},{4,6},{6,4},{1,3},{3,1},{5,7},{7,5},{8,10},{10,8},{12,... | collective-permute-start | bytes 454664 | tf_op jit(solution)/shard_map/ppermute | solution.py:268
  7.1 8.6 %collective-permute-start.1 = (bf16[592,128]{1,0:T(8,128)(2,1)S(1)}, bf16[592,128]{1,0:T(8,128)(2,1)S(1)}, u32[]{:S(2)}, u32[]{:S(2)}) collective-permute-start(bf16[592,128]{1,0:T(8,128)(2,1)S(1)} %pack.1.refs_0_.refs_3_), channel_id=1, source_target_pairs={{0,24},{8,16},{16,8},{24,0},{1,25},{9,17},{17,9},{25,1},{2,26},{10... | collective-permute-start | bytes 454664 | tf_op jit(solution)/shard_map/ppermute | solution.py:265
  10.7 7.5 %collective-permute-start = (bf16[592,128]{1,0:T(8,128)(2,1)S(1)}, bf16[592,128]{1,0:T(8,128)(2,1)S(1)}, u32[]{:S(2)}, u32[]{:S(2)}) collective-permute-start(bf16[592,128]{1,0:T(8,128)(2,1)S(1)} %pack.1.refs_0_.refs_3_), channel_id=1, source_target_pairs={{0,8},{8,0},{16,24},{24,16},{1,9},{9,1},{17,25},{25,17},{2,10},{10... | collective-permute-start | bytes 454664 | tf_op jit(solution)/shard_map/ppermute | solution.py:265
  10.7 7.4 %collective-permute-start.6 = (bf16[592,128]{1,0:T(8,128)(2,1)S(1)}, bf16[592,128]{1,0:T(8,128)(2,1)S(1)}, u32[]{:S(2)}, u32[]{:S(2)}) collective-permute-start(bf16[592,128]{1,0:T(8,128)(2,1)S(1)} %collective-permute-done.2.after_ref.refs_4_), channel_id=1, source_target_pairs={{0,6},{2,4},{4,2},{6,0},{1,7},{3,5},{5,3},{7,1},{8,14},{10,12},{12... | collective-permute-start | bytes 454664 | tf_op jit(solution)/shard_map/ppermute | solution.py:267
  11.6 6.5 %collective-permute-start.4 = (bf16[592,128]{1,0:T(8,128)(2,1)S(1)}, bf16[592,128]{1,0:T(8,128)(2,1)S(1)}, u32[]{:S(2)}, u32[]{:S(2)}) collective-permute-start(bf16[592,128]{1,0:T(8,128)(2,1)S(1)} %collective-permute-done.2.after_ref.refs_4_), channel_id=1, source_target_pairs={{0,2},{2,0},{4,6},{6,4},{1,3},{3,1},{5,7},{7,5},{8,10},{10,8},{12,... | collective-permute-start | bytes 454664 | tf_op jit(solution)/shard_map/ppermute | solution.py:268
  12.4 0.7 %copy-start.3 = (s32[1,1,1,2,512]{4,3,2,1,0:T(2,128)S(1)}, s32[1,1,1,2,512]{4,3,2,1,0:T(2,128)}, u32[]{:S(2)}) copy-start(s32[1,1,1,2,512]{4,3,2,1,0:T(2,128)} %param.13) | copy-start | bytes 12292
  12.4 0.7 %copy-start.4 = (bf16[6,64]{1,0:T(8,128)(2,1)S(1)}, bf16[6,64]{1,0:T(8,128)(2,1)}, u32[]{:S(2)}) copy-start(bf16[6,64]{1,0:T(8,128)(2,1)} %emb_hbm.1) | copy-start | bytes 2308
  12.4 0.7 %copy-start.7 = (bf16[64]{0:T(256)(128)(2,1)S(1)}, bf16[64]{0:T(256)(128)(2,1)}, u32[]{:S(2)}) copy-start(bf16[64]{0:T(256)(128)(2,1)} %param.17) | copy-start | bytes 388
  20.6 3.7 %collective-permute-start.9 = (f32[3,3,128]{2,1,0:T(4,128)S(1)}, f32[3,3,128]{2,1,0:T(4,128)S(1)}, u32[]{:S(2)}, u32[]{:S(2)}) collective-permute-start(f32[3,3,128]{2,1,0:T(4,128)S(1)} %slice_bitcast_fusion.1), channel_id=1, source_target_pairs={{0,1},{1,0},{2,3},{3,2},{4,5},{5,4},{6,7},{7,6},{8,9},{9,8},{10,11... | collective-permute-start | bytes 13832 | tf_op jit(solution)/shard_map/ppermute | solution.py:319
  21.2 5.4 %collective-permute-start.8 = (f32[3,128]{1,0:T(4,128)S(1)}, f32[3,128]{1,0:T(4,128)S(1)}, u32[]{:S(2)}, u32[]{:S(2)}) collective-permute-start(f32[3,128]{1,0:T(4,128)S(1)} %get-tuple-element.26), channel_id=1, source_target_pairs={{0,24},{8,16},{16,8},{24,0},{1,25},{9,17},{17,9},{25,1},{2,26},{10... | collective-permute-start | bytes 4616 | tf_op jit(solution)/shard_map/ppermute | solution.py:316
  23.4 3.6 %collective-permute-start.7 = (f32[3,128]{1,0:T(4,128)S(1)}, f32[3,128]{1,0:T(4,128)S(1)}, u32[]{:S(2)}, u32[]{:S(2)}) collective-permute-start(f32[3,128]{1,0:T(4,128)S(1)} %get-tuple-element.27), channel_id=1, source_target_pairs={{0,8},{8,0},{16,24},{24,16},{1,9},{9,1},{17,25},{25,17},{2,10},{10... | collective-permute-start | bytes 4616 | tf_op jit(solution)/shard_map/ppermute | solution.py:316
  24.3 2.7 %collective-permute-start.10 = (f32[3,128]{1,0:T(4,128)S(1)}, f32[3,128]{1,0:T(4,128)S(1)}, u32[]{:S(2)}, u32[]{:S(2)}) collective-permute-start(f32[3,128]{1,0:T(4,128)S(1)} %get-tuple-element.24), channel_id=1, source_target_pairs={{0,2},{2,0},{4,6},{6,4},{1,3},{3,1},{5,7},{7,5},{8,10},{10,8},{12,... | collective-permute-start | bytes 4616 | tf_op jit(solution)/shard_map/ppermute | solution.py:322
  24.3 3.1 %collective-permute-start.11 = (f32[3,128]{1,0:T(4,128)S(1)}, f32[3,128]{1,0:T(4,128)S(1)}, u32[]{:S(2)}, u32[]{:S(2)}) collective-permute-start(f32[3,128]{1,0:T(4,128)S(1)} %get-tuple-element.25), channel_id=1, source_target_pairs={{0,6},{2,4},{4,2},{6,0},{1,7},{3,5},{5,3},{7,1},{8,14},{10,12},{12... | collective-permute-start | bytes 4616 | tf_op jit(solution)/shard_map/ppermute | solution.py:322

commit v3 on v2

--- a/solution.py
+++ b/solution.py
@@ -85,7 +85,7 @@
         ],
         compiler_params=pltpu.CompilerParams(vmem_limit_bytes=4 * 1024 * 1024),
         name="pack",
-    )(positions, features, species)
+    )(*(pltpu.with_memory_space_constraint(x, pltpu.HBM) for x in (positions, features, species)))
 
 
 def prep_kernel(plan, edges_hbm, count_ref, emb_hbm, w1_hbm, w2_hbm, wo_hbm, after_ref, *refs):
@@ -121,7 +121,8 @@
 
 def edge_kernel(plan, *refs):
     n_plate, n_column, n_gz, counts, atoms = plan
-    block_refs = refs[: n_plate + n_column]
+    n_far = n_column - n_gz
+    block_refs = refs[n_column : n_plate + n_column] + refs[n_far:n_column] + refs[:n_far]
     (hot_i_ref, hot_j_ref, side_ref, emb_ref, w1_ref, w2_ref, wo_ref) = refs[n_plate + n_column : n_plate + n_column + 7]
     energy_ref, plate_ref, column_ref = refs[n_plate + n_column + 7 :]
     rows = block_refs[0].shape[0]
@@ -264,8 +265,11 @@
     n_gz = 1 + len(gz_moves)
     plate_blocks = [packed] + [lax.ppermute(packed, "plate", there) for there, _ in plate_moves]
     gz_blocks = [packed] + [lax.ppermute(packed, "gz", there) for there, _ in gz_moves]
-    far = [[lax.ppermute(b, "tower", there) for b in gz_blocks] for there, _ in tower_moves[1:]]
     near = [[lax.ppermute(b, "tower", there) for b in gz_blocks] for there, _ in tower_moves[:1]]
+    relay = list(gz_blocks)
+    if near and gz_moves:
+        relay[1:] = lax.optimization_barrier((*gz_blocks[1:], near[0][0]))[:-1]
+    far = [[lax.ppermute(b, "tower", there) for b in relay] for there, _ in tower_moves[1:]]
     column_blocks = gz_blocks + [b for blocks in near + far for b in blocks]
     n_plate, n_column = len(plate_blocks), len(column_blocks)
 
@@ -297,7 +301,12 @@
         ],
         compiler_params=pltpu.CompilerParams(vmem_limit_bytes=8 * 1024 * 1024),
         name="prep",
-    )(edge_list, edge_count.reshape(1), emb_table, w_table, w_second, w_row, gz_blocks[-1])
+    )(
+        pltpu.with_memory_space_constraint(edge_list, pltpu.HBM),
+        edge_count.reshape(1),
+        *(pltpu.with_memory_space_constraint(w, pltpu.HBM) for w in (emb_table, w_table, w_second, w_row)),
+        gz_blocks[-1],
+    )
     energy, plate_part, column_part = pl.pallas_call(
         functools.partial(edge_kernel, plan),
         out_shape=(
@@ -309,7 +318,7 @@
         out_specs=(vmem, vmem, vmem),
         compiler_params=pltpu.CompilerParams(vmem_limit_bytes=32 * 1024 * 1024),
         name="edge_work",
-    )(*plate_blocks, *column_blocks, *prepared)
+    )(*column_blocks[n_gz:], *column_blocks[:n_gz], *plate_blocks, *prepared)
 
     forces = 0.0
     for k, (_, back) in enumerate(plate_moves):

time: 28.2 us -> 27.4 us (0.972)
  local copies, waits for them, and re-layouts: 2.82 us -> 0.58 us
  Pallas kernels: 3.37 us -> 4.91 us
  starting transfers between devices: 11.8 us -> 13.3 us
  waiting for transfers between devices: 8.61 us -> 7.11 us
    unnamed x17 -> x1, local copies, waits for them, and re-layouts: 2.81 us -> 0.57 us
    ppermute x2, waiting for transfers between devices: 2.07 us -> 0.65 us  [shards(): forces = forces + lax.ppermute(plate_part[k], 'plate', back)]
    ppermute x2, starting transfers between devices: 0.62 us -> 1.63 us  [shards(): forces = forces + lax.ppermute(column[1 + k], 'tower', back)]
    pallas_call x1, Pallas kernels: 0.69 us -> 1.49 us  [shards(): pl.pallas_call(functools.partial(prep_kernel, plan), out_shape=(jax.Shape...]
    ppermute x2, waiting for transfers between devices: 4.34 us -> 3.58 us  [shards(): lax.ppermute(packed, 'plate', there)]
    pallas_call x1, Pallas kernels: 0.23 us -> 0.97 us  [pack(): pl.pallas_call(pack_kernel, out_shape=jax.ShapeDtypeStruct((rows + EXTRA,...]
    ppermute x4, starting transfers between devices: 1.75 us -> 2.21 us  [shards(): lax.ppermute(b, 'tower', there)]
    ppermute x2, waiting for transfers between devices: 0.39 us -> 0.8 us  [shards(): forces = forces + lax.ppermute(column[1 + k], 'tower', back)]
  transfers between devices with their start and end apart: 12 -> 12, of which waited for: 7 -> 6; matrix products, arithmetic and copies ran while one was open for 0% -> 0% of each run, Pallas kernels for 2% -> 5%
where the time goes in v3:
time: 27.4 us; the launch traced here: 27.2 us
  starting transfers between devices  13.3 us (49%)
  waiting for transfers between devices  7.11 us (26%)
  Pallas kernels  4.91 us (18%)
  between operations  1.32 us (5%)
  local copies, waits for them, and re-layouts  0.58 us (2%)
    ppermute x2, starting transfers between devices, shards(): lax.ppermute(packed, 'plate', there)  3.6 us
    ppermute x2, waiting for transfers between devices, shards(): lax.ppermute(packed, 'plate', there)  3.58 us
    ppermute x1, starting transfers between devices, shards(): lax.ppermute(packed, 'gz', there)  3 us
    pallas_call x1, Pallas kernels, shards(): pl.pallas_call(functools.partial(edge_kernel, plan), out_shape=(jax.Shape...  2.45 us
    ppermute x2, starting transfers between devices, shards(): forces = forces + lax.ppermute(plate_part[k], 'plate', back)  2.22 us
    ppermute x4, starting transfers between devices, shards(): lax.ppermute(b, 'tower', there)  2.21 us
    ppermute x2, starting transfers between devices, shards(): forces = forces + lax.ppermute(column[1 + k], 'tower', back)  1.63 us
    pallas_call x1, Pallas kernels, shards(): pl.pallas_call(functools.partial(prep_kernel, plan), out_shape=(jax.Shape...  1.49 us
  transfers between devices with their start and end apart: 12, of which 6 were waited for; matrix products, arithmetic and copies ran while one was open for 0% of the time, Pallas kernels for 5%

profile of v3, /device:TPU:0, one launch (start us, length us, event | category | flops | bytes accessed | tf_op | source)
XLA Modules:
  0.0 27.2 jit_solution(10483696880430306279)
XLA Ops:
  0.6 1.0 %pack.1.refs_4_.refs_6_ = bf16[592,128]{1,0:T(8,128)(2,1)S(1)} custom-call(f32[3,1,128]{2,1,0:T(1,128)} %bitcast.38, bf16[576,128]{1,0:T(8,128)(2,1)} %bitcast.35, s32[1,128]{1,0:T(1,128)} %bitcast.39), custom_call_target="tpu_custom_call" | custom-call | tf_op jit(solution)/shard_map/pack/pallas_call | solution.py:76
  1.6 3.0 %collective-permute-start.1 = (bf16[592,128]{1,0:T(8,128)(2,1)S(1)}, bf16[592,128]{1,0:T(8,128)(2,1)S(1)}, u32[]{:S(2)}, u32[]{:S(2)}) collective-permute-start(bf16[592,128]{1,0:T(8,128)(2,1)S(1)} %pack.1.refs_4_.refs_6_), channel_id=1, source_target_pairs={{0,1},{1,0},{2,3},{3,2},{4,5},{5,4},{6,7},{7,6},{8,9},{9,8},{10,11... | collective-permute-start | bytes 454664 | tf_op jit(solution)/shard_map/ppermute | solution.py:267
  4.6 0.0 collective-permute-start
  4.6 3.6 %collective-permute-start.6 = (bf16[592,128]{1,0:T(8,128)(2,1)S(1)}, bf16[592,128]{1,0:T(8,128)(2,1)S(1)}, u32[]{:S(2)}, u32[]{:S(2)}) collective-permute-start(bf16[592,128]{1,0:T(8,128)(2,1)S(1)} %pack.1.refs_4_.refs_6_), channel_id=1, source_target_pairs={{0,24},{8,16},{16,8},{24,0},{1,25},{9,17},{17,9},{25,1},{2,26},{10... | collective-permute-start | bytes 454664 | tf_op jit(solution)/shard_map/ppermute | solution.py:266
  8.2 0.0 collective-permute-start.5
  8.2 1.4 %collective-permute-start.3 = (bf16[592,128]{1,0:T(8,128)(2,1)S(1)}, bf16[592,128]{1,0:T(8,128)(2,1)S(1)}, u32[]{:S(2)}, u32[]{:S(2)}) collective-permute-start(bf16[592,128]{1,0:T(8,128)(2,1)S(1)} %pack.1.refs_4_.refs_6_), channel_id=1, source_target_pairs={{0,6},{2,4},{4,2},{6,0},{1,7},{3,5},{5,3},{7,1},{8,14},{10,12},{12... | collective-permute-start | bytes 454664 | tf_op jit(solution)/shard_map/ppermute | solution.py:272
  9.6 0.0 collective-permute-done.1.after_ref.refs_5_
  9.6 0.0 collective-permute-done.refs_0_
  9.6 0.3 %collective-permute-start.2 = (bf16[592,128]{1,0:T(8,128)(2,1)S(1)}, bf16[592,128]{1,0:T(8,128)(2,1)S(1)}, u32[]{:S(2)}, u32[]{:S(2)}) collective-permute-start(bf16[592,128]{1,0:T(8,128)(2,1)S(1)} %collective-permute-done.1.after_ref.refs_5_), channel_id=1, source_target_pairs={{0,2},{2,0},{4,6},{6,4},{1,3},{3,1},{5,7},{7,5},{8,10},{10,8},{12,... | collective-permute-start | bytes 454664 | tf_op jit(solution)/shard_map/ppermute | solution.py:268
  9.9 0.6 %collective-permute-start.4 = (bf16[592,128]{1,0:T(8,128)(2,1)S(1)}, bf16[592,128]{1,0:T(8,128)(2,1)S(1)}, u32[]{:S(2)}, u32[]{:S(2)}) collective-permute-start(bf16[592,128]{1,0:T(8,128)(2,1)S(1)} %collective-permute-done.1.after_ref.refs_5_), channel_id=1, source_target_pairs={{0,6},{2,4},{4,2},{6,0},{1,7},{3,5},{5,3},{7,1},{8,14},{10,12},{12... | collective-permute-start | bytes 454664 | tf_op jit(solution)/shard_map/ppermute | solution.py:272
  11.1 1.5 %prep.1 = (bf16[384,512]{1,0:T(8,128)(2,1)S(1)}, bf16[768,512]{1,0:T(8,128)(2,1)S(1)}, f32[8,512]{1,0:T(8,128)S(1)}, bf16[6,64]{1,0:T(8,128)(2,1)S(1)}, bf16[328...) custom-call(s32[2,512]{1,0:T(2,128)} %bitcast.37, s32[1]{0:T(128)} %bitcast.34.count_ref, ...), custom_call_target="tpu_custom_call" | custom-call | tf_op jit(solution)/shard_map/prep/pallas_call | solution.py:284
  12.6 0.6 %collective-permute-done.6.refs_8_ = bf16[592,128]{1,0:T(8,128)(2,1)S(1)} collective-permute-done((bf16[592,128]{1,0:T(8,128)(2,1)S(1)}, bf16[592,128]{1,0:T(8,128)(2,1)S(1)}, u32[]{:S(2)}, u32[]{:S(2)}) %collective-permute-start.6) | collective-permute-done | bytes 151584 | tf_op jit(solution)/shard_map/ppermute | solution.py:266
  13.2 3.0 %collective-permute-done.5.refs_7_ = bf16[592,128]{1,0:T(8,128)(2,1)S(1)} collective-permute-done((bf16[592,128]{1,0:T(8,128)(2,1)S(1)}, bf16[592,128]{1,0:T(8,128)(2,1)S(1)}, u32[]{:S(2)}, u32[]{:S(2)}) %collective-permute-start.5) | collective-permute-done | bytes 151584 | tf_op jit(solution)/shard_map/ppermute | solution.py:266
  16.2 0.0 collective-permute-done.3.refs_2_
  16.2 0.0 collective-permute-done.2.refs_1_
  16.2 1.2 %collective-permute-done.4.refs_3_ = bf16[592,128]{1,0:T(8,128)(2,1)S(1)} collective-permute-done((bf16[592,128]{1,0:T(8,128)(2,1)S(1)}, bf16[592,128]{1,0:T(8,128)(2,1)S(1)}, u32[]{:S(2)}, u32[]{:S(2)}) %collective-permute-start.4) | collective-permute-done | bytes 151584 | tf_op jit(solution)/shard_map/ppermute | solution.py:272
  17.4 2.4 %edge_work.1 = (f32[1,512]{1,0:T(1,128)}, f32[2,3,128]{2,1,0:T(4,128)S(1)}, f32[3,2,3,128]{3,2,1,0:T(4,128)S(1)}) custom-call(bf16[592,128]{1,0:T(8,128)(2,1)S(1)} %collective-permute-done.refs_0_, bf16[592,128]{1,0:T(8,128)(2,1)S(1)} %collective-permute-done.2.refs_1_, bf16[592,128]{1,0:T(8,128)(2,1)S(1)} %collective-permute-done.3.refs_2_, ...), custom_call_target="tpu_custom_call" | custom-call | tf_op jit(solution)/shard_map/edge_work/pallas_call | solution.py:310
  19.8 0.6 %collective-permute-start.9 = (f32[3,3,128]{2,1,0:T(4,128)S(1)}, f32[3,3,128]{2,1,0:T(4,128)S(1)}, u32[]{:S(2)}, u32[]{:S(2)}) collective-permute-start(f32[3,3,128]{2,1,0:T(4,128)S(1)} %slice_bitcast_fusion.1), channel_id=1, source_target_pairs={{0,1},{1,0},{2,3},{3,2},{4,5},{5,4},{6,7},{7,6},{8,9},{9,8},{10,11... | collective-permute-start | bytes 13832 | tf_op jit(solution)/shard_map/ppermute | solution.py:328
  20.4 1.6 %collective-permute-start.8 = (f32[3,128]{1,0:T(4,128)S(1)}, f32[3,128]{1,0:T(4,128)S(1)}, u32[]{:S(2)}, u32[]{:S(2)}) collective-permute-start(f32[3,128]{1,0:T(4,128)S(1)} %get-tuple-element.28), channel_id=1, source_target_pairs={{0,24},{8,16},{16,8},{24,0},{1,25},{9,17},{17,9},{25,1},{2,26},{10... | collective-permute-start | bytes 4616 | tf_op jit(solution)/shard_map/ppermute | solution.py:325
  22.0 0.7 %collective-permute-start.7 = (f32[3,128]{1,0:T(4,128)S(1)}, f32[3,128]{1,0:T(4,128)S(1)}, u32[]{:S(2)}, u32[]{:S(2)}) collective-permute-start(f32[3,128]{1,0:T(4,128)S(1)} %get-tuple-element.29), channel_id=1, source_target_pairs={{0,8},{8,0},{16,24},{24,16},{1,9},{9,1},{17,25},{25,17},{2,10},{10... | collective-permute-start | bytes 4616 | tf_op jit(solution)/shard_map/ppermute | solution.py:325
  22.6 0.9 %collective-permute-done.9 = f32[3,3,128]{2,1,0:T(4,128)S(1)} collective-permute-done((f32[3,3,128]{2,1,0:T(4,128)S(1)}, f32[3,3,128]{2,1,0:T(4,128)S(1)}, u32[]{:S(2)}, u32[]{:S(2)}) %collective-permute-start.9) | collective-permute-done | bytes 4640 | tf_op jit(solution)/shard_map/ppermute | solution.py:328
  23.5 0.0 collective-permute-start.10
  23.5 1.6 %collective-permute-start.11 = (f32[3,128]{1,0:T(4,128)S(1)}, f32[3,128]{1,0:T(4,128)S(1)}, u32[]{:S(2)}, u32[]{:S(2)}) collective-permute-start(f32[3,128]{1,0:T(4,128)S(1)} %get-tuple-element.27), channel_id=1, source_target_pairs={{0,6},{2,4},{4,2},{6,0},{1,7},{3,5},{5,3},{7,1},{8,14},{10,12},{12... | collective-permute-start | bytes 4616 | tf_op jit(solution)/shard_map/ppermute | solution.py:331
  25.2 0.6 %collective-permute-done.8 = f32[3,128]{1,0:T(4,128)S(1)} collective-permute-done((f32[3,128]{1,0:T(4,128)S(1)}, f32[3,128]{1,0:T(4,128)S(1)}, u32[]{:S(2)}, u32[]{:S(2)}) %collective-permute-start.8) | collective-permute-done | bytes 1568 | tf_op jit(solution)/shard_map/ppermute | solution.py:325
  25.8 0.0 collective-permute-done.7
  25.8 0.0 collective-permute-done.10
  25.8 0.8 %collective-permute-done.11 = f32[3,128]{1,0:T(4,128)S(1)} collective-permute-done((f32[3,128]{1,0:T(4,128)S(1)}, f32[3,128]{1,0:T(4,128)S(1)}, u32[]{:S(2)}, u32[]{:S(2)}) %collective-permute-start.11) | collective-permute-done | bytes 1568 | tf_op jit(solution)/shard_map/ppermute | solution.py:331
  26.6 0.6 %copy.12 = f32[1,1,1,3,128]{4,2,3,1,0:T(1,128)} copy(f32[1,1,1,3,128]{4,3,2,1,0:T(4,128)S(1)} %fusion.4) | data formatting | bytes 3072
  (5 shorter events, 0.0 us)
Async XLA Ops:
  1.6 8.0 %collective-permute-start.1 = (bf16[592,128]{1,0:T(8,128)(2,1)S(1)}, bf16[592,128]{1,0:T(8,128)(2,1)S(1)}, u32[]{:S(2)}, u32[]{:S(2)}) collective-permute-start(bf16[592,128]{1,0:T(8,128)(2,1)S(1)} %pack.1.refs_4_.refs_6_), channel_id=1, source_target_pairs={{0,1},{1,0},{2,3},{3,2},{4,5},{5,4},{6,7},{7,6},{8,9},{9,8},{10,11... | collective-permute-start | bytes 454664 | tf_op jit(solution)/shard_map/ppermute | solution.py:267
  4.6 5.0 %collective-permute-start = (bf16[592,128]{1,0:T(8,128)(2,1)S(1)}, bf16[592,128]{1,0:T(8,128)(2,1)S(1)}, u32[]{:S(2)}, u32[]{:S(2)}) collective-permute-start(bf16[592,128]{1,0:T(8,128)(2,1)S(1)} %pack.1.refs_4_.refs_6_), channel_id=1, source_target_pairs={{0,2},{2,0},{4,6},{6,4},{1,3},{3,1},{5,7},{7,5},{8,10},{10,8},{12,... | collective-permute-start | bytes 454664 | tf_op jit(solution)/shard_map/ppermute | solution.py:268
  4.6 8.6 %collective-permute-start.6 = (bf16[592,128]{1,0:T(8,128)(2,1)S(1)}, bf16[592,128]{1,0:T(8,128)(2,1)S(1)}, u32[]{:S(2)}, u32[]{:S(2)}) collective-permute-start(bf16[592,128]{1,0:T(8,128)(2,1)S(1)} %pack.1.refs_4_.refs_6_), channel_id=1, source_target_pairs={{0,24},{8,16},{16,8},{24,0},{1,25},{9,17},{17,9},{25,1},{2,26},{10... | collective-permute-start | bytes 454664 | tf_op jit(solution)/shard_map/ppermute | solution.py:266
  8.2 8.0 %collective-permute-start.5 = (bf16[592,128]{1,0:T(8,128)(2,1)S(1)}, bf16[592,128]{1,0:T(8,128)(2,1)S(1)}, u32[]{:S(2)}, u32[]{:S(2)}) collective-permute-start(bf16[592,128]{1,0:T(8,128)(2,1)S(1)} %pack.1.refs_4_.refs_6_), channel_id=1, source_target_pairs={{0,8},{8,0},{16,24},{24,16},{1,9},{9,1},{17,25},{25,17},{2,10},{10... | collective-permute-start | bytes 454664 | tf_op jit(solution)/shard_map/ppermute | solution.py:266
  8.2 8.0 %collective-permute-start.3 = (bf16[592,128]{1,0:T(8,128)(2,1)S(1)}, bf16[592,128]{1,0:T(8,128)(2,1)S(1)}, u32[]{:S(2)}, u32[]{:S(2)}) collective-permute-start(bf16[592,128]{1,0:T(8,128)(2,1)S(1)} %pack.1.refs_4_.refs_6_), channel_id=1, source_target_pairs={{0,6},{2,4},{4,2},{6,0},{1,7},{3,5},{5,3},{7,1},{8,14},{10,12},{12... | collective-permute-start | bytes 454664 | tf_op jit(solution)/shard_map/ppermute | solution.py:272
  9.6 6.6 %collective-permute-start.2 = (bf16[592,128]{1,0:T(8,128)(2,1)S(1)}, bf16[592,128]{1,0:T(8,128)(2,1)S(1)}, u32[]{:S(2)}, u32[]{:S(2)}) collective-permute-start(bf16[592,128]{1,0:T(8,128)(2,1)S(1)} %collective-permute-done.1.after_ref.refs_5_), channel_id=1, source_target_pairs={{0,2},{2,0},{4,6},{6,4},{1,3},{3,1},{5,7},{7,5},{8,10},{10,8},{12,... | collective-permute-start | bytes 454664 | tf_op jit(solution)/shard_map/ppermute | solution.py:268
  9.9 7.5 %collective-permute-start.4 = (bf16[592,128]{1,0:T(8,128)(2,1)S(1)}, bf16[592,128]{1,0:T(8,128)(2,1)S(1)}, u32[]{:S(2)}, u32[]{:S(2)}) collective-permute-start(bf16[592,128]{1,0:T(8,128)(2,1)S(1)} %collective-permute-done.1.after_ref.refs_5_), channel_id=1, source_target_pairs={{0,6},{2,4},{4,2},{6,0},{1,7},{3,5},{5,3},{7,1},{8,14},{10,12},{12... | collective-permute-start | bytes 454664 | tf_op jit(solution)/shard_map/ppermute | solution.py:272
  19.8 3.7 %collective-permute-start.9 = (f32[3,3,128]{2,1,0:T(4,128)S(1)}, f32[3,3,128]{2,1,0:T(4,128)S(1)}, u32[]{:S(2)}, u32[]{:S(2)}) collective-permute-start(f32[3,3,128]{2,1,0:T(4,128)S(1)} %slice_bitcast_fusion.1), channel_id=1, source_target_pairs={{0,1},{1,0},{2,3},{3,2},{4,5},{5,4},{6,7},{7,6},{8,9},{9,8},{10,11... | collective-permute-start | bytes 13832 | tf_op jit(solution)/shard_map/ppermute | solution.py:328
  20.4 5.4 %collective-permute-start.8 = (f32[3,128]{1,0:T(4,128)S(1)}, f32[3,128]{1,0:T(4,128)S(1)}, u32[]{:S(2)}, u32[]{:S(2)}) collective-permute-start(f32[3,128]{1,0:T(4,128)S(1)} %get-tuple-element.28), channel_id=1, source_target_pairs={{0,24},{8,16},{16,8},{24,0},{1,25},{9,17},{17,9},{25,1},{2,26},{10... | collective-permute-start | bytes 4616 | tf_op jit(solution)/shard_map/ppermute | solution.py:325
  22.0 3.8 %collective-permute-start.7 = (f32[3,128]{1,0:T(4,128)S(1)}, f32[3,128]{1,0:T(4,128)S(1)}, u32[]{:S(2)}, u32[]{:S(2)}) collective-permute-start(f32[3,128]{1,0:T(4,128)S(1)} %get-tuple-element.29), channel_id=1, source_target_pairs={{0,8},{8,0},{16,24},{24,16},{1,9},{9,1},{17,25},{25,17},{2,10},{10... | collective-permute-start | bytes 4616 | tf_op jit(solution)/shard_map/ppermute | solution.py:325
  23.5 2.3 %collective-permute-start.10 = (f32[3,128]{1,0:T(4,128)S(1)}, f32[3,128]{1,0:T(4,128)S(1)}, u32[]{:S(2)}, u32[]{:S(2)}) collective-permute-start(f32[3,128]{1,0:T(4,128)S(1)} %get-tuple-element.26), channel_id=1, source_target_pairs={{0,2},{2,0},{4,6},{6,4},{1,3},{3,1},{5,7},{7,5},{8,10},{10,8},{12,... | collective-permute-start | bytes 4616 | tf_op jit(solution)/shard_map/ppermute | solution.py:331
  23.5 3.1 %collective-permute-start.11 = (f32[3,128]{1,0:T(4,128)S(1)}, f32[3,128]{1,0:T(4,128)S(1)}, u32[]{:S(2)}, u32[]{:S(2)}) collective-permute-start(f32[3,128]{1,0:T(4,128)S(1)} %get-tuple-element.27), channel_id=1, source_target_pairs={{0,6},{2,4},{4,2},{6,0},{1,7},{3,5},{5,3},{7,1},{8,14},{10,12},{12... | collective-permute-start | bytes 4616 | tf_op jit(solution)/shard_map/ppermute | solution.py:331

commit v4 on v3

--- a/solution.py
+++ b/solution.py
@@ -28,7 +28,8 @@
     if count == 2:
         return [(first, first)]
     second = [(i, ((i + 1) if i % 2 else (i - 1)) % count) for i in range(count)]
-    return [(first, first), (second, second)]
+    pair = [(first, first), (second, second)]
+    return pair[::-1] if axis == "plate" else pair
 
 
 def which_block(shift, axis, count):
@@ -37,6 +38,8 @@
     if count == 2:
         return jnp.where(shift == 1, 0, 1)
     odd = 1 if count % 2 else lax.axis_index(axis) % 2
+    if axis == "plate" and count % 2 == 0:
+        odd = 1 - odd
     return jnp.where(shift == 1, 0, jnp.where(shift == 2, 1 + odd, 2 - odd))
 
 
@@ -56,7 +59,7 @@
     copies = [
         pltpu.make_async_copy(pos_ref, pos_vmem, sems.at[0]),
         pltpu.make_async_copy(kind_ref, kind_vmem, sems.at[1]),
-        pltpu.make_async_copy(feat_ref, out_ref.at[pl.ds(0, rows)], sems.at[2]),
+        pltpu.make_async_copy(feat_ref, out_ref.at[pl.ds(EXTRA, rows)], sems.at[2]),
     ]
     for copy in copies:
         copy.start()
@@ -66,7 +69,7 @@
     high = pos.astype(BF16).astype(F32)
     fill = jnp.zeros((EXTRA - 7, atoms), F32)
     small = jnp.concatenate([high, pos - high, kind_vmem[...].astype(F32), fill], axis=0)
-    out_ref[pl.ds(rows, EXTRA), :] = small.astype(BF16)
+    out_ref[pl.ds(0, EXTRA), :] = small.astype(BF16)
     copies[2].wait()
 
 
@@ -88,9 +91,10 @@
     )(*(pltpu.with_memory_space_constraint(x, pltpu.HBM) for x in (positions, features, species)))
 
 
-def prep_kernel(plan, edges_hbm, count_ref, emb_hbm, w1_hbm, w2_hbm, wo_hbm, after_ref, *refs):
+def prep_kernel(plan, edges_hbm, count_ref, emb_hbm, w1_hbm, w2_hbm, wo_hbm, *refs):
     n_plate, n_column, n_gz, counts, atoms = plan
-    hot_i_ref, hot_j_ref, side_ref, emb_ref, w1_ref, w2_ref, wo_ref, edges_ref, row_ref, sems = refs
+    held, refs = refs[:n_gz], refs[n_gz:]
+    part_i_ref, part_j_ref, hot_i_ref, hot_j_ref, side_ref, emb_ref, w1_ref, w2_ref, wo_ref, edges_ref, row_ref, sems = refs
     pairs = ((edges_hbm, edges_ref), (emb_hbm, emb_ref), (w1_hbm, w1_ref), (w2_hbm, w2_ref), (wo_hbm, row_ref))
     copies = [pltpu.make_async_copy(src, dst, sems.at[k]) for k, (src, dst) in enumerate(pairs)]
     for copy in copies:
@@ -111,6 +115,9 @@
     hot_i_ref[...] = jnp.where(iota_i == row_i, 1.0, 0.0).astype(BF16)
     iota_j = lax.broadcasted_iota(jnp.int32, (n_column * atoms, total), 0)
     hot_j_ref[...] = jnp.where(iota_j == row_j, 1.0, 0.0).astype(BF16)
+    part_i_ref[...] = jnp.dot(held[0][...], hot_i_ref[pl.ds(0, atoms), :], preferred_element_type=F32)
+    here = jnp.concatenate([ref[...] for ref in held], axis=1)
+    part_j_ref[...] = jnp.dot(here, hot_j_ref[pl.ds(0, n_gz * atoms), :], preferred_element_type=F32)
     slots = lax.broadcasted_iota(jnp.int32, (1, total), 1)
     live = jnp.where(slots < count_ref[0], 1, 0)
     side_ref[...] = jnp.concatenate([side_i - 1, u_j - 1, v_j - 1, live] * 2, axis=0).astype(F32)
@@ -121,25 +128,26 @@
 
 def edge_kernel(plan, *refs):
     n_plate, n_column, n_gz, counts, atoms = plan
-    n_far = n_column - n_gz
-    block_refs = refs[n_column : n_plate + n_column] + refs[n_far:n_column] + refs[:n_far]
-    (hot_i_ref, hot_j_ref, side_ref, emb_ref, w1_ref, w2_ref, wo_ref) = refs[n_plate + n_column : n_plate + n_column + 7]
-    energy_ref, plate_ref, column_ref = refs[n_plate + n_column + 7 :]
-    rows = block_refs[0].shape[0]
-    total = hot_i_ref.shape[1]
+    n_far, n_away = n_column - n_gz, n_plate - 1
+    far_refs, away_refs, refs = refs[:n_far], refs[n_far : n_far + n_away], refs[n_far + n_away :]
+    part_i_ref, part_j_ref, hot_i_ref, hot_j_ref, side_ref, emb_ref, w1_ref, w2_ref, wo_ref = refs[:9]
+    energy_ref, plate_ref, column_ref = refs[9:]
+    rows, total = part_i_ref.shape
     width = (rows - EXTRA) // 9
     hot_i = hot_i_ref[...]
     hot_j = hot_j_ref[...]
 
-    plate_all = jnp.concatenate([block_refs[k][...] for k in range(n_plate)], axis=1)
-    column_all = jnp.concatenate([block_refs[n_plate + k][...] for k in range(n_column)], axis=1)
-    got_i = jnp.dot(plate_all, hot_i, preferred_element_type=F32)
-    got_j = jnp.dot(column_all, hot_j, preferred_element_type=F32)
-
-    base = 9 * width
+    def gather(part, blocks, hot, start):
+        if not blocks:
+            return part
+        block = jnp.concatenate([ref[...] for ref in blocks], axis=1)
+        return part + jnp.dot(block, hot[start * atoms :], preferred_element_type=F32)
+
+    got_i = gather(part_i_ref[...], away_refs, hot_i, 1)
+    got_j = gather(part_j_ref[...], far_refs, hot_j, n_gz)
 
     def row(got, k):
-        return got[base + k : base + k + 1, :]
+        return got[k : k + 1, :]
 
     d = []
     for axis in range(3):
@@ -175,7 +183,7 @@
     env = gap * gap
 
     def feat(got, m):
-        return got[m * width : (m + 1) * width, :]
+        return got[EXTRA + m * width : EXTRA + (m + 1) * width, :]
 
     def degrees(got):
         one = harm[1] * feat(got, 1) + harm[2] * feat(got, 2) + harm[3] * feat(got, 3)
@@ -284,6 +292,8 @@
     prepared = pl.pallas_call(
         functools.partial(prep_kernel, plan),
         out_shape=(
+            jax.ShapeDtypeStruct((packed.shape[0], total), F32),
+            jax.ShapeDtypeStruct((packed.shape[0], total), F32),
             jax.ShapeDtypeStruct((n_plate * atoms, total), BF16),
             jax.ShapeDtypeStruct((n_column * atoms, total), BF16),
             jax.ShapeDtypeStruct((8, total), F32),
@@ -292,20 +302,20 @@
             jax.ShapeDtypeStruct(w_second.shape, BF16),
             jax.ShapeDtypeStruct((w_row.shape[1], 1), F32),
         ),
-        in_specs=[hbm, smem, hbm, hbm, hbm, hbm, pl.BlockSpec(memory_space=pl.ANY)],
-        out_specs=(vmem,) * 7,
+        in_specs=[hbm, smem, hbm, hbm, hbm, hbm] + [vmem] * n_gz,
+        out_specs=(vmem,) * 9,
         scratch_shapes=[
             pltpu.VMEM(edge_list.shape, jnp.int32),
             pltpu.VMEM(w_row.shape, BF16),
             pltpu.SemaphoreType.DMA((5,)),
         ],
-        compiler_params=pltpu.CompilerParams(vmem_limit_bytes=8 * 1024 * 1024),
+        compiler_params=pltpu.CompilerParams(vmem_limit_bytes=16 * 1024 * 1024),
         name="prep",
     )(
         pltpu.with_memory_space_constraint(edge_list, pltpu.HBM),
         edge_count.reshape(1),
         *(pltpu.with_memory_space_constraint(w, pltpu.HBM) for w in (emb_table, w_table, w_second, w_row)),
-        gz_blocks[-1],
+        *gz_blocks,
     )
     energy, plate_part, column_part = pl.pallas_call(
         functools.partial(edge_kernel, plan),
@@ -314,11 +324,11 @@
             jax.ShapeDtypeStruct((max(n_plate - 1, 1), 3, atoms), F32),
             jax.ShapeDtypeStruct((1 + len(tower_moves), n_gz, 3, atoms), F32),
         ),
-        in_specs=[vmem] * (n_plate + n_column + 7),
+        in_specs=[vmem] * (n_plate - 1 + n_column - n_gz + 9),
         out_specs=(vmem, vmem, vmem),
         compiler_params=pltpu.CompilerParams(vmem_limit_bytes=32 * 1024 * 1024),
         name="edge_work",
-    )(*column_blocks[n_gz:], *column_blocks[:n_gz], *plate_blocks, *prepared)
+    )(*column_blocks[n_gz:], *plate_blocks[1:], *prepared)
 
     forces = 0.0
     for k, (_, back) in enumerate(plate_moves):

time: 27.4 us -> 27.1 us (0.989)
  starting transfers between devices: 13.3 us -> 12.3 us
  waiting for transfers between devices: 7.11 us -> 7.69 us
    ppermute x2, waiting for transfers between devices: 0.65 us -> 2.07 us  [shards(): forces = forces + lax.ppermute(plate_part[k], 'plate', back)]
    ppermute x4, waiting for transfers between devices: 1.21 us -> 0.01 us  [shards(): lax.ppermute(b, 'tower', there)]
    ppermute x2, starting transfers between devices: 1.63 us -> 0.62 us  [shards(): forces = forces + lax.ppermute(column[1 + k], 'tower', back)]
    ppermute x2, waiting for transfers between devices: 3.58 us -> 4.34 us  [shards(): lax.ppermute(packed, 'plate', there)]
    ppermute x2, waiting for transfers between devices: 0.8 us -> 0.38 us  [shards(): forces = forces + lax.ppermute(column[1 + k], 'tower', back)]
  transfers between devices with their start and end apart: 12 -> 12, of which waited for: 6 -> 6; matrix products, arithmetic and copies ran while one was open for 0% -> 0% of each run, Pallas kernels for 5% -> 6%
where the time goes in v4:
time: 27.1 us; the launch traced here: 26.9 us
  starting transfers between devices  12.3 us (45%)
  waiting for transfers between devices  7.69 us (28%)
  Pallas kernels  5.03 us (19%)
  between operations  1.33 us (5%)
  local copies, waits for them, and re-layouts  0.58 us (2%)
    ppermute x2, waiting for transfers between devices, shards(): lax.ppermute(packed, 'plate', there)  4.34 us
    ppermute x2, starting transfers between devices, shards(): lax.ppermute(packed, 'plate', there)  3.6 us
    ppermute x1, starting transfers between devices, shards(): lax.ppermute(packed, 'gz', there)  3 us
    pallas_call x1, Pallas kernels, shards(): pl.pallas_call(functools.partial(edge_kernel, plan), out_shape=(jax.Shape...  2.32 us
    ppermute x4, starting transfers between devices, shards(): lax.ppermute(b, 'tower', there)  2.31 us
    ppermute x2, starting transfers between devices, shards(): forces = forces + lax.ppermute(plate_part[k], 'plate', back)  2.22 us
    ppermute x2, waiting for transfers between devices, shards(): forces = forces + lax.ppermute(plate_part[k], 'plate', back)  2.07 us
    pallas_call x1, Pallas kernels, shards(): pl.pallas_call(functools.partial(prep_kernel, plan), out_shape=(jax.Shape...  1.74 us
  transfers between devices with their start and end apart: 12, of which 6 were waited for; matrix products, arithmetic and copies ran while one was open for 0% of the time, Pallas kernels for 6%

profile of v4, /device:TPU:0, one launch (start us, length us, event | category | flops | bytes accessed | tf_op | source)
XLA Modules:
  0.0 26.9 jit_solution(5165489796457025598)
XLA Ops:
  0.6 1.0 %pack.1.refs_0_ = bf16[592,128]{1,0:T(8,128)(2,1)S(1)} custom-call(f32[3,1,128]{2,1,0:T(1,128)} %bitcast.38, bf16[576,128]{1,0:T(8,128)(2,1)} %bitcast.35, s32[1,128]{1,0:T(1,128)} %bitcast.39), custom_call_target="tpu_custom_call" | custom-call | tf_op jit(solution)/shard_map/pack/pallas_call | solution.py:79
  1.6 3.0 %collective-permute-start.1 = (bf16[592,128]{1,0:T(8,128)(2,1)S(1)}, bf16[592,128]{1,0:T(8,128)(2,1)S(1)}, u32[]{:S(2)}, u32[]{:S(2)}) collective-permute-start(bf16[592,128]{1,0:T(8,128)(2,1)S(1)} %pack.1.refs_0_), channel_id=1, source_target_pairs={{0,1},{1,0},{2,3},{3,2},{4,5},{5,4},{6,7},{7,6},{8,9},{9,8},{10,11... | collective-permute-start | bytes 454664 | tf_op jit(solution)/shard_map/ppermute | solution.py:275
  4.6 0.0 collective-permute-start
  4.6 1.6 %collective-permute-start.3 = (bf16[592,128]{1,0:T(8,128)(2,1)S(1)}, bf16[592,128]{1,0:T(8,128)(2,1)S(1)}, u32[]{:S(2)}, u32[]{:S(2)}) collective-permute-start(bf16[592,128]{1,0:T(8,128)(2,1)S(1)} %pack.1.refs_0_), channel_id=1, source_target_pairs={{0,6},{2,4},{4,2},{6,0},{1,7},{3,5},{5,3},{7,1},{8,14},{10,12},{12... | collective-permute-start | bytes 454664 | tf_op jit(solution)/shard_map/ppermute | solution.py:280
  6.2 3.6 %collective-permute-start.5 = (bf16[592,128]{1,0:T(8,128)(2,1)S(1)}, bf16[592,128]{1,0:T(8,128)(2,1)S(1)}, u32[]{:S(2)}, u32[]{:S(2)}) collective-permute-start(bf16[592,128]{1,0:T(8,128)(2,1)S(1)} %pack.1.refs_0_), channel_id=1, source_target_pairs={{0,24},{8,16},{16,8},{24,0},{1,25},{9,17},{17,9},{25,1},{2,26},{10... | collective-permute-start | bytes 454664 | tf_op jit(solution)/shard_map/ppermute | solution.py:274
  9.8 0.0 collective-permute-start.6
  9.9 0.0 collective-permute-done.1.refs_1_
  9.9 0.0 collective-permute-done.refs_0_
  9.9 0.1 collective-permute-start.4
  9.9 0.6 %collective-permute-start.2 = (bf16[592,128]{1,0:T(8,128)(2,1)S(1)}, bf16[592,128]{1,0:T(8,128)(2,1)S(1)}, u32[]{:S(2)}, u32[]{:S(2)}) collective-permute-start(bf16[592,128]{1,0:T(8,128)(2,1)S(1)} %collective-permute-done.1.refs_1_), channel_id=1, source_target_pairs={{0,2},{2,0},{4,6},{6,4},{1,3},{3,1},{5,7},{7,5},{8,10},{10,8},{12,... | collective-permute-start | bytes 454664 | tf_op jit(solution)/shard_map/ppermute | solution.py:276
  11.2 1.7 %prep.1 = (f32[592,512]{1,0:T(8,128)S(1)}, f32[592,512]{1,0:T(8,128)S(1)}, bf16[384,512]{1,0:T(8,128)(2,1)S(1)}, bf16[768,512]{1,0:T(8,128)(2,1)S(1)}, f32[8,512...) custom-call(s32[2,512]{1,0:T(2,128)} %bitcast.37, ...), custom_call_target="tpu_custom_call" | custom-call | tf_op jit(solution)/shard_map/prep/pallas_call | solution.py:292
  12.9 0.0 collective-permute-done.3.refs_2_
  13.0 1.9 %collective-permute-done.5.refs_4_ = bf16[592,128]{1,0:T(8,128)(2,1)S(1)} collective-permute-done((bf16[592,128]{1,0:T(8,128)(2,1)S(1)}, bf16[592,128]{1,0:T(8,128)(2,1)S(1)}, u32[]{:S(2)}, u32[]{:S(2)}) %collective-permute-start.5) | collective-permute-done | bytes 151584 | tf_op jit(solution)/shard_map/ppermute | solution.py:274
  14.9 2.4 %collective-permute-done.6.refs_5_ = bf16[592,128]{1,0:T(8,128)(2,1)S(1)} collective-permute-done((bf16[592,128]{1,0:T(8,128)(2,1)S(1)}, bf16[592,128]{1,0:T(8,128)(2,1)S(1)}, u32[]{:S(2)}, u32[]{:S(2)}) %collective-permute-start.6) | collective-permute-done | bytes 151584 | tf_op jit(solution)/shard_map/ppermute | solution.py:274
  17.3 0.0 collective-permute-done.4.refs_3_
  17.3 0.0 collective-permute-done.2.refs_1_
  17.3 2.3 %edge_work.1 = (f32[1,512]{1,0:T(1,128)}, f32[2,3,128]{2,1,0:T(4,128)S(1)}, f32[3,2,3,128]{3,2,1,0:T(4,128)S(1)}) custom-call(bf16[592,128]{1,0:T(8,128)(2,1)S(1)} %collective-permute-done.refs_0_, bf16[592,128]{1,0:T(8,128)(2,1)S(1)} %collective-permute-done.2.refs_1_, bf16[592,128]{1,0:T(8,128)(2,1)S(1)} %collective-permute-done.3.refs_2_, ...), custom_call_target="tpu_custom_call" | custom-call | tf_op jit(solution)/shard_map/edge_work/pallas_call | solution.py:320
  19.6 0.5 %collective-permute-start.9 = (f32[3,3,128]{2,1,0:T(4,128)S(1)}, f32[3,3,128]{2,1,0:T(4,128)S(1)}, u32[]{:S(2)}, u32[]{:S(2)}) collective-permute-start(f32[3,3,128]{2,1,0:T(4,128)S(1)} %slice_bitcast_fusion.1), channel_id=1, source_target_pairs={{0,1},{1,0},{2,3},{3,2},{4,5},{5,4},{6,7},{7,6},{8,9},{9,8},{10,11... | collective-permute-start | bytes 13832 | tf_op jit(solution)/shard_map/ppermute | solution.py:338
  20.2 2.2 %collective-permute-start.7 = (f32[3,128]{1,0:T(4,128)S(1)}, f32[3,128]{1,0:T(4,128)S(1)}, u32[]{:S(2)}, u32[]{:S(2)}) collective-permute-start(f32[3,128]{1,0:T(4,128)S(1)} %get-tuple-element.33), channel_id=1, source_target_pairs={{0,24},{8,16},{16,8},{24,0},{1,25},{9,17},{17,9},{25,1},{2,26},{10... | collective-permute-start | bytes 4616 | tf_op jit(solution)/shard_map/ppermute | solution.py:335
  22.4 0.0 collective-permute-start.8
  22.4 0.9 %collective-permute-done.9 = f32[3,3,128]{2,1,0:T(4,128)S(1)} collective-permute-done((f32[3,3,128]{2,1,0:T(4,128)S(1)}, f32[3,3,128]{2,1,0:T(4,128)S(1)}, u32[]{:S(2)}, u32[]{:S(2)}) %collective-permute-start.9) | collective-permute-done | bytes 4640 | tf_op jit(solution)/shard_map/ppermute | solution.py:338
  23.3 0.0 collective-permute-start.10
  23.3 0.6 %collective-permute-start.11 = (f32[3,128]{1,0:T(4,128)S(1)}, f32[3,128]{1,0:T(4,128)S(1)}, u32[]{:S(2)}, u32[]{:S(2)}) collective-permute-start(f32[3,128]{1,0:T(4,128)S(1)} %get-tuple-element.31), channel_id=1, source_target_pairs={{0,6},{2,4},{4,2},{6,0},{1,7},{3,5},{5,3},{7,1},{8,14},{10,12},{12... | collective-permute-start | bytes 4616 | tf_op jit(solution)/shard_map/ppermute | solution.py:341
  23.9 1.7 %collective-permute-done.7 = f32[3,128]{1,0:T(4,128)S(1)} collective-permute-done((f32[3,128]{1,0:T(4,128)S(1)}, f32[3,128]{1,0:T(4,128)S(1)}, u32[]{:S(2)}, u32[]{:S(2)}) %collective-permute-start.7) | collective-permute-done | bytes 1568 | tf_op jit(solution)/shard_map/ppermute | solution.py:335
  25.6 0.4 %collective-permute-done.8 = f32[3,128]{1,0:T(4,128)S(1)} collective-permute-done((f32[3,128]{1,0:T(4,128)S(1)}, f32[3,128]{1,0:T(4,128)S(1)}, u32[]{:S(2)}, u32[]{:S(2)}) %collective-permute-start.8) | collective-permute-done | bytes 1568 | tf_op jit(solution)/shard_map/ppermute | solution.py:335
  26.0 0.0 collective-permute-done.10
  26.0 0.4 %collective-permute-done.11 = f32[3,128]{1,0:T(4,128)S(1)} collective-permute-done((f32[3,128]{1,0:T(4,128)S(1)}, f32[3,128]{1,0:T(4,128)S(1)}, u32[]{:S(2)}, u32[]{:S(2)}) %collective-permute-start.11) | collective-permute-done | bytes 1568 | tf_op jit(solution)/shard_map/ppermute | solution.py:341
  26.4 0.6 %copy.12 = f32[1,1,1,3,128]{4,2,3,1,0:T(1,128)} copy(f32[1,1,1,3,128]{4,3,2,1,0:T(4,128)S(1)} %fusion.4) | data formatting | bytes 3072
  (5 shorter events, 0.0 us)
Async XLA Ops:
  1.6 8.2 %collective-permute-start.1 = (bf16[592,128]{1,0:T(8,128)(2,1)S(1)}, bf16[592,128]{1,0:T(8,128)(2,1)S(1)}, u32[]{:S(2)}, u32[]{:S(2)}) collective-permute-start(bf16[592,128]{1,0:T(8,128)(2,1)S(1)} %pack.1.refs_0_), channel_id=1, source_target_pairs={{0,1},{1,0},{2,3},{3,2},{4,5},{5,4},{6,7},{7,6},{8,9},{9,8},{10,11... | collective-permute-start | bytes 454664 | tf_op jit(solution)/shard_map/ppermute | solution.py:275
  4.6 5.2 %collective-permute-start = (bf16[592,128]{1,0:T(8,128)(2,1)S(1)}, bf16[592,128]{1,0:T(8,128)(2,1)S(1)}, u32[]{:S(2)}, u32[]{:S(2)}) collective-permute-start(bf16[592,128]{1,0:T(8,128)(2,1)S(1)} %pack.1.refs_0_), channel_id=1, source_target_pairs={{0,2},{2,0},{4,6},{6,4},{1,3},{3,1},{5,7},{7,5},{8,10},{10,8},{12,... | collective-permute-start | bytes 454664 | tf_op jit(solution)/shard_map/ppermute | solution.py:276
  4.6 8.3 %collective-permute-start.3 = (bf16[592,128]{1,0:T(8,128)(2,1)S(1)}, bf16[592,128]{1,0:T(8,128)(2,1)S(1)}, u32[]{:S(2)}, u32[]{:S(2)}) collective-permute-start(bf16[592,128]{1,0:T(8,128)(2,1)S(1)} %pack.1.refs_0_), channel_id=1, source_target_pairs={{0,6},{2,4},{4,2},{6,0},{1,7},{3,5},{5,3},{7,1},{8,14},{10,12},{12... | collective-permute-start | bytes 454664 | tf_op jit(solution)/shard_map/ppermute | solution.py:280
  6.2 8.6 %collective-permute-start.5 = (bf16[592,128]{1,0:T(8,128)(2,1)S(1)}, bf16[592,128]{1,0:T(8,128)(2,1)S(1)}, u32[]{:S(2)}, u32[]{:S(2)}) collective-permute-start(bf16[592,128]{1,0:T(8,128)(2,1)S(1)} %pack.1.refs_0_), channel_id=1, source_target_pairs={{0,24},{8,16},{16,8},{24,0},{1,25},{9,17},{17,9},{25,1},{2,26},{10... | collective-permute-start | bytes 454664 | tf_op jit(solution)/shard_map/ppermute | solution.py:274
  9.8 7.5 %collective-permute-start.6 = (bf16[592,128]{1,0:T(8,128)(2,1)S(1)}, bf16[592,128]{1,0:T(8,128)(2,1)S(1)}, u32[]{:S(2)}, u32[]{:S(2)}) collective-permute-start(bf16[592,128]{1,0:T(8,128)(2,1)S(1)} %pack.1.refs_0_), channel_id=1, source_target_pairs={{0,8},{8,0},{16,24},{24,16},{1,9},{9,1},{17,25},{25,17},{2,10},{10... | collective-permute-start | bytes 454664 | tf_op jit(solution)/shard_map/ppermute | solution.py:274
  9.9 7.4 %collective-permute-start.4 = (bf16[592,128]{1,0:T(8,128)(2,1)S(1)}, bf16[592,128]{1,0:T(8,128)(2,1)S(1)}, u32[]{:S(2)}, u32[]{:S(2)}) collective-permute-start(bf16[592,128]{1,0:T(8,128)(2,1)S(1)} %collective-permute-done.1.refs_1_), channel_id=1, source_target_pairs={{0,6},{2,4},{4,2},{6,0},{1,7},{3,5},{5,3},{7,1},{8,14},{10,12},{12... | collective-permute-start | bytes 454664 | tf_op jit(solution)/shard_map/ppermute | solution.py:280
  9.9 7.4 %collective-permute-start.2 = (bf16[592,128]{1,0:T(8,128)(2,1)S(1)}, bf16[592,128]{1,0:T(8,128)(2,1)S(1)}, u32[]{:S(2)}, u32[]{:S(2)}) collective-permute-start(bf16[592,128]{1,0:T(8,128)(2,1)S(1)} %collective-permute-done.1.refs_1_), channel_id=1, source_target_pairs={{0,2},{2,0},{4,6},{6,4},{1,3},{3,1},{5,7},{7,5},{8,10},{10,8},{12,... | collective-permute-start | bytes 454664 | tf_op jit(solution)/shard_map/ppermute | solution.py:276
  19.6 3.6 %collective-permute-start.9 = (f32[3,3,128]{2,1,0:T(4,128)S(1)}, f32[3,3,128]{2,1,0:T(4,128)S(1)}, u32[]{:S(2)}, u32[]{:S(2)}) collective-permute-start(f32[3,3,128]{2,1,0:T(4,128)S(1)} %slice_bitcast_fusion.1), channel_id=1, source_target_pairs={{0,1},{1,0},{2,3},{3,2},{4,5},{5,4},{6,7},{7,6},{8,9},{9,8},{10,11... | collective-permute-start | bytes 13832 | tf_op jit(solution)/shard_map/ppermute | solution.py:338
  20.2 5.4 %collective-permute-start.7 = (f32[3,128]{1,0:T(4,128)S(1)}, f32[3,128]{1,0:T(4,128)S(1)}, u32[]{:S(2)}, u32[]{:S(2)}) collective-permute-start(f32[3,128]{1,0:T(4,128)S(1)} %get-tuple-element.33), channel_id=1, source_target_pairs={{0,24},{8,16},{16,8},{24,0},{1,25},{9,17},{17,9},{25,1},{2,26},{10... | collective-permute-start | bytes 4616 | tf_op jit(solution)/shard_map/ppermute | solution.py:335
  22.4 3.6 %collective-permute-start.8 = (f32[3,128]{1,0:T(4,128)S(1)}, f32[3,128]{1,0:T(4,128)S(1)}, u32[]{:S(2)}, u32[]{:S(2)}) collective-permute-start(f32[3,128]{1,0:T(4,128)S(1)} %get-tuple-element.32), channel_id=1, source_target_pairs={{0,8},{8,0},{16,24},{24,16},{1,9},{9,1},{17,25},{25,17},{2,10},{10... | collective-permute-start | bytes 4616 | tf_op jit(solution)/shard_map/ppermute | solution.py:335
  23.3 2.7 %collective-permute-start.10 = (f32[3,128]{1,0:T(4,128)S(1)}, f32[3,128]{1,0:T(4,128)S(1)}, u32[]{:S(2)}, u32[]{:S(2)}) collective-permute-start(f32[3,128]{1,0:T(4,128)S(1)} %get-tuple-element.30), channel_id=1, source_target_pairs={{0,2},{2,0},{4,6},{6,4},{1,3},{3,1},{5,7},{7,5},{8,10},{10,8},{12,... | collective-permute-start | bytes 4616 | tf_op jit(solution)/shard_map/ppermute | solution.py:341
  23.3 3.1 %collective-permute-start.11 = (f32[3,128]{1,0:T(4,128)S(1)}, f32[3,128]{1,0:T(4,128)S(1)}, u32[]{:S(2)}, u32[]{:S(2)}) collective-permute-start(f32[3,128]{1,0:T(4,128)S(1)} %get-tuple-element.31), channel_id=1, source_target_pairs={{0,6},{2,4},{4,2},{6,0},{1,7},{3,5},{5,3},{7,1},{8,14},{10,12},{12... | collective-permute-start | bytes 4616 | tf_op jit(solution)/shard_map/ppermute | solution.py:341

commit v5 on v4

--- a/solution.py
+++ b/solution.py
@@ -29,7 +29,7 @@
         return [(first, first)]
     second = [(i, ((i + 1) if i % 2 else (i - 1)) % count) for i in range(count)]
     pair = [(first, first), (second, second)]
-    return pair[::-1] if axis == "plate" else pair
+    return pair[::-1] if axis in ("plate", "tower") else pair
 
 
 def which_block(shift, axis, count):
@@ -38,7 +38,7 @@
     if count == 2:
         return jnp.where(shift == 1, 0, 1)
     odd = 1 if count % 2 else lax.axis_index(axis) % 2
-    if axis == "plate" and count % 2 == 0:
+    if axis in ("plate", "tower") and count % 2 == 0:
         odd = 1 - odd
     return jnp.where(shift == 1, 0, jnp.where(shift == 2, 1 + odd, 2 - odd))
 
@@ -51,7 +51,7 @@
 
 
 def sigmoid(v):
-    return 1.0 / (1.0 + jnp.exp(-v))
+    return 0.5 + 0.5 * jnp.tanh(0.5 * v)
 
 
 def pack_kernel(pos_ref, feat_ref, kind_ref, out_ref, pos_vmem, kind_vmem, sems):
@@ -126,25 +126,17 @@
     wo_ref[...] = jnp.sum(jnp.where(eye, row_ref[...].astype(F32), 0.0), axis=1, keepdims=True)
 
 
-def edge_kernel(plan, *refs):
-    n_plate, n_column, n_gz, counts, atoms = plan
-    n_far, n_away = n_column - n_gz, n_plate - 1
-    far_refs, away_refs, refs = refs[:n_far], refs[n_far : n_far + n_away], refs[n_far + n_away :]
-    part_i_ref, part_j_ref, hot_i_ref, hot_j_ref, side_ref, emb_ref, w1_ref, w2_ref, wo_ref = refs[:9]
-    energy_ref, plate_ref, column_ref = refs[9:]
-    rows, total = part_i_ref.shape
-    width = (rows - EXTRA) // 9
-    hot_i = hot_i_ref[...]
-    hot_j = hot_j_ref[...]
-
-    def gather(part, blocks, hot, start):
-        if not blocks:
+def edge_part(lanes, size, rows, width, atoms, n_gz, away, far, inputs, energy_ref, out):
+    part_i_ref, part_j_ref, hot_i_ref, hot_j_ref, side_ref, emb_ref, w1_ref, w2_ref, wo_ref = inputs
+
+    def gather(part, block, hot, start):
+        if block is None:
             return part
-        block = jnp.concatenate([ref[...] for ref in blocks], axis=1)
-        return part + jnp.dot(block, hot[start * atoms :], preferred_element_type=F32)
-
-    got_i = gather(part_i_ref[...], away_refs, hot_i, 1)
-    got_j = gather(part_j_ref[...], far_refs, hot_j, n_gz)
+        return part + jnp.dot(block, hot[start * atoms :, lanes], preferred_element_type=F32)
+
+    got_i = gather(part_i_ref[:, lanes], away, hot_i_ref, 1)
+    got_j = gather(part_j_ref[:, lanes], far, hot_j_ref, n_gz)
+    yield
 
     def row(got, k):
         return got[k : k + 1, :]
@@ -153,15 +145,15 @@
     for axis in range(3):
         ci = row(got_i, axis) + row(got_i, 3 + axis)
         cj = row(got_j, axis) + row(got_j, 3 + axis)
-        off = side_ref[axis : axis + 1, :]
+        off = side_ref[axis : axis + 1, lanes]
         if axis == 0:
             ci = ci + off
         else:
             cj = cj + off
         d.append(cj - ci)
     r2 = d[0] * d[0] + d[1] * d[1] + d[2] * d[2] + SOFTEN
-    r = jnp.sqrt(r2)
-    inv = 1.0 / r
+    inv = lax.rsqrt(r2)
+    r = r2 * inv
     nx, ny, nz = d[0] * inv, d[1] * inv, d[2] * inv
     root3, root5, root15 = math.sqrt(3.0), math.sqrt(5.0), math.sqrt(15.0)
     harm = [
@@ -196,8 +188,9 @@
     s_j = degrees(got_j)
     q = jnp.concatenate([(a * b).astype(BF16) for a, b in zip(s_i, s_j)], axis=0)
 
+    yield
     kinds = emb_ref.shape[0]
-    kind_iota = lax.broadcasted_iota(jnp.int32, (kinds, total), 0).astype(F32)
+    kind_iota = lax.broadcasted_iota(jnp.int32, (kinds, size), 0).astype(F32)
     tn = (((0,), (0,)), ((), ()))
 
     def emb_of(got):
@@ -214,40 +207,83 @@
         + lax.dot_general(w_emb, emb, tn, preferred_element_type=F32)
         + lax.dot_general(w_rad, radial.astype(BF16), tn, preferred_element_type=F32)
     )
+    yield
     sig1 = sigmoid(pre1)
     hidden = (pre1 * sig1).astype(BF16)
     w2 = w2_ref[...]
     pre2 = jnp.dot(w2, hidden, preferred_element_type=F32)
+    yield
     sig2 = sigmoid(pre2)
     w_out = wo_ref[...]
     score = jnp.sum(w_out * (pre2 * sig2), axis=0, keepdims=True)
-    live = side_ref[3:4, :]
+    live = side_ref[3:4, lanes]
     live_env = live * env
-    energy_ref[...] = live_env * score
+    energy_ref[:, lanes] = live_env * score
 
     g2 = (live_env * w_out) * (sig2 * (1.0 + pre2 * (1.0 - sig2)))
     dh = lax.dot_general(w2, g2.astype(BF16), tn, preferred_element_type=F32).astype(BF16).astype(F32)
+    yield
     g1 = (dh * (sig1 * (1.0 + pre1 * (1.0 - sig1)))).astype(BF16)
     dq = jnp.dot(w_q, g1, preferred_element_type=F32).astype(BF16).astype(F32)
     dradial = jnp.dot(w_rad, g1, preferred_element_type=F32).astype(BF16).astype(F32)
+    yield
     dy = [None] * 9
     for deg, members in ((1, range(1, 4)), (2, range(4, 9))):
         part = dq[deg * width : (deg + 1) * width, :]
         for_i = part * s_j[deg]
         for_j = part * s_i[deg]
         for m in members:
-            dy[m] = jnp.sum(for_i * feat(got_i, m) + for_j * feat(got_j, m), axis=0, keepdims=True)
-    gn = [
+            both = for_i * feat(got_i, m) + for_j * feat(got_j, m)
+            dy[m] = jnp.sum(both.reshape(width // 8, 8, size), axis=0)
+    gn = [jnp.sum(term, axis=0, keepdims=True) for term in (
         root3 * dy[1] + root15 * (ny * dy[4] + nz * dy[7] + nx * dy[8]),
         root3 * dy[2] + root15 * (nx * dy[4] + nz * dy[5] - ny * dy[8]),
         root3 * dy[3] + root15 * (ny * dy[5] + nx * dy[7]) + (3.0 * root5) * nz * dy[6],
-    ]
+    )]
     dr = jnp.sum(dradial * (freq * wave - radial), axis=0, keepdims=True)
     dr = (dr - (gn[0] * nx + gn[1] * ny + gn[2] * nz)) * inv
     dr2 = dr * (0.5 * inv) - (live * score) * gap * (2.0 / (RADIUS * RADIUS))
     grad = jnp.concatenate([gn[k] * inv + 2.0 * d[k] * dr2 for k in range(3)], axis=0)
     high = grad.astype(BF16).astype(F32)
-    both = jnp.concatenate([high, grad - high, jnp.zeros((10, total), F32)], axis=0).astype(BF16)
+    both = jnp.concatenate([high, grad - high, jnp.zeros((10, size), F32)], axis=0).astype(BF16)
+    out.append(both)
+
+
+def unsort(order, refs):
+    out = [None] * len(order)
+    for place, k in enumerate(order):
+        out[k] = refs[place]
+    return out
+
+
+def edge_kernel(plan, order, *refs):
+    n_plate, n_column, n_gz, counts, atoms = plan
+    n_far, n_away = n_column - n_gz, n_plate - 1
+    arrived = unsort(order, refs)
+    far_refs, away_refs, refs = arrived[:n_far], arrived[n_far:], refs[n_far + n_away :]
+    inputs = refs[:9]
+    part_i_ref, _, hot_i_ref, hot_j_ref = inputs[:4]
+    energy_ref, plate_ref, column_ref = refs[9:]
+    rows, total = part_i_ref.shape
+    width = (rows - EXTRA) // 9
+    def lay(refs):
+        return jnp.concatenate([ref[...] for ref in refs], axis=1) if refs else None
+
+    away, far = lay(away_refs), lay(far_refs)
+    pieces = 2 if total % (128 * 2) == 0 else 1
+    size = total // pieces
+    outs = [[] for _ in range(pieces)]
+    steps = [
+        edge_part(slice(k * size, (k + 1) * size), size, rows, width, atoms, n_gz, away, far, inputs, energy_ref, outs[k])
+        for k in range(pieces)
+    ]
+    running = [True] * pieces
+    while any(running):
+        for k, step in enumerate(steps):
+            if running[k]:
+                running[k] = next(step, "end") != "end"
+    both = jnp.concatenate([out[0] for out in outs], axis=1)
+    hot_i, hot_j = hot_i_ref[...], hot_j_ref[...]
     nt = (((1,), (1,)), ((), ()))
 
     def spread(hot):
@@ -274,10 +310,7 @@
     plate_blocks = [packed] + [lax.ppermute(packed, "plate", there) for there, _ in plate_moves]
     gz_blocks = [packed] + [lax.ppermute(packed, "gz", there) for there, _ in gz_moves]
     near = [[lax.ppermute(b, "tower", there) for b in gz_blocks] for there, _ in tower_moves[:1]]
-    relay = list(gz_blocks)
-    if near and gz_moves:
-        relay[1:] = lax.optimization_barrier((*gz_blocks[1:], near[0][0]))[:-1]
-    far = [[lax.ppermute(b, "tower", there) for b in relay] for there, _ in tower_moves[1:]]
+    far = [[lax.ppermute(b, "tower", there) for b in gz_blocks] for there, _ in tower_moves[1:]]
     column_blocks = gz_blocks + [b for blocks in near + far for b in blocks]
     n_plate, n_column = len(plate_blocks), len(column_blocks)
 
@@ -317,8 +350,11 @@
         *(pltpu.with_memory_space_constraint(w, pltpu.HBM) for w in (emb_table, w_table, w_second, w_row)),
         *gz_blocks,
     )
+    arrived = column_blocks[n_gz:] + plate_blocks[1:]
+    groups = [("ac", "bd")[m > 0][k] for k in range(len(tower_moves)) for m in range(n_gz)] + list("ef"[: n_plate - 1])
+    order = sorted(range(len(arrived)), key=lambda k: "cdfaeb".index(groups[k]))
     energy, plate_part, column_part = pl.pallas_call(
-        functools.partial(edge_kernel, plan),
+        functools.partial(edge_kernel, plan, order),
         out_shape=(
             jax.ShapeDtypeStruct((1, total), F32),
             jax.ShapeDtypeStruct((max(n_plate - 1, 1), 3, atoms), F32),
@@ -328,7 +364,7 @@
         out_specs=(vmem, vmem, vmem),
         compiler_params=pltpu.CompilerParams(vmem_limit_bytes=32 * 1024 * 1024),
         name="edge_work",
-    )(*column_blocks[n_gz:], *plate_blocks[1:], *prepared)
+    )(*(arrived[k] for k in order), *prepared)
 
     forces = 0.0
     for k, (_, back) in enumerate(plate_moves):

time: 27.1 us -> 26.8 us (0.989)
  waiting for transfers between devices: 7.69 us -> 5.37 us
  starting transfers between devices: 12.3 us -> 14.3 us
    ppermute x2, starting transfers between devices: 2.22 us -> 3.73 us  [shards(): forces = forces + lax.ppermute(plate_part[k], 'plate', back)]
    ppermute x2, waiting for transfers between devices: 4.34 us -> 3.28 us  [shards(): lax.ppermute(packed, 'plate', there)]
    ppermute x1, waiting for transfers between devices: 0.87 us -> 0.01 us  [shards(): column = column + lax.ppermute(column_part[:, 1 + k], 'gz', back)]
    ppermute x2, waiting for transfers between devices: 2.07 us -> 1.45 us  [shards(): forces = forces + lax.ppermute(plate_part[k], 'plate', back)]
    ppermute x2, starting transfers between devices: 3.6 us -> 4.05 us  [shards(): lax.ppermute(packed, 'plate', there)]
    ppermute x2, starting transfers between devices: 0.62 us -> 0.99 us  [shards(): forces = forces + lax.ppermute(column[1 + k], 'tower', back)]
    ppermute x4, starting transfers between devices: 2.31 us -> 1.97 us  [shards(): lax.ppermute(b, 'tower', there)]
  transfers between devices with their start and end apart: 12 -> 12, of which waited for: 6 -> 4; matrix products, arithmetic and copies ran while one was open for 0% -> 0% of each run, Pallas kernels for 6% -> 7%
where the time goes in v5:
time: 26.8 us; the launch traced here: 26.6 us
  starting transfers between devices  14.3 us (53%)
  waiting for transfers between devices  5.37 us (20%)
  Pallas kernels  4.93 us (18%)
  between operations  1.34 us (5%)
  local copies, waits for them, and re-layouts  0.58 us (2%)
    ppermute x2, starting transfers between devices, shards(): lax.ppermute(packed, 'plate', there)  4.05 us
    ppermute x2, starting transfers between devices, shards(): forces = forces + lax.ppermute(plate_part[k], 'plate', back)  3.73 us
    ppermute x2, waiting for transfers between devices, shards(): lax.ppermute(packed, 'plate', there)  3.28 us
    ppermute x1, starting transfers between devices, shards(): lax.ppermute(packed, 'gz', there)  3 us
    pallas_call x1, Pallas kernels, shards(): pl.pallas_call(functools.partial(edge_kernel, plan, order), out_shape=(ja...  2.22 us
    ppermute x4, starting transfers between devices, shards(): lax.ppermute(b, 'tower', there)  1.97 us
    pallas_call x1, Pallas kernels, shards(): pl.pallas_call(functools.partial(prep_kernel, plan), out_shape=(jax.Shape...  1.74 us
    ppermute x2, waiting for transfers between devices, shards(): forces = forces + lax.ppermute(plate_part[k], 'plate', back)  1.45 us
  transfers between devices with their start and end apart: 12, of which 4 were waited for; matrix products, arithmetic and copies ran while one was open for 0% of the time, Pallas kernels for 7%

profile of v5, /device:TPU:0, one launch (start us, length us, event | category | flops | bytes accessed | tf_op | source)
XLA Modules:
  0.0 26.6 jit_solution(18152084282741674331)
XLA Ops:
  0.6 1.0 %pack.1.refs_0_ = bf16[592,128]{1,0:T(8,128)(2,1)S(1)} custom-call(f32[3,1,128]{2,1,0:T(1,128)} %bitcast.38, bf16[576,128]{1,0:T(8,128)(2,1)} %bitcast.35, s32[1,128]{1,0:T(1,128)} %bitcast.39), custom_call_target="tpu_custom_call" | custom-call | tf_op jit(solution)/shard_map/pack/pallas_call | solution.py:79
  1.6 3.0 %collective-permute-start.1 = (bf16[592,128]{1,0:T(8,128)(2,1)S(1)}, bf16[592,128]{1,0:T(8,128)(2,1)S(1)}, u32[]{:S(2)}, u32[]{:S(2)}) collective-permute-start(bf16[592,128]{1,0:T(8,128)(2,1)S(1)} %pack.1.refs_0_), channel_id=1, source_target_pairs={{0,1},{1,0},{2,3},{3,2},{4,5},{5,4},{6,7},{7,6},{8,9},{9,8},{10,11... | collective-permute-start | bytes 454664 | tf_op jit(solution)/shard_map/ppermute | solution.py:311
  4.6 0.0 collective-permute-start
  4.6 1.6 %collective-permute-start.3 = (bf16[592,128]{1,0:T(8,128)(2,1)S(1)}, bf16[592,128]{1,0:T(8,128)(2,1)S(1)}, u32[]{:S(2)}, u32[]{:S(2)}) collective-permute-start(bf16[592,128]{1,0:T(8,128)(2,1)S(1)} %pack.1.refs_0_), channel_id=1, source_target_pairs={{0,8},{8,0},{16,24},{24,16},{1,9},{9,1},{17,25},{25,17},{2,10},{10... | collective-permute-start | bytes 454664 | tf_op jit(solution)/shard_map/ppermute | solution.py:310
  6.2 1.4 %collective-permute-start.4 = (bf16[592,128]{1,0:T(8,128)(2,1)S(1)}, bf16[592,128]{1,0:T(8,128)(2,1)S(1)}, u32[]{:S(2)}, u32[]{:S(2)}) collective-permute-start(bf16[592,128]{1,0:T(8,128)(2,1)S(1)} %pack.1.refs_0_), channel_id=1, source_target_pairs={{0,6},{2,4},{4,2},{6,0},{1,7},{3,5},{5,3},{7,1},{8,14},{10,12},{12... | collective-permute-start | bytes 454664 | tf_op jit(solution)/shard_map/ppermute | solution.py:312
  7.5 2.5 %collective-permute-start.5 = (bf16[592,128]{1,0:T(8,128)(2,1)S(1)}, bf16[592,128]{1,0:T(8,128)(2,1)S(1)}, u32[]{:S(2)}, u32[]{:S(2)}) collective-permute-start(bf16[592,128]{1,0:T(8,128)(2,1)S(1)} %pack.1.refs_0_), channel_id=1, source_target_pairs={{0,24},{8,16},{16,8},{24,0},{1,25},{9,17},{17,9},{25,1},{2,26},{10... | collective-permute-start | bytes 454664 | tf_op jit(solution)/shard_map/ppermute | solution.py:310
  10.0 0.0 collective-permute-done.1.refs_1_
  10.0 0.0 collective-permute-start.2
  10.0 0.0 collective-permute-done.refs_0_
  10.0 0.6 %collective-permute-start.6 = (bf16[592,128]{1,0:T(8,128)(2,1)S(1)}, bf16[592,128]{1,0:T(8,128)(2,1)S(1)}, u32[]{:S(2)}, u32[]{:S(2)}) collective-permute-start(bf16[592,128]{1,0:T(8,128)(2,1)S(1)} %collective-permute-done.1.refs_1_), channel_id=1, source_target_pairs={{0,6},{2,4},{4,2},{6,0},{1,7},{3,5},{5,3},{7,1},{8,14},{10,12},{12... | collective-permute-start | bytes 454664 | tf_op jit(solution)/shard_map/ppermute | solution.py:312
  11.3 1.7 %prep.1 = (f32[592,512]{1,0:T(8,128)S(1)}, f32[592,512]{1,0:T(8,128)S(1)}, bf16[384,512]{1,0:T(8,128)(2,1)S(1)}, bf16[768,512]{1,0:T(8,128)(2,1)S(1)}, f32[8,512...) custom-call(s32[2,512]{1,0:T(2,128)} %bitcast.37, ...), custom_call_target="tpu_custom_call" | custom-call | tf_op jit(solution)/shard_map/prep/pallas_call | solution.py:325
  13.0 0.0 collective-permute-done.3.refs_2_
  13.1 0.0 collective-permute-done.4.refs_3_
  13.1 3.3 %collective-permute-done.5.refs_4_ = bf16[592,128]{1,0:T(8,128)(2,1)S(1)} collective-permute-done((bf16[592,128]{1,0:T(8,128)(2,1)S(1)}, bf16[592,128]{1,0:T(8,128)(2,1)S(1)}, u32[]{:S(2)}, u32[]{:S(2)}) %collective-permute-start.5) | collective-permute-done | bytes 151584 | tf_op jit(solution)/shard_map/ppermute | solution.py:310
  16.3 0.0 collective-permute-done.2.refs_1_
  16.3 0.0 collective-permute-done.6.refs_5_
  16.3 2.2 %edge_work.1 = (f32[1,512]{1,0:T(1,128)}, f32[2,3,128]{2,1,0:T(4,128)S(1)}, f32[3,2,3,128]{3,2,1,0:T(4,128)S(1)}) custom-call(bf16[592,128]{1,0:T(8,128)(2,1)S(1)} %collective-permute-done.refs_0_, bf16[592,128]{1,0:T(8,128)(2,1)S(1)} %collective-permute-done.2.refs_1_, bf16[592,128]{1,0:T(8,128)(2,1)S(1)} %collective-permute-done.3.refs_2_, ...), custom_call_target="tpu_custom_call" | custom-call | tf_op jit(solution)/shard_map/edge_work/pallas_call | solution.py:356
  18.6 0.6 %collective-permute-start.9 = (f32[3,3,128]{2,1,0:T(4,128)S(1)}, f32[3,3,128]{2,1,0:T(4,128)S(1)}, u32[]{:S(2)}, u32[]{:S(2)}) collective-permute-start(f32[3,3,128]{2,1,0:T(4,128)S(1)} %slice_bitcast_fusion.1), channel_id=1, source_target_pairs={{0,1},{1,0},{2,3},{3,2},{4,5},{5,4},{6,7},{7,6},{8,9},{9,8},{10,11... | collective-permute-start | bytes 13832 | tf_op jit(solution)/shard_map/ppermute | solution.py:374
  19.2 2.6 %collective-permute-start.7 = (f32[3,128]{1,0:T(4,128)S(1)}, f32[3,128]{1,0:T(4,128)S(1)}, u32[]{:S(2)}, u32[]{:S(2)}) collective-permute-start(f32[3,128]{1,0:T(4,128)S(1)} %get-tuple-element.31), channel_id=1, source_target_pairs={{0,24},{8,16},{16,8},{24,0},{1,25},{9,17},{17,9},{25,1},{2,26},{10... | collective-permute-start | bytes 4616 | tf_op jit(solution)/shard_map/ppermute | solution.py:371
  21.8 1.1 %collective-permute-start.8 = (f32[3,128]{1,0:T(4,128)S(1)}, f32[3,128]{1,0:T(4,128)S(1)}, u32[]{:S(2)}, u32[]{:S(2)}) collective-permute-start(f32[3,128]{1,0:T(4,128)S(1)} %get-tuple-element.30), channel_id=1, source_target_pairs={{0,8},{8,0},{16,24},{24,16},{1,9},{9,1},{17,25},{25,17},{2,10},{10... | collective-permute-start | bytes 4616 | tf_op jit(solution)/shard_map/ppermute | solution.py:371
  22.9 0.0 collective-permute-done.9
  22.9 0.1 collective-permute-start.10
  23.0 0.9 %collective-permute-start.11 = (f32[3,128]{1,0:T(4,128)S(1)}, f32[3,128]{1,0:T(4,128)S(1)}, u32[]{:S(2)}, u32[]{:S(2)}) collective-permute-start(f32[3,128]{1,0:T(4,128)S(1)} %get-tuple-element.29), channel_id=1, source_target_pairs={{0,2},{2,0},{4,6},{6,4},{1,3},{3,1},{5,7},{7,5},{8,10},{10,8},{12,... | collective-permute-start | bytes 4616 | tf_op jit(solution)/shard_map/ppermute | solution.py:377
  23.9 0.6 %collective-permute-done.7 = f32[3,128]{1,0:T(4,128)S(1)} collective-permute-done((f32[3,128]{1,0:T(4,128)S(1)}, f32[3,128]{1,0:T(4,128)S(1)}, u32[]{:S(2)}, u32[]{:S(2)}) %collective-permute-start.7) | collective-permute-done | bytes 1568 | tf_op jit(solution)/shard_map/ppermute | solution.py:371
  24.5 0.8 %collective-permute-done.8 = f32[3,128]{1,0:T(4,128)S(1)} collective-permute-done((f32[3,128]{1,0:T(4,128)S(1)}, f32[3,128]{1,0:T(4,128)S(1)}, u32[]{:S(2)}, u32[]{:S(2)}) %collective-permute-start.8) | collective-permute-done | bytes 1568 | tf_op jit(solution)/shard_map/ppermute | solution.py:371
  25.3 0.6 %collective-permute-done.10 = f32[3,128]{1,0:T(4,128)S(1)} collective-permute-done((f32[3,128]{1,0:T(4,128)S(1)}, f32[3,128]{1,0:T(4,128)S(1)}, u32[]{:S(2)}, u32[]{:S(2)}) %collective-permute-start.10) | collective-permute-done | bytes 1568 | tf_op jit(solution)/shard_map/ppermute | solution.py:377
  26.0 0.0 collective-permute-done.11
  26.0 0.6 %copy.12 = f32[1,1,1,3,128]{4,2,3,1,0:T(1,128)} copy(f32[1,1,1,3,128]{4,3,2,1,0:T(4,128)S(1)} %fusion.4) | data formatting | bytes 3072
  (5 shorter events, 0.0 us)
Async XLA Ops:
  1.6 8.4 %collective-permute-start.1 = (bf16[592,128]{1,0:T(8,128)(2,1)S(1)}, bf16[592,128]{1,0:T(8,128)(2,1)S(1)}, u32[]{:S(2)}, u32[]{:S(2)}) collective-permute-start(bf16[592,128]{1,0:T(8,128)(2,1)S(1)} %pack.1.refs_0_), channel_id=1, source_target_pairs={{0,1},{1,0},{2,3},{3,2},{4,5},{5,4},{6,7},{7,6},{8,9},{9,8},{10,11... | collective-permute-start | bytes 454664 | tf_op jit(solution)/shard_map/ppermute | solution.py:311
  4.6 5.4 %collective-permute-start = (bf16[592,128]{1,0:T(8,128)(2,1)S(1)}, bf16[592,128]{1,0:T(8,128)(2,1)S(1)}, u32[]{:S(2)}, u32[]{:S(2)}) collective-permute-start(bf16[592,128]{1,0:T(8,128)(2,1)S(1)} %pack.1.refs_0_), channel_id=1, source_target_pairs={{0,2},{2,0},{4,6},{6,4},{1,3},{3,1},{5,7},{7,5},{8,10},{10,8},{12,... | collective-permute-start | bytes 454664 | tf_op jit(solution)/shard_map/ppermute | solution.py:313
  4.6 8.4 %collective-permute-start.3 = (bf16[592,128]{1,0:T(8,128)(2,1)S(1)}, bf16[592,128]{1,0:T(8,128)(2,1)S(1)}, u32[]{:S(2)}, u32[]{:S(2)}) collective-permute-start(bf16[592,128]{1,0:T(8,128)(2,1)S(1)} %pack.1.refs_0_), channel_id=1, source_target_pairs={{0,8},{8,0},{16,24},{24,16},{1,9},{9,1},{17,25},{25,17},{2,10},{10... | collective-permute-start | bytes 454664 | tf_op jit(solution)/shard_map/ppermute | solution.py:310
  6.2 6.9 %collective-permute-start.4 = (bf16[592,128]{1,0:T(8,128)(2,1)S(1)}, bf16[592,128]{1,0:T(8,128)(2,1)S(1)}, u32[]{:S(2)}, u32[]{:S(2)}) collective-permute-start(bf16[592,128]{1,0:T(8,128)(2,1)S(1)} %pack.1.refs_0_), channel_id=1, source_target_pairs={{0,6},{2,4},{4,2},{6,0},{1,7},{3,5},{5,3},{7,1},{8,14},{10,12},{12... | collective-permute-start | bytes 454664 | tf_op jit(solution)/shard_map/ppermute | solution.py:312
  7.5 8.8 %collective-permute-start.5 = (bf16[592,128]{1,0:T(8,128)(2,1)S(1)}, bf16[592,128]{1,0:T(8,128)(2,1)S(1)}, u32[]{:S(2)}, u32[]{:S(2)}) collective-permute-start(bf16[592,128]{1,0:T(8,128)(2,1)S(1)} %pack.1.refs_0_), channel_id=1, source_target_pairs={{0,24},{8,16},{16,8},{24,0},{1,25},{9,17},{17,9},{25,1},{2,26},{10... | collective-permute-start | bytes 454664 | tf_op jit(solution)/shard_map/ppermute | solution.py:310
  10.0 6.3 %collective-permute-start.2 = (bf16[592,128]{1,0:T(8,128)(2,1)S(1)}, bf16[592,128]{1,0:T(8,128)(2,1)S(1)}, u32[]{:S(2)}, u32[]{:S(2)}) collective-permute-start(bf16[592,128]{1,0:T(8,128)(2,1)S(1)} %collective-permute-done.1.refs_1_), channel_id=1, source_target_pairs={{0,2},{2,0},{4,6},{6,4},{1,3},{3,1},{5,7},{7,5},{8,10},{10,8},{12,... | collective-permute-start | bytes 454664 | tf_op jit(solution)/shard_map/ppermute | solution.py:313
  10.0 6.3 %collective-permute-start.6 = (bf16[592,128]{1,0:T(8,128)(2,1)S(1)}, bf16[592,128]{1,0:T(8,128)(2,1)S(1)}, u32[]{:S(2)}, u32[]{:S(2)}) collective-permute-start(bf16[592,128]{1,0:T(8,128)(2,1)S(1)} %collective-permute-done.1.refs_1_), channel_id=1, source_target_pairs={{0,6},{2,4},{4,2},{6,0},{1,7},{3,5},{5,3},{7,1},{8,14},{10,12},{12... | collective-permute-start | bytes 454664 | tf_op jit(solution)/shard_map/ppermute | solution.py:312
  18.6 4.3 %collective-permute-start.9 = (f32[3,3,128]{2,1,0:T(4,128)S(1)}, f32[3,3,128]{2,1,0:T(4,128)S(1)}, u32[]{:S(2)}, u32[]{:S(2)}) collective-permute-start(f32[3,3,128]{2,1,0:T(4,128)S(1)} %slice_bitcast_fusion.1), channel_id=1, source_target_pairs={{0,1},{1,0},{2,3},{3,2},{4,5},{5,4},{6,7},{7,6},{8,9},{9,8},{10,11... | collective-permute-start | bytes 13832 | tf_op jit(solution)/shard_map/ppermute | solution.py:374
  19.2 5.4 %collective-permute-start.7 = (f32[3,128]{1,0:T(4,128)S(1)}, f32[3,128]{1,0:T(4,128)S(1)}, u32[]{:S(2)}, u32[]{:S(2)}) collective-permute-start(f32[3,128]{1,0:T(4,128)S(1)} %get-tuple-element.31), channel_id=1, source_target_pairs={{0,24},{8,16},{16,8},{24,0},{1,25},{9,17},{17,9},{25,1},{2,26},{10... | collective-permute-start | bytes 4616 | tf_op jit(solution)/shard_map/ppermute | solution.py:371
  21.8 3.6 %collective-permute-start.8 = (f32[3,128]{1,0:T(4,128)S(1)}, f32[3,128]{1,0:T(4,128)S(1)}, u32[]{:S(2)}, u32[]{:S(2)}) collective-permute-start(f32[3,128]{1,0:T(4,128)S(1)} %get-tuple-element.30), channel_id=1, source_target_pairs={{0,8},{8,0},{16,24},{24,16},{1,9},{9,1},{17,25},{25,17},{2,10},{10... | collective-permute-start | bytes 4616 | tf_op jit(solution)/shard_map/ppermute | solution.py:371
  22.9 3.1 %collective-permute-start.10 = (f32[3,128]{1,0:T(4,128)S(1)}, f32[3,128]{1,0:T(4,128)S(1)}, u32[]{:S(2)}, u32[]{:S(2)}) collective-permute-start(f32[3,128]{1,0:T(4,128)S(1)} %get-tuple-element.28), channel_id=1, source_target_pairs={{0,6},{2,4},{4,2},{6,0},{1,7},{3,5},{5,3},{7,1},{8,14},{10,12},{12... | collective-permute-start | bytes 4616 | tf_op jit(solution)/shard_map/ppermute | solution.py:377
  23.0 3.0 %collective-permute-start.11 = (f32[3,128]{1,0:T(4,128)S(1)}, f32[3,128]{1,0:T(4,128)S(1)}, u32[]{:S(2)}, u32[]{:S(2)}) collective-permute-start(f32[3,128]{1,0:T(4,128)S(1)} %get-tuple-element.29), channel_id=1, source_target_pairs={{0,2},{2,0},{4,6},{6,4},{1,3},{3,1},{5,7},{7,5},{8,10},{10,8},{12,... | collective-permute-start | bytes 4616 | tf_op jit(solution)/shard_map/ppermute | solution.py:377
